TPU v7x, 32 devices: a whole 2x2x4 slice. The times are simulated.
32 devices in a mesh: dp: 8 (over y, x, core), seq: 4 (over z).
Axes of the slice: x: 2, y: 2, z: 4, core: 2. Of those that a mesh axis runs over, the one named last changes fastest.
Arguments:
- clips: float32 [24, 512, 1024], P('dp', 'seq'), may hold values from -6 to 6
- counts: int32 [8], P('dp'), may hold values from 1 to 3, as said below
- out_cotangent: float32 [24, 512, 1024], P('dp', 'seq'), may hold values from -6 to 6
- norm1_gain: float32 [1024], P(('dp', 'seq')), may hold values from 0.5 to 1.5
- norm1_shift: float32 [1024], P(('dp', 'seq')), may hold values from -1 to 1
- qkv_weight: float32 [3145728], P(('dp', 'seq')), may hold values from -0.1875 to 0.1875
- query_bias: float32 [1024], P(('dp', 'seq')), may hold values from -3 to 3
- value_bias: float32 [1024], P(('dp', 'seq')), may hold values from -0.26516503 to 0.26516503
- proj_weight: float32 [1048576], P(('dp', 'seq')), may hold values from -2.5 to 2.5
- proj_bias: float32 [1024], P(('dp', 'seq')), may hold values from -1 to 1
- norm2_gain: float32 [1024], P(('dp', 'seq')), may hold values from 0.5 to 1.5
- norm2_shift: float32 [1024], P(('dp', 'seq')), may hold values from -1 to 1
- up_weight: float32 [4194304], P(('dp', 'seq')), may hold values from -0.1875 to 0.1875
- up_bias: float32 [4096], P(('dp', 'seq')), may hold values from -3 to 3
- down_weight: float32 [4194304], P(('dp', 'seq')), may hold values from -0.09375 to 0.09375
- down_bias: float32 [1024], P(('dp', 'seq')), may hold values from -1 to 1
Outputs:
- block_out: float32 [24, 512, 1024], P('dp', 'seq')
- input_grad: float32 [24, 512, 1024], P('dp', 'seq')
- norm1_gain_grad: float32 [1024], P(('dp', 'seq'))
- norm1_shift_grad: float32 [1024], P(('dp', 'seq'))
- qkv_weight_grad: float32 [3145728], P(('dp', 'seq'))
- query_bias_grad: float32 [1024], P(('dp', 'seq'))
- value_bias_grad: float32 [1024], P(('dp', 'seq'))
- proj_weight_grad: float32 [1048576], P(('dp', 'seq'))
- proj_bias_grad: float32 [1024], P(('dp', 'seq'))
- norm2_gain_grad: float32 [1024], P(('dp', 'seq'))
- norm2_shift_grad: float32 [1024], P(('dp', 'seq'))
- up_weight_grad: float32 [4194304], P(('dp', 'seq'))
- up_bias_grad: float32 [4096], P(('dp', 'seq'))
- down_weight_grad: float32 [4194304], P(('dp', 'seq'))
- down_bias_grad: float32 [1024], P(('dp', 'seq'))
Inputs may be any that keep to these rules, and one draw needn't show every extreme that they name: `counts`: some data group holds 3 clips and another holds 1.
All inputs are finite; a program needn't handle non-finite values.
Results may differ from a plain program's by a relative error of at most 0.03.
Values may be sent and summed in bfloat16 or wider, within the bound.
A program may use at most 256 MiB of HBM per device.

v0:
```python
import math

import jax
import jax.numpy as jnp
from jax import lax
from jax.sharding import PartitionSpec as P

D = 1024
FF = 4096
HEADS = 16
HEAD_DIM = 64


EPSILON = 1e-05


def layer_norm(values, gain_vec, shift_vec):
    center = values - jnp.mean(values, axis=-1, keepdims=True)
    spread = jnp.mean(center * center, axis=-1, keepdims=True)
    return center * lax.rsqrt(spread + EPSILON) * gain_vec + shift_vec


def gelu_exact(values):
    return jax.nn.gelu(values, approximate=False)


def shaped(flat_list):
    return (
        flat_list[0],
        flat_list[1],
        flat_list[2].reshape(D, 3 * D),
        flat_list[3],
        flat_list[4],
        flat_list[5].reshape(D, D),
        flat_list[6],
        flat_list[7],
        flat_list[8],
        flat_list[9].reshape(D, FF),
        flat_list[10],
        flat_list[11].reshape(FF, D),
        flat_list[12],
    )


def fetch_forward(rounded):
    return (
        lax.all_gather(rounded[0], ("dp", "seq"), axis=0, tiled=True),
        lax.all_gather(rounded[1], ("dp", "seq"), axis=0, tiled=True),
        lax.all_gather(rounded[2], ("dp", "seq"), axis=0, tiled=True),
        lax.all_gather(rounded[3], ("dp", "seq"), axis=0, tiled=True),
        lax.all_gather(rounded[4], ("dp", "seq"), axis=0, tiled=True),
        lax.all_gather(rounded[5], ("dp", "seq"), axis=0, tiled=True),
        lax.all_gather(rounded[6], ("dp", "seq"), axis=0, tiled=True),
        lax.all_gather(rounded[7], ("dp", "seq"), axis=0, tiled=True),
        lax.all_gather(rounded[8], ("dp", "seq"), axis=0, tiled=True),
        lax.all_gather(rounded[9], ("dp", "seq"), axis=0, tiled=True),
        lax.all_gather(rounded[10], ("dp", "seq"), axis=0, tiled=True),
        lax.all_gather(rounded[11], ("dp", "seq"), axis=0, tiled=True),
        lax.all_gather(rounded[12], ("dp", "seq"), axis=0, tiled=True),
    )


def fetch_backward(rounded):
    return (
        lax.all_gather(rounded[0], ("dp", "seq"), axis=0, tiled=True),
        lax.all_gather(rounded[1], ("dp", "seq"), axis=0, tiled=True),
        lax.all_gather(rounded[2], ("dp", "seq"), axis=0, tiled=True),
        lax.all_gather(rounded[3], ("dp", "seq"), axis=0, tiled=True),
        lax.all_gather(rounded[4], ("dp", "seq"), axis=0, tiled=True),
        lax.all_gather(rounded[5], ("dp", "seq"), axis=0, tiled=True),
        lax.all_gather(rounded[6], ("dp", "seq"), axis=0, tiled=True),
        lax.all_gather(rounded[7], ("dp", "seq"), axis=0, tiled=True),
        lax.all_gather(rounded[8], ("dp", "seq"), axis=0, tiled=True),
        lax.all_gather(rounded[9], ("dp", "seq"), axis=0, tiled=True),
        lax.all_gather(rounded[10], ("dp", "seq"), axis=0, tiled=True),
        lax.all_gather(rounded[11], ("dp", "seq"), axis=0, tiled=True),
        lax.all_gather(rounded[12], ("dp", "seq"), axis=0, tiled=True),
    )


def reduce_end(grads):
    return (
        lax.psum_scatter(grads[0], ("dp", "seq"), scatter_dimension=0, tiled=True),
        lax.psum_scatter(grads[1], ("dp", "seq"), scatter_dimension=0, tiled=True),
        lax.psum_scatter(grads[2], ("dp", "seq"), scatter_dimension=0, tiled=True),
        lax.psum_scatter(grads[3], ("dp", "seq"), scatter_dimension=0, tiled=True),
        lax.psum_scatter(grads[4], ("dp", "seq"), scatter_dimension=0, tiled=True),
        lax.psum_scatter(grads[5], ("dp", "seq"), scatter_dimension=0, tiled=True),
        lax.psum_scatter(grads[6], ("dp", "seq"), scatter_dimension=0, tiled=True),
        lax.psum_scatter(grads[7], ("dp", "seq"), scatter_dimension=0, tiled=True),
        lax.psum_scatter(grads[8], ("dp", "seq"), scatter_dimension=0, tiled=True),
        lax.psum_scatter(grads[9], ("dp", "seq"), scatter_dimension=0, tiled=True),
        lax.psum_scatter(grads[10], ("dp", "seq"), scatter_dimension=0, tiled=True),
        lax.psum_scatter(grads[11], ("dp", "seq"), scatter_dimension=0, tiled=True),
        lax.psum_scatter(grads[12], ("dp", "seq"), scatter_dimension=0, tiled=True),
    )


def attention_scores(query_heads, key_heads):
    scale = 1.0 / math.sqrt(query_heads.shape[-1])
    return (
        jnp.einsum("qhd,khd->hqk", query_heads, key_heads, preferred_element_type=jnp.float32)
        * scale
    )


def run_forward(inputs, weights):
    (
        gain_first,
        shift_first,
        qkv_matrix,
        query_shift,
        value_shift,
        proj_matrix,
        proj_shift,
        gain_second,
        shift_second,
        up_matrix,
        up_shift,
        down_matrix,
        down_shift,
    ) = weights
    row_count = inputs.shape[0]
    normed_first = layer_norm(
        inputs, gain_first.astype(jnp.float32), shift_first.astype(jnp.float32)
    ).astype(jnp.bfloat16)
    projected = jnp.dot(normed_first, qkv_matrix, preferred_element_type=jnp.float32)
    queries = (projected[:, :D] + query_shift.astype(jnp.float32)).astype(jnp.bfloat16)
    keys_local = projected[:, D : 2 * D].astype(jnp.bfloat16)
    values_local = (projected[:, 2 * D :] + value_shift.astype(jnp.float32)).astype(jnp.bfloat16)
    keys_all, values_all = (
        lax.all_gather(keys_local, "seq", axis=0, tiled=True),
        lax.all_gather(values_local, "seq", axis=0, tiled=True),
    )
    query_heads = queries.reshape(row_count, HEADS, HEAD_DIM)
    key_heads = keys_all.reshape(-1, HEADS, HEAD_DIM)
    value_heads = values_all.reshape(-1, HEADS, HEAD_DIM)
    scores = attention_scores(query_heads, key_heads)
    highest = jnp.max(scores, axis=-1, keepdims=True)
    exponent = jnp.exp(scores - highest)
    totals = jnp.sum(exponent, axis=-1, keepdims=True)
    softened = exponent / totals
    log_total = highest + jnp.log(totals)
    mixed_heads = jnp.einsum(
        "hqk,khd->qhd",
        softened.astype(jnp.bfloat16),
        value_heads,
        preferred_element_type=jnp.float32,
    )
    attended = mixed_heads.reshape(row_count, D).astype(jnp.bfloat16)
    middle = (
        inputs
        + jnp.dot(attended, proj_matrix, preferred_element_type=jnp.float32)
        + proj_shift.astype(jnp.float32)
    )
    normed_second = layer_norm(
        middle, gain_second.astype(jnp.float32), shift_second.astype(jnp.float32)
    ).astype(jnp.bfloat16)
    upper_part = jnp.dot(
        normed_second, up_matrix, preferred_element_type=jnp.float32
    ) + up_shift.astype(jnp.float32)
    hidden = gelu_exact(upper_part).astype(jnp.bfloat16)
    result = (
        middle
        + jnp.dot(hidden, down_matrix, preferred_element_type=jnp.float32)
        + down_shift.astype(jnp.float32)
    )
    saved_state = (
        normed_first,
        query_heads,
        key_heads,
        value_heads,
        log_total,
        attended,
        middle,
        normed_second,
        upper_part,
        hidden,
    )
    return (result, saved_state)


def run_backward(inputs, upstream, weights, saved_state):
    (
        gain_first,
        shift_first,
        qkv_matrix,
        query_shift,
        value_shift,
        proj_matrix,
        proj_shift,
        gain_second,
        shift_second,
        up_matrix,
        up_shift,
        down_matrix,
        down_shift,
    ) = weights
    (
        normed_first,
        query_heads,
        key_heads,
        value_heads,
        log_total,
        attended,
        middle,
        normed_second,
        upper_part,
        hidden,
    ) = saved_state
    row_count = inputs.shape[0]
    out_grad = upstream.astype(jnp.bfloat16)
    down_shift_grad = jnp.sum(out_grad.astype(jnp.float32), axis=0)
    down_matrix_grad = jnp.dot(hidden.T, out_grad, preferred_element_type=jnp.float32)
    hidden_grad = jnp.dot(out_grad, down_matrix.T, preferred_element_type=jnp.float32)
    unused_gelu, gelu_back = jax.vjp(gelu_exact, upper_part)
    upper_grad = gelu_back(hidden_grad)[0].astype(jnp.bfloat16)
    up_shift_grad = jnp.sum(upper_grad.astype(jnp.float32), axis=0)
    up_matrix_grad = jnp.dot(normed_second.T, upper_grad, preferred_element_type=jnp.float32)
    normed_grad = jnp.dot(upper_grad, up_matrix.T, preferred_element_type=jnp.float32)
    unused_second, second_back = jax.vjp(
        layer_norm, middle, gain_second.astype(jnp.float32), shift_second.astype(jnp.float32)
    )
    middle_part, gain_second_grad, shift_second_grad = second_back(normed_grad)
    middle_grad = upstream + middle_part
    branch_grad = middle_grad.astype(jnp.bfloat16)
    proj_shift_grad = jnp.sum(branch_grad.astype(jnp.float32), axis=0)
    proj_matrix_grad = jnp.dot(attended.T, branch_grad, preferred_element_type=jnp.float32)
    attended_grad = jnp.dot(branch_grad, proj_matrix.T, preferred_element_type=jnp.float32)
    attended_grad = attended_grad.astype(jnp.bfloat16).reshape(row_count, HEADS, HEAD_DIM)
    scores = attention_scores(query_heads, key_heads)
    softened = jnp.exp(scores - log_total)
    soft_grad = jnp.einsum(
        "qhd,khd->hqk", attended_grad, value_heads, preferred_element_type=jnp.float32
    )
    weighted_sum = jnp.sum(softened * soft_grad, axis=-1, keepdims=True)
    score_grad = (softened * (soft_grad - weighted_sum)).astype(jnp.bfloat16)
    scale = 1.0 / math.sqrt(HEAD_DIM)
    query_grad = (
        jnp.einsum("hqk,khd->qhd", score_grad, key_heads, preferred_element_type=jnp.float32)
        * scale
    )
    query_grad = query_grad.reshape(row_count, D).astype(jnp.bfloat16)
    value_part = jnp.einsum(
        "hqk,qhd->khd",
        softened.astype(jnp.bfloat16),
        attended_grad,
        preferred_element_type=jnp.float32,
    )
    key_part = (
        jnp.einsum("hqk,qhd->khd", score_grad, query_heads, preferred_element_type=jnp.float32)
        * scale
    )
    key_total, value_total = (
        lax.psum_scatter(
            key_part.reshape(-1, D).astype(jnp.bfloat16), "seq", scatter_dimension=0, tiled=True
        ).astype(jnp.float32),
        lax.psum_scatter(
            value_part.reshape(-1, D).astype(jnp.bfloat16), "seq", scatter_dimension=0, tiled=True
        ).astype(jnp.float32),
    )
    key_grad = key_total.astype(jnp.bfloat16)
    value_grad = value_total.astype(jnp.bfloat16)
    joined_grad = jnp.concatenate([query_grad, key_grad, value_grad], axis=1)
    query_shift_grad = jnp.sum(query_grad.astype(jnp.float32), axis=0)
    value_shift_grad = jnp.sum(value_grad.astype(jnp.float32), axis=0)
    qkv_matrix_grad = jnp.dot(normed_first.T, joined_grad, preferred_element_type=jnp.float32)
    first_grad = jnp.dot(joined_grad, qkv_matrix.T, preferred_element_type=jnp.float32)
    unused_first, first_back = jax.vjp(
        layer_norm, inputs, gain_first.astype(jnp.float32), shift_first.astype(jnp.float32)
    )
    input_part, gain_first_grad, shift_first_grad = first_back(first_grad)
    input_grad = middle_grad + input_part
    gradients = (
        gain_first_grad,
        shift_first_grad,
        qkv_matrix_grad.reshape(-1),
        query_shift_grad,
        value_shift_grad,
        proj_matrix_grad.reshape(-1),
        proj_shift_grad,
        gain_second_grad,
        shift_second_grad,
        up_matrix_grad.reshape(-1),
        up_shift_grad,
        down_matrix_grad.reshape(-1),
        down_shift_grad,
    )
    return (input_grad, gradients)


def per_device(
    clips,
    counts,
    out_cotangent,
    norm1_gain,
    norm1_shift,
    qkv_weight,
    query_bias,
    value_bias,
    proj_weight,
    proj_bias,
    norm2_gain,
    norm2_shift,
    up_weight,
    up_bias,
    down_weight,
    down_bias,
):
    params = (
        norm1_gain,
        norm1_shift,
        qkv_weight,
        query_bias,
        value_bias,
        proj_weight,
        proj_bias,
        norm2_gain,
        norm2_shift,
        up_weight,
        up_bias,
        down_weight,
        down_bias,
    )
    rounded = tuple((parameter.astype(jnp.bfloat16) for parameter in params))
    batch_count = clips.shape[0]
    outputs = []
    input_grads = []
    running = None
    for batch_index in range(batch_count):
        living = (batch_index < counts[0]).astype(jnp.float32)
        forward_weights = shaped(fetch_forward(rounded))
        result, saved_state = run_forward(clips[batch_index], forward_weights)
        outputs.append(result * living)
        backward_weights = shaped(fetch_backward(rounded))
        input_grad, gradients = run_backward(
            clips[batch_index], out_cotangent[batch_index] * living, backward_weights, saved_state
        )
        input_grads.append(input_grad)
        running = gradients if running is None else jax.tree.map(jnp.add, running, gradients)
    running = reduce_end(running)
    return (
        jnp.stack(outputs),
        jnp.stack(input_grads),
        running[0],
        running[1],
        running[2],
        running[3],
        running[4],
        running[5],
        running[6],
        running[7],
        running[8],
        running[9],
        running[10],
        running[11],
        running[12],
    )


def solution(mesh):
    in_specs = (
        P("dp", "seq", None),
        P("dp"),
        P("dp", "seq", None),
        P(("dp", "seq")),
        P(("dp", "seq")),
        P(("dp", "seq")),
        P(("dp", "seq")),
        P(("dp", "seq")),
        P(("dp", "seq")),
        P(("dp", "seq")),
        P(("dp", "seq")),
        P(("dp", "seq")),
        P(("dp", "seq")),
        P(("dp", "seq")),
        P(("dp", "seq")),
        P(("dp", "seq")),
    )
    out_specs = (
        P("dp", "seq", None),
        P("dp", "seq", None),
        P(("dp", "seq")),
        P(("dp", "seq")),
        P(("dp", "seq")),
        P(("dp", "seq")),
        P(("dp", "seq")),
        P(("dp", "seq")),
        P(("dp", "seq")),
        P(("dp", "seq")),
        P(("dp", "seq")),
        P(("dp", "seq")),
        P(("dp", "seq")),
        P(("dp", "seq")),
        P(("dp", "seq")),
    )
    return jax.shard_map(
        per_device, mesh=mesh, in_specs=in_specs, out_specs=out_specs, check_vma=False
    )
```

profile of v0, /device:TPU:0, one launch (start us, length us, event | category | flops | bytes accessed | tf_op | source)
XLA Modules:
  0.0 1517.1 jit_solution(12894608537740885272)
XLA Ops:
  17.6 42.3 %all-reduce.23 = (bf16[1024]{0:T(1024)(128)(2,1)S(1)}, bf16[1024]{0:T(1024)(128)(2,1)S(1)}, bf16[1024]{0:T(1024)(128)(2,1)S(1)}, bf16[1024]{0:T(1024)(128)(2,1)S...) all-reduce(bf16[1024]{0:T(1024)(128)(2,1)S(1)} %dynamic-update-slic, ...), channel_id=1, replica_groups=mesh['dp'=8,'seq'=4] {'dp','seq'}, use_global_device_ids=true, to_apply=%add.1 | all-reduce | flops 8192 | bytes 32768
  61.9 22.1 %all-gather.12.cloned.1.call-done = bf16[3145728]{0:T(1024)(128)(2,1)} async-done(((bf16[98304]{0:T(1024)(128)(2,1)}), bf16[3145728]{0:T(1024)(128)(2,1)}) %all-gather.12.cloned.1.call-update) | async-done | bytes 6291472 | tf_op jit(solution)/shard_map/all_gather | solution.py:49
  84.0 10.3 reshape.470
  116.0 66.1 %all-gather = bf16[32,1,128]{2,1,0:T(2,128)(2,1)S(1)} all-gather(bf16[1,1,128]{2,1,0:T(2,128)(2,1)S(1)} %convert_bitcast_fusion), channel_id=1, replica_groups=mesh['dp'=8,'seq'=4] {'dp','seq'}, dimensions={0}, use_global_device_ids=true | all-gather | bytes 8448 | tf_op jit(solution)/shard_map/all_gather | solution.py:57
  189.3 10.6 all-gather.26.cloned.1.call-done
  201.4 27.9 %all-gather.28.cloned.1.call-done = bf16[512,1024]{1,0:T(8,128)(2,1)} async-done(((bf16[128,1024]{1,0:T(8,128)(2,1)}), bf16[512,1024]{1,0:T(8,128)(2,1)}) %all-gather.28.cloned.1.call-update) | async-done | bytes 1048592 | tf_op jit(solution)/shard_map/all_gather | solution.py:133
  231.7 27.2 %all-gather.14.cloned.1.call-done = bf16[512,1024]{1,0:T(8,128)(2,1)} async-done(((bf16[128,1024]{1,0:T(8,128)(2,1)}), bf16[512,1024]{1,0:T(8,128)(2,1)}) %all-gather.14.cloned.1.call-update) | async-done | bytes 1048592 | tf_op jit(solution)/shard_map/all_gather | solution.py:133
  261.1 26.8 %all-gather.24.cloned.1.call-done = bf16[512,1024]{1,0:T(8,128)(2,1)} async-done(((bf16[128,1024]{1,0:T(8,128)(2,1)}), bf16[512,1024]{1,0:T(8,128)(2,1)}) %all-gather.24.cloned.1.call-update) | async-done | bytes 1048592 | tf_op jit(solution)/shard_map/all_gather | solution.py:133
  290.1 26.8 %all-gather.16.cloned.1.call-done = bf16[512,1024]{1,0:T(8,128)(2,1)} async-done(((bf16[128,1024]{1,0:T(8,128)(2,1)}), bf16[512,1024]{1,0:T(8,128)(2,1)}) %all-gather.16.cloned.1.call-update) | async-done | bytes 1048592 | tf_op jit(solution)/shard_map/all_gather | solution.py:132
  337.0 59.6 %all-gather.20.cloned.1.call-done = bf16[4194304]{0:T(1024)(128)(2,1)} async-done(((bf16[131072]{0:T(1024)(128)(2,1)}), bf16[4194304]{0:T(1024)(128)(2,1)}) %all-gather.20.cloned.1.call-update) | async-done | bytes 8388624 | tf_op jit(solution)/shard_map/all_gather | solution.py:56
  396.6 13.8 reshape.475
  416.5 58.9 %all-gather.22.cloned.1.call-done = bf16[4194304]{0:T(1024)(128)(2,1)} async-done(((bf16[131072]{0:T(1024)(128)(2,1)}), bf16[4194304]{0:T(1024)(128)(2,1)}) %all-gather.22.cloned.1.call-update) | async-done | bytes 8388624 | tf_op jit(solution)/shard_map/all_gather | solution.py:58
  475.4 13.4 reshape.476
  488.8 10.5 convert_reduce_fusion.1
  499.3 6.7 fusion.168
  515.3 8.1 convert_reduce_fusion
  526.3 8.1 convert_reduce_fusion.2
  604.3 9.6 fusion.155
  613.8 9.7 fusion.132
  633.3 9.6 fusion.154
  642.8 9.8 fusion.131
  652.9 19.6 %add_bitcast_fusion = f32[512,8,8,128]{3,2,1,0:T(8,128)} fusion(f32[4096,1024]{1,0:T(8,128)} %fusion.131, f32[4096,1024]{1,0:T(8,128)} %fusion.132, f32[3,128,1024]{2,1,0:T(8,128)S(1)} %copy-done.25, f32[]{:T(128)} %bitcast.27, f32[128,4096]{1,0:T(8,128)} %copy-done.62), kind=kOutput, calls=%fused_computation | convolution fusion | flops 1116471296 | bytes 52953092 | tf_op jit(solution)/shard_map/dot_general | solution.py:214
  672.5 18.7 %add_bitcast_fusion.1 = f32[128,32,8,128]{3,2,1,0:T(8,128)} fusion(f32[1024,4096]{1,0:T(8,128)} %fusion.154, f32[1024,4096]{1,0:T(8,128)} %fusion.155, bf16[128,4096]{1,0:T(8,128)(2,1)} %copy-done.37, f32[128,1024]{1,0:T(8,128)S(1)} %get-tuple-element.118, f32[128]{0:T(128)S(1)} %fusion.141, f32[128]{0:T(128)S(1)} %broadcast_multiply_fusion, ...), kind=kOutput, calls=%fused_computation.1 | convolution fusion | flops 1082785792 | bytes 51913728 | tf_op jit(solution)/shard_map/dot_general | solution.py:219
  701.2 9.5 copy.94
  712.0 7.3 copy.93
  733.3 7.6 fusion.76
  749.2 14.8 add_bitcast_fusion.2
  764.0 12.1 copy.91
  776.8 10.2 fusion.56
  787.1 8.7 fusion.59
  813.7 40.9 %all-reduce.21 = (f32[1024]{0:T(1024)S(1)}, f32[1024]{0:T(1024)S(1)}, f32[1024]{0:T(1024)S(1)}, f32[1024]{0:T(1024)S(1)}, f32[1024]{0:T(1024)S(1)}, /*index=5*/f...) all-reduce(f32[1024]{0:T(1024)S(1)} %add_add_fusion.14, ...), channel_id=8, replica_groups=mesh['dp'=8,'seq'=4] {'dp','seq'}, use_global_device_ids=true, to_apply=%region_42.0.clone | all-reduce | flops 12288 | bytes 98304
  861.3 642.0 %all-reduce.26.cloned.1.call-done = (f32[3145728]{0:T(1024)}, f32[1048576]{0:T(1024)}, f32[4194304]{0:T(1024)}, f32[4194304]{0:T(1024)}) async-done(((f32[3145728]{0:T(1024)}, f32[1048576]{0:T(1024)}, f32[4194304]{0:T(1024)}, f32[4194304]{0:T(1024)}), (f32[3145728]{0:T(1024)}, f32[1048576]{0:T(1024)}, f32[4194304]{0:T(1024)}, f32[4194304]{0:T(1024)})) %all-reduce.26.cloned.1.call-update) | async-done | bytes 50331664
  (505 shorter events, 231.0 us)
Async XLA Ops:
  7.2 54.4 %copy-start.5 = (f32[3,128,1024]{2,1,0:T(8,128)S(1)}, f32[3,128,1024]{2,1,0:T(8,128)}, u32[]{:S(2)}) copy-start(f32[3,128,1024]{2,1,0:T(8,128)} %param.16) | copy-start | bytes 4718596
  7.2 76.8 %all-gather.12.cloned.1.call-start = ((), (), s32[]{:S(2)}) async-start(), calls=%async_computation.6 | async-start | bytes 6488064 | tf_op jit(solution)/shard_map/all_gather | solution.py:49
  9.1 173.2 %all-gather.18.cloned.1.call-start = ((), (), s32[]{:S(2)}) async-start(), calls=%async_computation.9 | async-start | bytes 2162688 | tf_op jit(solution)/shard_map/all_gather | solution.py:52
  10.7 176.4 %all-gather.30.cloned.1.call-start = ((), (), s32[]{:S(2)}) async-start(), calls=%async_computation.15 | async-start | bytes 1310720 | tf_op jit(solution)/shard_map/all_gather | solution.py:132
  59.9 46.1 %copy-start.69 = (f32[1024]{0:T(1024)}, f32[1024]{0:T(1024)S(1)}, u32[]{:S(2)}) copy-start(f32[1024]{0:T(1024)S(1)} %convert_element_type.435) | copy-start | bytes 12292
  59.9 46.1 %copy-start.59 = (f32[1024]{0:T(1024)}, f32[1024]{0:T(1024)S(1)}, u32[]{:S(2)}) copy-start(f32[1024]{0:T(1024)S(1)} %convert_element_type.433) | copy-start | bytes 12292
  61.5 44.6 %copy-start.92 = (f32[128]{0:T(128)}, f32[128]{0:T(128)S(1)}, u32[]{:S(2)}) copy-start(f32[128]{0:T(128)S(1)} %broadcast_multiply_fusion.5) | copy-start | bytes 1540
  61.5 32.8 %copy-start.94 = (f32[128]{0:T(128)}, f32[128]{0:T(128)S(1)}, u32[]{:S(2)}) copy-start(f32[128]{0:T(128)S(1)} %get-tuple-element.147) | copy-start | bytes 1540
  61.5 38.7 %copy-start.90 = (f32[128]{0:T(128)}, f32[128]{0:T(128)S(1)}, u32[]{:S(2)}) copy-start(f32[128]{0:T(128)S(1)} %get-tuple-element.148) | copy-start | bytes 1540
  61.8 32.4 %copy-start.121 = (f32[128]{0:T(128)}, f32[128]{0:T(128)S(1)}, u32[]{:S(2)}) copy-start(f32[128]{0:T(128)S(1)} %get-tuple-element.29) | copy-start | bytes 1540
  61.8 38.3 %copy-start.123 = (f32[128]{0:T(128)}, f32[128]{0:T(128)S(1)}, u32[]{:S(2)}) copy-start(f32[128]{0:T(128)S(1)} %get-tuple-element.30) | copy-start | bytes 1540
  61.9 44.2 %copy-start.125 = (f32[128]{0:T(128)}, f32[128]{0:T(128)S(1)}, u32[]{:S(2)}) copy-start(f32[128]{0:T(128)S(1)} %get-tuple-element.28) | copy-start | bytes 1540
  100.1 99.8 %all-gather.26.cloned.1.call-start = ((), (), s32[]{:S(2)}) async-start(), calls=%async_computation.13 | async-start | bytes 1310720 | tf_op jit(solution)/shard_map/all_gather | solution.py:132
  106.0 123.4 %all-gather.28.cloned.1.call-start = ((), (), s32[]{:S(2)}) async-start(), calls=%async_computation.14 | async-start | bytes 1310720 | tf_op jit(solution)/shard_map/all_gather | solution.py:133
  111.5 147.3 %all-gather.14.cloned.1.call-start = ((), (), s32[]{:S(2)}) async-start(), calls=%async_computation.7 | async-start | bytes 1310720 | tf_op jit(solution)/shard_map/all_gather | solution.py:133
  112.1 175.8 %all-gather.24.cloned.1.call-start = ((), (), s32[]{:S(2)}) async-start(), calls=%async_computation.12 | async-start | bytes 1310720 | tf_op jit(solution)/shard_map/all_gather | solution.py:133
  112.8 204.1 %all-gather.16.cloned.1.call-start = ((), (), s32[]{:S(2)}) async-start(), calls=%async_computation.8 | async-start | bytes 1310720 | tf_op jit(solution)/shard_map/all_gather | solution.py:132
  113.7 283.0 %all-gather.20.cloned.1.call-start = ((), (), s32[]{:S(2)}) async-start(), calls=%async_computation.10 | async-start | bytes 8650752 | tf_op jit(solution)/shard_map/all_gather | solution.py:56
  114.5 360.9 %all-gather.22.cloned.1.call-start = ((), (), s32[]{:S(2)}) async-start(), calls=%async_computation.11 | async-start | bytes 8650752 | tf_op jit(solution)/shard_map/all_gather | solution.py:58
  115.3 609.5 %reduce-scatter.29.cloned.1.call-start = ((), (), s32[]{:S(2)}) async-start(), calls=%async_computation.21 | async-start | bytes 1310720
  185.3 145.8 %copy-start.54 = (bf16[128,1024]{0,1:T(8,128)(2,1)}, bf16[128,1024]{0,1:T(8,128)(2,1)S(1)}, u32[]{:S(2)}) copy-start(bf16[128,1024]{0,1:T(8,128)(2,1)S(1)} %copy.74) | copy-start | bytes 786436
  201.4 117.7 %copy-start.20 = (bf16[512,1024]{0,1:T(8,128)(2,1)}, bf16[512,1024]{0,1:T(8,128)(2,1)S(1)}, u32[]{:S(2)}) copy-start(bf16[512,1024]{0,1:T(8,128)(2,1)S(1)} %copy.72) | copy-start | bytes 3145732
  336.2 74.3 %copy-start.73 = (bf16[16,64,128]{2,1,0:T(8,128)(2,1)}, bf16[16,64,128]{2,1,0:T(8,128)(2,1)S(1)}, u32[]{:S(2)}) copy-start(bf16[16,64,128]{2,1,0:T(8,128)(2,1)S(1)} %fusion.63) | copy-start | bytes 786436
  550.6 175.5 %reduce-scatter.25.cloned.1.call-start = ((), (), s32[]{:S(2)}) async-start(), calls=%async_computation.19 | async-start | bytes 1310720
  561.6 166.3 %reduce-scatter.21.cloned.1.call-start = ((), (), s32[]{:S(2)}) async-start(), calls=%async_computation.17 | async-start | bytes 1310720
  576.3 153.4 %reduce-scatter.19.cloned.1.call-start = ((), (), s32[]{:S(2)}) async-start(), calls=%async_computation.16 | async-start | bytes 1310720
  596.7 134.7 %reduce-scatter.23.cloned.1.call-start = ((), (), s32[]{:S(2)}) async-start(), calls=%async_computation.18 | async-start | bytes 1310720
  623.6 123.8 %reduce-scatter.27.cloned.1.call-start = ((), (), s32[]{:S(2)}) async-start(), calls=%async_computation.20 | async-start | bytes 1310720
  652.7 850.6 %all-reduce.26.cloned.1.call-start = ((), (), s32[]{:S(2)}) async-start(), calls=%async_computation.22 | async-start | bytes 100663296
  812.6 47.2 %copy-start.36 = (f32[128,1024]{1,0:T(8,128)S(1)}, f32[128,1024]{1,0:T(8,128)}, u32[]{:S(2)}) copy-start(f32[128,1024]{1,0:T(8,128)} %copy-done.35) | copy-start | bytes 1572868
  812.6 47.2 %copy-start.67 = (f32[128,1024]{1,0:T(8,128)S(1)}, f32[128,1024]{1,0:T(8,128)}, u32[]{:S(2)}) copy-start(f32[128,1024]{1,0:T(8,128)} %get-tuple-element.88) | copy-start | bytes 1572868
  812.7 47.2 %copy-start.115 = (f32[128]{0:T(128)S(1)}, f32[128]{0:T(128)}, u32[]{:S(2)}) copy-start(f32[128]{0:T(128)} %copy-done.114) | copy-start | bytes 1540
  (125 other events, 594.5 us)
Sparse Core Ops, SparseCore 0:
  11.5 72.4 all-gather.11
  87.5 55.0 all-gather.17
  144.2 26.8 all-gather.29
  172.5 27.4 all-gather.25
  201.9 27.4 all-gather.27
  231.4 27.4 all-gather.13
  260.4 27.4 all-gather.23
  289.4 27.4 all-gather.15
  319.8 76.7 all-gather.19
  399.4 75.9 all-gather.21
  550.7 25.7 reduce-scatter.28
  578.7 25.7 reduce-scatter.24
  606.9 25.7 reduce-scatter.20
  634.9 25.7 reduce-scatter.18
  663.5 25.7 reduce-scatter.22
  691.6 25.7 reduce-scatter.26
  776.2 727.0 all-reduce.25
where the time goes:
time: 1530 us; the launch traced here: 1520 us
  waiting for transfers between devices  903 us (59%)
  matrix products  258 us (17%)
  local copies, waits for them, and re-layouts  150 us (10%)
  blocking collectives  149 us (10%)
  other arithmetic  37.8 us (2%)
  between operations  16.8 us (1%)
    unnamed x24, waiting for transfers between devices  643 us
    unnamed x325, local copies, waits for them, and re-layouts  87.5 us
    unnamed x2, blocking collectives  83.2 us
    all_gather x3, waiting for transfers between devices, run_forward(): lax.all_gather(values_local, 'seq', axis=0, tiled=True)  81.9 us
    all_gather x1, blocking collectives, fetch_forward(): lax.all_gather(rounded[10], ('dp', 'seq'), axis=0, tiled=True)  66.1 us
    all_gather x1, waiting for transfers between devices, fetch_forward(): lax.all_gather(rounded[9], ('dp', 'seq'), axis=0, tiled=True)  59.6 us
    all_gather x1, waiting for transfers between devices, fetch_forward(): lax.all_gather(rounded[11], ('dp', 'seq'), axis=0, tiled=True)  58.9 us
    dot_general x3, matrix products, run_backward(): jnp.dot(hidden.T, out_grad, preferred_element_type=jnp.float32)  39.2 us
  transfers between devices with their start and end apart: 17, of which 9 were waited for; matrix products, arithmetic and copies ran while one was open for 21% of the time, Pallas kernels for 0%

commit v1 on v0

v1 whole, which is shorter than its diff:
```python
import functools

import jax
import jax.numpy as jnp
from jax import lax
from jax.experimental import pallas as pl
from jax.experimental.pallas import tpu as pltpu
from jax.sharding import PartitionSpec as P

D = 1024
FF = 4096
HEADS = 16
HEAD_DIM = 64
EPSILON = 1e-05
LANES = 128
BF = jnp.bfloat16
F32 = jnp.float32
AXES = ("dp", "seq")
RING = (0, 1, 3, 2)


def dot(a, b):
    return jnp.dot(a, b, preferred_element_type=F32)


def dot_nt(a, b):
    return lax.dot_general(a, b, (((1,), (1,)), ((), ())), preferred_element_type=F32)


def dot_tn(a, b):
    return lax.dot_general(a, b, (((0,), (0,)), ((), ())), preferred_element_type=F32)


def soft_t(q2, k_half):
    scores = dot_nt(k_half, q2) * (HEAD_DIM**-0.5)
    top = jnp.max(scores, axis=0, keepdims=True)
    e = jnp.exp(scores - top)
    return e * (1.0 / jnp.sum(e, axis=0, keepdims=True))


def attend_kernel(q_ref, k_ref, v_ref, o_ref):
    q2, k2, v2 = q_ref[...], k_ref[...], v_ref[...]
    low = lax.broadcasted_iota(jnp.int32, k2.shape, 1) < HEAD_DIM
    v_t = v2.T
    zero = jnp.zeros_like(k2)
    parts = []
    for h in range(2):
        k_half = jnp.where(low == (h == 0), k2, zero)
        p_t = soft_t(q2, k_half).astype(BF)
        parts.append(dot(v_t[h * HEAD_DIM : (h + 1) * HEAD_DIM], p_t))
    o_ref[...] = jnp.concatenate(parts, axis=0).T.astype(BF)


def attend(qkv):
    t = qkv.shape[0]
    n = D // LANES
    spec = lambda off: pl.BlockSpec((t, LANES), lambda h: (0, off + h))
    return pl.pallas_call(
        attend_kernel,
        grid=(n,),
        out_shape=jax.ShapeDtypeStruct((t, D), BF),
        in_specs=[spec(0), spec(n), spec(2 * n)],
        out_specs=spec(0),
        compiler_params=pltpu.CompilerParams(vmem_limit_bytes=48 * 2**20),
        cost_estimate=pl.CostEstimate(
            flops=16 * 4 * t * t * HEAD_DIM, bytes_accessed=8 * t * D, transcendentals=16 * t * t
        ),
    )(qkv, qkv, qkv)


def attend_back_kernel(q_ref, k_ref, v_ref, do_ref, dq_ref, dk_ref, dv_ref):
    q2, k2, v2, do2 = q_ref[...], k_ref[...], v_ref[...], do_ref[...]
    low = lax.broadcasted_iota(jnp.int32, k2.shape, 1) < HEAD_DIM
    k_t = k2.T
    zero = jnp.zeros_like(k2)
    dq, dk, dv = [], [], []
    for h in range(2):
        mine = low == (h == 0)
        p = soft_t(q2, jnp.where(mine, k2, zero))
        dp = dot_nt(jnp.where(mine, v2, zero), do2)
        total = jnp.sum(p * dp, axis=0, keepdims=True)
        ds = (p * (dp - total)).astype(BF)
        dv.append(dot(p.astype(BF), do2))
        dk.append(dot(ds, q2))
        dq.append(dot(k_t[h * HEAD_DIM : (h + 1) * HEAD_DIM], ds))
    scale = HEAD_DIM**-0.5
    dq_ref[...] = (jnp.concatenate(dq, axis=0).T * scale).astype(BF)
    dk_ref[...] = (jnp.where(low, dk[0], dk[1]) * scale).astype(BF)
    dv_ref[...] = jnp.where(low, dv[0], dv[1]).astype(BF)


def attend_back(qkv, do):
    t = qkv.shape[0]
    n = D // LANES
    spec = lambda off: pl.BlockSpec((t, LANES), lambda h: (0, off + h))
    return pl.pallas_call(
        attend_back_kernel,
        grid=(n,),
        out_shape=[jax.ShapeDtypeStruct((t, D), BF)] * 3,
        in_specs=[spec(0), spec(n), spec(2 * n), spec(0)],
        out_specs=[spec(0)] * 3,
        compiler_params=pltpu.CompilerParams(vmem_limit_bytes=48 * 2**20),
        cost_estimate=pl.CostEstimate(
            flops=16 * 10 * t * t * HEAD_DIM, bytes_accessed=14 * t * D, transcendentals=16 * t * t
        ),
    )(qkv, qkv, qkv, do)


class Links:
    def __init__(self, n_dp, n_seq):
        self.n_dp, self.n_seq = n_dp, n_seq
        self.short = n_dp == 8 and n_seq == len(RING)
        self.dp = lax.axis_index("dp")
        self.z = lax.axis_index("seq")

    def cross(self, x, bit):
        s = self.n_seq
        pairs = [(d * s + z, (d ^ bit) * s + z) for d in range(self.n_dp) for z in range(s)]
        return lax.ppermute(x, AXES, pairs)

    def ring(self, x):
        s = self.n_seq
        step = {RING[i]: RING[(i + 1) % s] for i in range(s)}
        pairs = [(d * s + z, d * s + step[z]) for d in range(self.n_dp) for z in range(s)]
        return lax.ppermute(x, AXES, pairs)

    def place(self):
        return jnp.array(RING, jnp.int32)[self.z]

    def gather(self, shard):
        if not self.short:
            whole = lax.all_gather(shard, AXES, axis=0, tiled=True)
            return list(jnp.split(whole, self.n_dp, axis=0))
        rows = shard.shape[0]
        held = [shard]
        for _ in range(3):
            held.append(self.ring(held[-1]))
        held = jnp.stack(held)
        place = self.place()
        own = jnp.concatenate(
            [lax.dynamic_index_in_dim(held, (place - RING[k]) % 4, 0, False) for k in range(4)]
        )
        half = 2 * rows
        from_x = self.cross(own, 2)
        from_y = self.cross(own, 4)
        far = jnp.concatenate([self.cross(from_x[:half], 4), self.cross(from_y[half:], 2)])
        blocks = []
        for b in (own, from_x, from_y, far):
            blocks += [b, self.cross(b, 1)]
        return blocks

    def reduce(self, blocks):
        if not self.short:
            whole = jnp.concatenate(blocks).astype(BF)
            return lax.psum_scatter(whole, AXES, scatter_dimension=0, tiled=True).astype(F32)
        sums = []
        for j in (3, 1, 2, 0):
            theirs = self.cross(blocks[2 * j + 1].astype(BF), 1)
            sums.append(blocks[2 * j].astype(F32) + theirs.astype(F32))
        far, to_x, to_y, own = sums
        half = far.shape[0] // 2
        far = far.astype(BF)
        low = self.cross(far[:half], 2).astype(F32)
        high = self.cross(far[half:], 4).astype(F32)
        to_y = jnp.concatenate([to_y[:half] + low, to_y[half:]])
        to_x = jnp.concatenate([to_x[:half], to_x[half:] + high])
        own = own + self.cross(to_x.astype(BF), 2).astype(F32) + self.cross(to_y.astype(BF), 4).astype(F32)
        rows = own.shape[0] // 4
        place = self.place()
        order = jnp.array(RING, jnp.int32)

        def piece(back):
            return lax.dynamic_slice_in_dim(own, order[(place - back) % 4] * rows, rows, 0)

        moving = self.ring(piece(1).astype(BF))
        for back in (2, 3):
            moving = self.ring((piece(back) + moving.astype(F32)).astype(BF))
        return piece(4) + moving.astype(F32)

    def blocks_of(self, x, axis):
        width = x.shape[axis] // self.n_dp
        if not self.short:
            return jnp.split(x, self.n_dp, axis=axis)
        return [
            lax.dynamic_slice_in_dim(x, (self.dp ^ m) * width, width, axis) for m in range(self.n_dp)
        ]

    def ordered(self, x, axis):
        return jnp.concatenate(self.blocks_of(x, axis), axis=axis)


    def lead(self, d, slots):
        return d % 2 if self.n_seq > slots else 0

    def shift_pairs(self, s, slots):
        n = self.n_seq
        pairs = []
        for d in range(self.n_dp):
            for z in range(n):
                to = (z + s) % n
                if 0 <= to - self.lead(d, slots) < slots:
                    pairs.append((d * n + z, d * n + to))
        return pairs

    def my_clip(self, slots):
        lead = self.dp % 2 if self.n_seq > slots else 0
        return self.z - lead

    def collect(self, x):
        slots, n = x.shape[0], self.n_seq
        clip = self.my_clip(slots)
        parts = []
        for s in range(n):
            lead = self.z - clip
            index = jnp.clip((self.z + s) % n - lead, 0, slots - 1)
            part = lax.dynamic_index_in_dim(x, index, 0, False)
            parts.append(part if s == 0 else lax.ppermute(part, AXES, self.shift_pairs(s, slots)))
        return jnp.concatenate(parts)

    def hand_back(self, y, slots):
        n = self.n_seq
        rows = y.shape[0] // n
        lead = self.z - self.my_clip(slots)
        back = []
        for s in range(n):
            part = y[s * rows : (s + 1) * rows]
            pairs = [(b, a) for a, b in self.shift_pairs(s, slots)]
            back.append(part if s == 0 else lax.ppermute(part, AXES, pairs))
        back = jnp.stack(back)
        return jnp.stack(
            [lax.dynamic_index_in_dim(back, (c + lead - self.z) % n, 0, False) for c in range(slots)]
        )


def norm_parts(v):
    center = v - jnp.mean(v, axis=-1, keepdims=True)
    r = lax.rsqrt(jnp.mean(center * center, axis=-1, keepdims=True) + EPSILON)
    return center * r, r


def norm_back(vhat, r, gain, e):
    t = e * gain
    grad = r * (
        t - jnp.mean(t, axis=-1, keepdims=True) - vhat * jnp.mean(t * vhat, axis=-1, keepdims=True)
    )
    return grad, jnp.sum(e * vhat, axis=0), jnp.sum(e, axis=0)


def gelu_both(u):
    cdf = 0.5 * (1.0 + lax.erf(u * 0.7071067811865476))
    pdf = 0.3989422804014327 * jnp.exp(-0.5 * u * u)
    return u * cdf, cdf + u * pdf


SMALL = (D, D, D, D, D, D, D, FF, D)


def per_device(
    n_dp,
    n_seq,
    clips,
    counts,
    out_cotangent,
    norm1_gain,
    norm1_shift,
    qkv_weight,
    query_bias,
    value_bias,
    proj_weight,
    proj_bias,
    norm2_gain,
    norm2_shift,
    up_weight,
    up_bias,
    down_weight,
    down_bias,
):
    links = Links(n_dp, n_seq)
    n = n_dp * n_seq
    slots = clips.shape[0]
    rows = D // n
    small = (
        norm1_gain,
        norm1_shift,
        query_bias,
        value_bias,
        proj_bias,
        norm2_gain,
        norm2_shift,
        up_bias,
        down_bias,
    )
    packed = jnp.concatenate(small)
    packed = jnp.pad(packed, (0, rows * LANES - packed.shape[0])).reshape(rows, LANES)
    shard_a = jnp.concatenate(
        [qkv_weight.reshape(rows, 3 * D), proj_weight.reshape(rows, D), packed], axis=1
    ).astype(BF)
    shard_u = up_weight.reshape(rows, FF).astype(BF)
    shard_d = down_weight.reshape(FF // n, D).astype(BF)

    x = links.collect(clips.astype(BF)).astype(F32)
    blocks_a = links.gather(shard_a)
    blocks_u = links.gather(shard_u)
    out_grad = links.collect(out_cotangent.astype(BF))
    blocks_d = links.gather(shard_d)

    clip = links.my_clip(slots)
    alive = (clip >= 0) & (clip < slots) & (clip < counts[0])
    out_grad = jnp.where(alive, out_grad, jnp.zeros_like(out_grad))

    a_mat = jnp.concatenate(blocks_a)
    table = a_mat[:, 4 * D :].reshape(n_dp, n_seq, rows * LANES)
    table = links.ordered(table, 0).reshape(n, rows * LANES).astype(F32)
    vectors, at = [], 0
    for size in SMALL:
        vectors.append(table[:, at : at + size // n].reshape(size))
        at += size // n
    gain1, shift1, q_bias, v_bias, p_bias, gain2, shift2, u_bias, d_bias = vectors

    vhat1, r1 = norm_parts(x)
    normed1 = (vhat1 * gain1 + shift1).astype(BF)
    normed1_b = links.ordered(normed1, 1)
    qkv_bias = jnp.concatenate([q_bias, jnp.zeros_like(q_bias), v_bias])
    qkv_mat, proj_mat = a_mat[:, : 3 * D], a_mat[:, 3 * D : 4 * D]
    qkv = (dot(normed1_b, qkv_mat) + qkv_bias).astype(BF)
    attended = attend(qkv)
    attended_b = links.ordered(attended, 1)
    branch = dot(attended_b, proj_mat) + p_bias
    middle = x + branch
    vhat2, r2 = norm_parts(middle)
    normed2_b = links.ordered((vhat2 * gain2 + shift2).astype(BF), 1)
    u_mat = jnp.concatenate(blocks_u)
    hidden, slope = gelu_both(dot(normed2_b, u_mat) + u_bias)
    hidden_b = links.ordered(hidden.astype(BF), 1)
    slope = slope.astype(BF)
    d_mat = jnp.concatenate(blocks_d)
    out_part = branch + dot(hidden_b, d_mat) + d_bias
    living = (jnp.arange(slots) < counts[0]).astype(F32)[:, None, None]
    block_out = living * (clips + links.hand_back(out_part.astype(BF), slots).astype(F32))

    d_down = dot_tn(hidden_b, out_grad).astype(BF)
    down_grad = links.reduce(jnp.split(d_down, n_dp, axis=0))
    hidden_grad = links.ordered(dot_nt(out_grad, d_mat), 1)
    upper_grad = (hidden_grad * slope).astype(BF)
    d_up = dot_tn(normed2_b, upper_grad).astype(BF)
    up_grad = links.reduce(jnp.split(d_up, n_dp, axis=0))
    normed_grad = links.ordered(dot_nt(upper_grad, u_mat), 1)
    part, gain2_grad, shift2_grad = norm_back(vhat2, r2, gain2, normed_grad)
    middle_part = out_grad.astype(F32) + part
    branch_grad = middle_part.astype(BF)
    attended_grad = links.ordered(dot_nt(branch_grad, proj_mat).astype(BF), 1)
    dq, dk, dv = attend_back(qkv, attended_grad)
    joined = jnp.concatenate([dq, dk, dv], axis=1)
    first_grad = links.ordered(dot_nt(joined, qkv_mat), 1)
    first_part, gain1_grad, shift1_grad = norm_back(vhat1, r1, gain1, first_grad)
    living_cot = living * out_cotangent
    input_grad = living_cot + links.hand_back((part + first_part).astype(BF), slots).astype(F32)

    total = lambda g: jnp.sum(g.astype(F32), axis=0)
    small_grads = (
        gain1_grad,
        shift1_grad,
        total(dq),
        total(dv),
        total(branch_grad),
        gain2_grad,
        shift2_grad,
        total(upper_grad),
        total(out_grad),
    )
    grad_table = jnp.concatenate([g.reshape(n, -1) for g in small_grads], axis=1)
    width = grad_table.shape[1]
    grad_table = jnp.pad(grad_table, ((0, 0), (0, rows * LANES - width)))
    grad_table = links.ordered(grad_table.reshape(n_dp, n_seq, rows * LANES), 0)
    d_a = jnp.concatenate(
        [
            dot_tn(normed1_b, joined).astype(BF),
            dot_tn(attended_b, branch_grad).astype(BF),
            grad_table.reshape(n * rows, LANES).astype(BF),
        ],
        axis=1,
    )
    a_grad = links.reduce(jnp.split(d_a, n_dp, axis=0))
    small_out = a_grad[:, 4 * D :].reshape(-1)
    pieces, at = [], 0
    for size in SMALL:
        pieces.append(small_out[at : at + size // n])
        at += size // n
    g1, s1, qb, vb, pb, g2, s2, ub, db = pieces
    return (
        block_out,
        input_grad,
        g1,
        s1,
        a_grad[:, : 3 * D].reshape(-1),
        qb,
        vb,
        a_grad[:, 3 * D : 4 * D].reshape(-1),
        pb,
        g2,
        s2,
        up_grad.reshape(-1),
        ub,
        down_grad.reshape(-1),
        db,
    )


def solution(mesh):
    flat = P(AXES)
    tokens = P("dp", "seq", None)
    return jax.shard_map(
        functools.partial(per_device, mesh.shape["dp"], mesh.shape["seq"]),
        mesh=mesh,
        in_specs=(tokens, P("dp"), tokens) + (flat,) * 13,
        out_specs=(tokens, tokens) + (flat,) * 13,
        check_vma=False,
    )
```

time: 1530 us -> 563 us (0.37)
  waiting for transfers between devices: 903 us -> 219 us
  matrix products: 258 us -> 82.8 us
  blocking collectives: 149 us -> 0 us
  starting transfers between devices: 1.81 us -> 90.5 us
  local copies, waits for them, and re-layouts: 150 us -> 72 us
  Pallas kernels: 0 us -> 33.2 us
    unnamed x24 -> x0, waiting for transfers between devices: 643 us -> none
    all_gather x10 -> x0, waiting for transfers between devices: 260 us -> none  [the longest x3 81.9 us: run_forward(): lax.all_gather(values_local, 'seq', axis=0, tiled=True)]
    ppermute x0 -> x78, waiting for transfers between devices: none -> 219 us  [the longest x48 161 us: cross(): return lax.ppermute(x, AXES, pairs)]
    dot_general x54 -> x12, matrix products: 258 us -> 82.8 us  [the longest x4 32.3 us: dot(): return jnp.dot(a, b, preferred_element_type=F32)]
    ppermute x0 -> x78, starting transfers between devices: none -> 90.5 us  [the longest x48 32.4 us: cross(): return lax.ppermute(x, AXES, pairs)]
    unnamed x2 -> x0, blocking collectives: 83.2 us -> none
    all_gather x1 -> x0, blocking collectives: 66.1 us -> none  [fetch_forward(): lax.all_gather(rounded[10], ('dp', 'seq'), axis=0, tiled=True)]
    unnamed x325 -> x265, local copies, waits for them, and re-layouts: 87.5 us -> 38.9 us
  transfers between devices with their start and end apart: 17 -> 78, of which waited for: 9 -> 34; matrix products, arithmetic and copies ran while one was open for 21% -> 18% of each run, Pallas kernels for 0% -> 0%
where the time goes in v1:
time: 563 us; the launch traced here: 555 us
  waiting for transfers between devices  219 us (39%)
  starting transfers between devices  90.5 us (16%)
  matrix products  82.8 us (15%)
  local copies, waits for them, and re-layouts  72 us (13%)
  other arithmetic  41.5 us (7%)
  Pallas kernels  33.2 us (6%)
  between operations  16.3 us (3%)
    ppermute x48, waiting for transfers between devices, cross(): return lax.ppermute(x, AXES, pairs)  161 us
    ppermute x18, waiting for transfers between devices, ring(): return lax.ppermute(x, AXES, pairs)  56.3 us
    unnamed x265, local copies, waits for them, and re-layouts  38.9 us
    ppermute x48, starting transfers between devices, cross(): return lax.ppermute(x, AXES, pairs)  32.4 us
    dot_general x4, matrix products, dot(): return jnp.dot(a, b, preferred_element_type=F32)  32.3 us
    ppermute x18, starting transfers between devices, ring(): return lax.ppermute(x, AXES, pairs)  26.3 us
    dot_general x4, matrix products, dot_nt(): lax.dot_general(a, b, (((1,), (1,)), ((), ())), preferred_element_type=F32)  25.8 us
    dot_general x4, matrix products, dot_tn(): lax.dot_general(a, b, (((0,), (0,)), ((), ())), preferred_element_type=F32)  24.6 us
  transfers between devices with their start and end apart: 78, of which 34 were waited for; matrix products, arithmetic and copies ran while one was open for 18% of the time, Pallas kernels for 0%

profile of v1, /device:TPU:0, one launch (start us, length us, event | category | flops | bytes accessed | tf_op | source)
XLA Modules:
  0.0 555.3 jit_solution(14176908372448280541)
XLA Ops:
  47.6 5.6 %collective-permute-done.3 = bf16[32,4224]{1,0:T(8,128)(2,1)S(1)} collective-permute-done((bf16[32,4224]{1,0:T(8,128)(2,1)S(1)}, bf16[32,4224]{1,0:T(8,128)(2,1)S(1)}, u32[]{:S(2)}, u32[]{:S(2)}) %collective-permute-start.3) | collective-permute-done | bytes 270368 | tf_op jit(solution)/shard_map/ppermute | solution.py:125
  54.2 10.2 %collective-permute-done.26 = bf16[128,1024]{1,0:T(8,128)(2,1)S(1)} collective-permute-done((bf16[128,1024]{1,0:T(8,128)(2,1)}, bf16[128,1024]{1,0:T(8,128)(2,1)S(1)}, u32[]{:S(2)}, u32[]{:S(2)}) %collective-permute-start.26) | collective-permute-done | bytes 262176 | tf_op jit(solution)/shard_map/ppermute | solution.py:125
  71.1 4.8 collective-permute-done.27
  88.0 16.9 %collective-permute-done.29 = bf16[512,1024]{1,0:T(8,128)(2,1)S(1)} collective-permute-done((bf16[512,1024]{1,0:T(8,128)(2,1)S(1)}, bf16[512,1024]{1,0:T(8,128)(2,1)S(1)}, u32[]{:S(2)}, u32[]{:S(2)}) %collective-permute-start.29) | collective-permute-done | bytes 1048608 | tf_op jit(solution)/shard_map/ppermute | solution.py:119
  107.2 18.7 %collective-permute-done.20 = bf16[128,4096]{1,0:T(8,128)(2,1)S(1)} collective-permute-done((bf16[128,4096]{1,0:T(8,128)(2,1)S(1)}, bf16[128,4096]{1,0:T(8,128)(2,1)S(1)}, u32[]{:S(2)}, u32[]{:S(2)}) %collective-permute-start.20) | collective-permute-done | bytes 1048608 | tf_op jit(solution)/shard_map/ppermute | solution.py:119
  129.9 20.7 %collective-permute-done.7 = bf16[128,4224]{1,0:T(8,128)(2,1)S(1)} collective-permute-done((bf16[128,4224]{1,0:T(8,128)(2,1)S(1)}, bf16[128,4224]{1,0:T(8,128)(2,1)S(1)}, u32[]{:S(2)}, u32[]{:S(2)}) %collective-permute-start.7) | collective-permute-done | bytes 1081376 | tf_op jit(solution)/shard_map/ppermute | solution.py:119
  151.4 10.4 %collective-permute-done.34 = bf16[256,1024]{1,0:T(8,128)(2,1)S(1)} collective-permute-done((bf16[256,1024]{1,0:T(8,128)(2,1)S(1)}, bf16[256,1024]{1,0:T(8,128)(2,1)S(1)}, u32[]{:S(2)}, u32[]{:S(2)}) %collective-permute-start.34) | collective-permute-done | bytes 524320 | tf_op jit(solution)/shard_map/ppermute | solution.py:119
  161.8 8.3 %collective-permute-done.23 = bf16[64,4096]{1,0:T(8,128)(2,1)S(1)} collective-permute-done((bf16[64,4096]{1,0:T(8,128)(2,1)S(1)}, bf16[64,4096]{1,0:T(8,128)(2,1)S(1)}, u32[]{:S(2)}, u32[]{:S(2)}) %collective-permute-start.23) | collective-permute-done | bytes 524320 | tf_op jit(solution)/shard_map/ppermute | solution.py:119
  172.4 7.1 %collective-permute-done.12 = bf16[64,4224]{1,0:T(8,128)(2,1)S(1)} collective-permute-done((bf16[64,4224]{1,0:T(8,128)(2,1)S(1)}, bf16[64,4224]{1,0:T(8,128)(2,1)S(1)}, u32[]{:S(2)}, u32[]{:S(2)}) %collective-permute-start.12) | collective-permute-done | bytes 540704 | tf_op jit(solution)/shard_map/ppermute | solution.py:119
  200.3 7.2 %fusion.42 = f32[512,4096]{1,0:T(8,128)S(1)} fusion(bf16[4096,1024]{1,0:T(8,128)(2,1)} %copy-done.55, bf16[128,1024]{1,0:T(8,128)(2,1)S(1)} %collective-permute-done.41, bf16[128,1024]{1,0:T(8,128)(2,1)S(1)} %collective-permute-done.40, bf16[128,1024]{1,0:T(8,128)(2,1)S(1)} %collective-permute-done.39, bf16[128,1024]{1,0:T(8,128)(2,1)S(1)} %get-tuple-element.102, ...), kind=kOutput, calls=%fused_computation.294 | convolution fusion | flops 4299685888 | bytes 17825792 | tf_op jit(solution)/shard_map/dot_general | solution.py:27
  216.7 6.4 %add_convert_fusion.q_ref.k_ref.v_ref = bf16[512,3072]{1,0:T(8,128)(2,1)S(1)} fusion(bf16[512,1024]{1,0:T(8,128)(2,1)S(1)} %constant_dynamic-update-slice_fusion.20, bf16[1024,4224]{1,0:T(8,128)(2,1)} %constant_dynamic-update-slice_fusion, f32[3072]{0:T(1024)S(1)} %pad_maximum_fusion.20), kind=kOutput, calls=%fused_computation.13 | convolution fusion | flops 3224371200 | bytes 10498048 | tf_op jit(solution)/shard_map/dot_general | solution.py:23
  223.1 12.3 %shard_map.352 = bf16[512,1024]{1,0:T(8,128)(2,1)S(1)} custom-call(bf16[512,3072]{1,0:T(8,128)(2,1)S(1)} %add_convert_fusion.q_ref.k_ref.v_ref, bf16[512,3072]{1,0:T(8,128)(2,1)S(1)} %add_convert_fusion.q_ref.k_ref.v_ref, bf16[512,3072]{1,0:T(8,128)(2,1)S(1)} %add_convert_fusion.q_ref.k_ref.v_ref), custom_call_target="tpu_custom_call" | custom-call | flops 1073741824 | bytes 4194304 | tf_op jit(solution)/shard_map/pallas_call | solution.py:58
  241.7 12.7 %convert_reduce_fusion = (bf16[4096]{0:T(1024)(128)(2,1)S(1)}, bf16[512,4096]{1,0:T(8,128)(2,1)}, bf16[512,4096]{1,0:T(8,128)(2,1)}) fusion(f32[512,4096]{1,0:T(8,128)S(1)} %bitcast.148, f32[4096]{0:T(1024)S(1)} %slice_bitcast_fusion.5, bf16[512,1024]{1,0:T(8,128)(2,1)S(1)} %constant_dynamic-update-slice_fusion.36, ...), kind=kOutput, calls=%fused_computation.7 | convolution fusion | flops 4330614784 | bytes 26238976 | tf_op jit(solution)/shard_map/dot_general | solution.py:23
  254.4 8.2 %fusion.54 = f32[512,1024]{1,0:T(8,128)S(1)} fusion(bf16[512,4096]{1,0:T(8,128)(2,1)} %get-tuple-element.30, bf16[1024,4096]{1,0:T(8,128)(2,1)} %constant_dynamic-update-slice_fusion.44), kind=kOutput, calls=%fused_computation.305 | convolution fusion | flops 4294967296 | bytes 14680064 | tf_op jit(solution)/shard_map/dot_general | solution.py:27
  272.7 20.9 %shard_map.353 = (bf16[512,1024]{1,0:T(8,128)(2,1)S(1)}, bf16[512,1024]{1,0:T(8,128)(2,1)S(1)}, bf16[512,1024]{1,0:T(8,128)(2,1)S(1)}) custom-call(bf16[512,3072]{1,0:T(8,128)(2,1)} %copy-done, bf16[512,3072]{1,0:T(8,128)(2,1)} %copy-done, bf16[512,3072]{1,0:T(8,128)(2,1)} %copy-done, bf16[512,1024]{1,0:T(8,128)(2,1)S(1)} %constant_dynamic-update-slice_fusion.68.do_ref), custom_call_target="tpu_custom_call" | custom-call | flops 2684354560 | bytes 7340032 | tf_op jit(solution)/shard_map/pallas_call | solution.py:96
  294.2 7.6 %fusion.5 = f32[512,1024]{1,0:T(8,128)} fusion(bf16[512,3072]{1,0:T(8,128)(2,1)S(1)} %constant_dynamic-update-slice_fusion.76, bf16[1024,4224]{1,0:T(8,128)(2,1)} %constant_dynamic-update-slice_fusion), kind=kOutput, calls=%fused_computation.15 | convolution fusion | flops 3221225472 | bytes 11534336 | tf_op jit(solution)/shard_map/dot_general | solution.py:27
  301.7 5.4 convolution_convert_fusion.2
  307.1 6.8 %convolution_convert_fusion.1 = bf16[1024,4096]{1,0:T(8,128)(2,1)} fusion(bf16[512,1024]{1,0:T(8,128)(2,1)S(1)} %constant_dynamic-update-slice_fusion.36, bf16[512,4096]{1,0:T(8,128)(2,1)S(1)} %copy-done.68), kind=kOutput, calls=%fused_computation.12 | convolution fusion | flops 4299161600 | bytes 13631488 | tf_op jit(solution)/shard_map/dot_general | solution.py:31
  340.9 8.7 %add_convert_fusion.4 = bf16[512,1024]{1,0:T(8,128)(2,1)S(1)} fusion(f32[512,1024]{1,0:T(8,128)S(1)} %copy-done.67, bf16[512,4096]{1,0:T(8,128)(2,1)S(1)} %dynamic-slice_dynamic-update-slice_fusion.8, bf16[4096,1024]{1,0:T(8,128)(2,1)} %copy-done.55, f32[1024]{0:T(1024)S(1)} %add.710, f32[1024]{0:T(1024)S(1)} %add.672), kind=kOutput, calls=%fused_computation.58 | convolution fusion | flops 4297064448 | bytes 15736832 | tf_op jit(solution)/shard_map/dot_general | solution.py:23
  359.5 9.9 %convolution_convert_fusion = bf16[4096,1024]{1,0:T(8,128)(2,1)} fusion(bf16[512,4096]{1,0:T(8,128)(2,1)} %copy-done.53, bf16[128,1024]{1,0:T(8,128)(2,1)S(1)} %copy-done.36, bf16[128,1024]{1,0:T(8,128)(2,1)S(1)} %copy-done.39, bf16[128,1024]{1,0:T(8,128)(2,1)S(1)} %copy-done.42, bf16[128,1024]{1,0:T(8,128)(2,1)S(1)} %copy-done.23, pred[]{:T(512)S(6)} %and.169), kind=kOutput, calls=%fused_computation.11 | convolution fusion | flops 4303880192 | bytes 13631489 | tf_op jit(solution)/shard_map/dot_general | solution.py:31
  411.1 6.4 %collective-permute-done.70 = bf16[256,1024]{1,0:T(8,128)(2,1)} collective-permute-done((bf16[256,1024]{1,0:T(8,128)(2,1)}, bf16[256,1024]{1,0:T(8,128)(2,1)}, u32[]{:S(2)}, u32[]{:S(2)}) %collective-permute-start.70) | collective-permute-done | bytes 524320 | tf_op jit(solution)/shard_map/ppermute | solution.py:119
  421.9 6.7 %collective-permute-done.59 = bf16[64,4096]{1,0:T(8,128)(2,1)} collective-permute-done((bf16[64,4096]{1,0:T(8,128)(2,1)}, bf16[64,4096]{1,0:T(8,128)(2,1)}, u32[]{:S(2)}, u32[]{:S(2)}) %collective-permute-start.59) | collective-permute-done | bytes 524320 | tf_op jit(solution)/shard_map/ppermute | solution.py:119
  433.3 6.9 %collective-permute-done.48 = bf16[64,4224]{1,0:T(8,128)(2,1)S(1)} collective-permute-done((bf16[64,4224]{1,0:T(8,128)(2,1)S(1)}, bf16[64,4224]{1,0:T(8,128)(2,1)S(1)}, u32[]{:S(2)}, u32[]{:S(2)}) %collective-permute-start.48) | collective-permute-done | bytes 540704 | tf_op jit(solution)/shard_map/ppermute | solution.py:119
  444.3 18.4 %collective-permute-done.74 = bf16[512,1024]{1,0:T(8,128)(2,1)S(1)} collective-permute-done((bf16[512,1024]{1,0:T(8,128)(2,1)S(1)}, bf16[512,1024]{1,0:T(8,128)(2,1)S(1)}, u32[]{:S(2)}, u32[]{:S(2)}) %collective-permute-start.74) | collective-permute-done | bytes 1048608 | tf_op jit(solution)/shard_map/ppermute | solution.py:119
  470.9 14.2 %collective-permute-done.63 = bf16[128,4096]{1,0:T(8,128)(2,1)S(1)} collective-permute-done((bf16[128,4096]{1,0:T(8,128)(2,1)S(1)}, bf16[128,4096]{1,0:T(8,128)(2,1)S(1)}, u32[]{:S(2)}, u32[]{:S(2)}) %collective-permute-start.63) | collective-permute-done | bytes 1048608 | tf_op jit(solution)/shard_map/ppermute | solution.py:119
  492.4 15.3 %collective-permute-done.52 = bf16[128,4224]{1,0:T(8,128)(2,1)S(1)} collective-permute-done((bf16[128,4224]{1,0:T(8,128)(2,1)S(1)}, bf16[128,4224]{1,0:T(8,128)(2,1)S(1)}, u32[]{:S(2)}, u32[]{:S(2)}) %collective-permute-start.52) | collective-permute-done | bytes 1081376 | tf_op jit(solution)/shard_map/ppermute | solution.py:119
  513.5 7.4 %collective-permute-done.53 = bf16[32,4224]{1,0:T(8,128)(2,1)S(1)} collective-permute-done((bf16[32,4224]{1,0:T(8,128)(2,1)S(1)}, bf16[32,4224]{1,0:T(8,128)(2,1)S(1)}, u32[]{:S(2)}, u32[]{:S(2)}) %collective-permute-start.53) | collective-permute-done | bytes 270368 | tf_op jit(solution)/shard_map/ppermute | solution.py:125
  521.8 4.6 collective-permute-done.76
  527.5 4.6 collective-permute-done.65
  533.1 4.8 collective-permute-done.54
  538.9 4.6 collective-permute-done.77
  544.5 4.7 collective-permute-done.66
  (556 shorter events, 231.5 us)
Async XLA Ops:
  2.7 40.1 %collective-permute-start.14 = (bf16[32,4096]{1,0:T(8,128)(2,1)}, bf16[32,4096]{1,0:T(8,128)(2,1)}, u32[]{:S(2)}, u32[]{:S(2)}) collective-permute-start(bf16[32,4096]{1,0:T(8,128)(2,1)} %convert_element_type.324), channel_id=1, source_target_pairs={{0,1},{1,3},{2,0},{3,2},{4,5},{5,7},{6,4},{7,6},{8,9},{9,11},{10,8... | collective-permute-start | bytes 786440 | tf_op jit(solution)/shard_map/ppermute | solution.py:125
  7.6 36.3 %collective-permute-start.25 = (bf16[128,1024]{1,0:T(8,128)(2,1)}, bf16[128,1024]{1,0:T(8,128)(2,1)}, u32[]{:S(2)}, u32[]{:S(2)}) collective-permute-start(bf16[128,1024]{1,0:T(8,128)(2,1)} %convert_element_type.328), channel_id=1, source_target_pairs={{0,1},{1,3},{2,0},{3,2},{4,5},{5,7},{6,4},{7,6},{8,9},{9,11},{10,8... | collective-permute-start | bytes 786440 | tf_op jit(solution)/shard_map/ppermute | solution.py:125
  11.3 36.0 %collective-permute-start.2 = (bf16[128,1024]{1,0:T(8,128)(2,1)}, bf16[128,1024]{1,0:T(8,128)(2,1)S(1)}, u32[]{:S(2)}, u32[]{:S(2)}) collective-permute-start(bf16[128,1024]{1,0:T(8,128)(2,1)} %get-tuple-element.107), channel_id=1, source_target_pairs={{1,0},{2,1},{3,2},{4,7},{6,5},{7,6},{9,8},{10,9},{11,10},{12,15},{... | collective-permute-start | bytes 786440 | tf_op jit(solution)/shard_map/ppermute | solution.py:217
  12.7 34.7 %collective-permute-start.1 = (bf16[128,1024]{1,0:T(8,128)(2,1)}, bf16[128,1024]{1,0:T(8,128)(2,1)S(1)}, u32[]{:S(2)}, u32[]{:S(2)}) collective-permute-start(bf16[128,1024]{1,0:T(8,128)(2,1)} %get-tuple-element.108), channel_id=1, source_target_pairs={{0,2},{2,0},{3,1},{4,6},{5,7},{7,5},{8,10},{10,8},{11,9},{12,14},{... | collective-permute-start | bytes 786440 | tf_op jit(solution)/shard_map/ppermute | solution.py:217
  17.1 30.2 %collective-permute-start = (bf16[128,1024]{1,0:T(8,128)(2,1)}, bf16[128,1024]{1,0:T(8,128)(2,1)S(1)}, u32[]{:S(2)}, u32[]{:S(2)}) collective-permute-start(bf16[128,1024]{1,0:T(8,128)(2,1)} %get-tuple-element.109), channel_id=1, source_target_pairs={{0,1},{1,2},{3,0},{4,5},{5,6},{6,7},{8,9},{9,10},{11,8},{12,13},{1... | collective-permute-start | bytes 786440 | tf_op jit(solution)/shard_map/ppermute | solution.py:217
  77.3 29.3 %collective-permute-start.31 = (bf16[512,1024]{1,0:T(8,128)(2,1)S(1)}, bf16[512,1024]{1,0:T(8,128)(2,1)S(1)}, u32[]{:S(2)}, u32[]{:S(2)}) collective-permute-start(bf16[512,1024]{1,0:T(8,128)(2,1)S(1)} %pad_maximum_fusion.11), channel_id=1, source_target_pairs={{0,16},{1,17},{2,18},{3,19},{4,20},{5,21},{6,22},{7,23},{8,24},{9,... | collective-permute-start | bytes 3145736 | tf_op jit(solution)/shard_map/ppermute | solution.py:119
  78.9 26.1 %collective-permute-start.29 = (bf16[512,1024]{1,0:T(8,128)(2,1)S(1)}, bf16[512,1024]{1,0:T(8,128)(2,1)S(1)}, u32[]{:S(2)}, u32[]{:S(2)}) collective-permute-start(bf16[512,1024]{1,0:T(8,128)(2,1)S(1)} %pad_maximum_fusion.11), channel_id=1, source_target_pairs={{0,8},{1,9},{2,10},{3,11},{4,12},{5,13},{6,14},{7,15},{8,0},{9,1},... | collective-permute-start | bytes 3145736 | tf_op jit(solution)/shard_map/ppermute | solution.py:119
  82.9 43.0 %collective-permute-start.20 = (bf16[128,4096]{1,0:T(8,128)(2,1)S(1)}, bf16[128,4096]{1,0:T(8,128)(2,1)S(1)}, u32[]{:S(2)}, u32[]{:S(2)}) collective-permute-start(bf16[128,4096]{1,0:T(8,128)(2,1)S(1)} %pad_maximum_fusion.8), channel_id=1, source_target_pairs={{0,16},{1,17},{2,18},{3,19},{4,20},{5,21},{6,22},{7,23},{8,24},{9,... | collective-permute-start | bytes 3145736 | tf_op jit(solution)/shard_map/ppermute | solution.py:119
  85.5 41.9 %collective-permute-start.18 = (bf16[128,4096]{1,0:T(8,128)(2,1)S(1)}, bf16[128,4096]{1,0:T(8,128)(2,1)S(1)}, u32[]{:S(2)}, u32[]{:S(2)}) collective-permute-start(bf16[128,4096]{1,0:T(8,128)(2,1)S(1)} %pad_maximum_fusion.8), channel_id=1, source_target_pairs={{0,8},{1,9},{2,10},{3,11},{4,12},{5,13},{6,14},{7,15},{8,0},{9,1},... | collective-permute-start | bytes 3145736 | tf_op jit(solution)/shard_map/ppermute | solution.py:119
  87.8 41.3 %collective-permute-start.6 = (bf16[128,4224]{1,0:T(8,128)(2,1)S(1)}, bf16[128,4224]{1,0:T(8,128)(2,1)S(1)}, u32[]{:S(2)}, u32[]{:S(2)}) collective-permute-start(bf16[128,4224]{1,0:T(8,128)(2,1)S(1)} %pad_maximum_fusion.2), channel_id=1, source_target_pairs={{0,4},{1,5},{2,6},{3,7},{4,0},{5,1},{6,2},{7,3},{8,12},{9,13},{10,... | collective-permute-start | bytes 3244040 | tf_op jit(solution)/shard_map/ppermute | solution.py:119
  105.0 45.6 %collective-permute-start.7 = (bf16[128,4224]{1,0:T(8,128)(2,1)S(1)}, bf16[128,4224]{1,0:T(8,128)(2,1)S(1)}, u32[]{:S(2)}, u32[]{:S(2)}) collective-permute-start(bf16[128,4224]{1,0:T(8,128)(2,1)S(1)} %pad_maximum_fusion.2), channel_id=1, source_target_pairs={{0,8},{1,9},{2,10},{3,11},{4,12},{5,13},{6,14},{7,15},{8,0},{9,1},... | collective-permute-start | bytes 3244040 | tf_op jit(solution)/shard_map/ppermute | solution.py:119
  106.6 44.7 %collective-permute-start.9 = (bf16[128,4224]{1,0:T(8,128)(2,1)S(1)}, bf16[128,4224]{1,0:T(8,128)(2,1)S(1)}, u32[]{:S(2)}, u32[]{:S(2)}) collective-permute-start(bf16[128,4224]{1,0:T(8,128)(2,1)S(1)} %pad_maximum_fusion.2), channel_id=1, source_target_pairs={{0,16},{1,17},{2,18},{3,19},{4,20},{5,21},{6,22},{7,23},{8,24},{9,... | collective-permute-start | bytes 3244040 | tf_op jit(solution)/shard_map/ppermute | solution.py:119
  125.9 35.9 %collective-permute-start.34 = (bf16[256,1024]{1,0:T(8,128)(2,1)S(1)}, bf16[256,1024]{1,0:T(8,128)(2,1)S(1)}, u32[]{:S(2)}, u32[]{:S(2)}) collective-permute-start(bf16[256,1024]{1,0:T(8,128)(2,1)S(1)} %slice.246), channel_id=1, source_target_pairs={{0,8},{1,9},{2,10},{3,11},{4,12},{5,13},{6,14},{7,15},{8,0},{9,1},... | collective-permute-start | bytes 1572872 | tf_op jit(solution)/shard_map/ppermute | solution.py:119
  127.4 44.8 %collective-permute-start.33 = (bf16[256,1024]{1,0:T(8,128)(2,1)S(1)}, bf16[256,1024]{1,0:T(8,128)(2,1)S(1)}, u32[]{:S(2)}, u32[]{:S(2)}) collective-permute-start(bf16[256,1024]{1,0:T(8,128)(2,1)S(1)} %slice.245), channel_id=1, source_target_pairs={{0,16},{1,17},{2,18},{3,19},{4,20},{5,21},{6,22},{7,23},{8,24},{9,... | collective-permute-start | bytes 1572872 | tf_op jit(solution)/shard_map/ppermute | solution.py:119
  129.2 41.0 %collective-permute-start.23 = (bf16[64,4096]{1,0:T(8,128)(2,1)S(1)}, bf16[64,4096]{1,0:T(8,128)(2,1)S(1)}, u32[]{:S(2)}, u32[]{:S(2)}) collective-permute-start(bf16[64,4096]{1,0:T(8,128)(2,1)S(1)} %slice.243), channel_id=1, source_target_pairs={{0,8},{1,9},{2,10},{3,11},{4,12},{5,13},{6,14},{7,15},{8,0},{9,1},... | collective-permute-start | bytes 1572872 | tf_op jit(solution)/shard_map/ppermute | solution.py:119
  151.3 35.8 %collective-permute-start.32 = (bf16[512,1024]{1,0:T(8,128)(2,1)S(1)}, bf16[512,1024]{1,0:T(8,128)(2,1)S(1)}, u32[]{:S(2)}, u32[]{:S(2)}) collective-permute-start(bf16[512,1024]{1,0:T(8,128)(2,1)S(1)} %collective-permute-done.31), channel_id=1, source_target_pairs={{0,4},{1,5},{2,6},{3,7},{4,0},{5,1},{6,2},{7,3},{8,12},{9,13},{10,... | collective-permute-start | bytes 3145736 | tf_op jit(solution)/shard_map/ppermute | solution.py:119
  324.7 48.3 %collective-permute-start.44 = (bf16[128,1024]{1,0:T(8,128)(2,1)S(1)}, bf16[128,1024]{1,0:T(8,128)(2,1)S(1)}, u32[]{:S(2)}, u32[]{:S(2)}) collective-permute-start(bf16[128,1024]{1,0:T(8,128)(2,1)S(1)} %get-tuple-element.92), channel_id=1, source_target_pairs={{0,1},{1,2},{2,3},{7,4},{5,6},{6,7},{8,9},{9,10},{10,11},{15,12},{... | collective-permute-start | bytes 786440 | tf_op jit(solution)/shard_map/ppermute | solution.py:228
  328.3 46.9 %collective-permute-start.43 = (bf16[128,1024]{1,0:T(8,128)(2,1)S(1)}, bf16[128,1024]{1,0:T(8,128)(2,1)S(1)}, u32[]{:S(2)}, u32[]{:S(2)}) collective-permute-start(bf16[128,1024]{1,0:T(8,128)(2,1)S(1)} %get-tuple-element.93), channel_id=1, source_target_pairs={{2,0},{0,2},{1,3},{6,4},{7,5},{5,7},{10,8},{8,10},{9,11},{14,12},{... | collective-permute-start | bytes 786440 | tf_op jit(solution)/shard_map/ppermute | solution.py:228
  331.6 43.7 %collective-permute-start.42 = (bf16[128,1024]{1,0:T(8,128)(2,1)S(1)}, bf16[128,1024]{1,0:T(8,128)(2,1)S(1)}, u32[]{:S(2)}, u32[]{:S(2)}) collective-permute-start(bf16[128,1024]{1,0:T(8,128)(2,1)S(1)} %get-tuple-element.94), channel_id=1, source_target_pairs={{1,0},{2,1},{0,3},{5,4},{6,5},{7,6},{9,8},{10,9},{8,11},{13,12},{1... | collective-permute-start | bytes 786440 | tf_op jit(solution)/shard_map/ppermute | solution.py:228
  350.5 26.1 %collective-permute-start.38 = (bf16[128,1024]{1,0:T(8,128)(2,1)S(1)}, bf16[128,1024]{1,0:T(8,128)(2,1)S(1)}, u32[]{:S(2)}, u32[]{:S(2)}) collective-permute-start(bf16[128,1024]{1,0:T(8,128)(2,1)S(1)} %get-tuple-element.99), channel_id=1, source_target_pairs={{0,1},{1,2},{2,3},{7,4},{5,6},{6,7},{8,9},{9,10},{10,11},{15,12},{... | collective-permute-start | bytes 786440 | tf_op jit(solution)/shard_map/ppermute | solution.py:228
  354.6 25.3 %collective-permute-start.37 = (bf16[128,1024]{1,0:T(8,128)(2,1)}, bf16[128,1024]{1,0:T(8,128)(2,1)}, u32[]{:S(2)}, u32[]{:S(2)}) collective-permute-start(bf16[128,1024]{1,0:T(8,128)(2,1)} %get-tuple-element.100), channel_id=1, source_target_pairs={{2,0},{0,2},{1,3},{6,4},{7,5},{5,7},{10,8},{8,10},{9,11},{14,12},{... | collective-permute-start | bytes 786440 | tf_op jit(solution)/shard_map/ppermute | solution.py:228
  387.3 55.4 %collective-permute-start.67 = (bf16[512,1024]{1,0:T(8,128)(2,1)}, bf16[512,1024]{1,0:T(8,128)(2,1)}, u32[]{:S(2)}, u32[]{:S(2)}) collective-permute-start(bf16[512,1024]{1,0:T(8,128)(2,1)} %get-tuple-element.67), channel_id=1, source_target_pairs={{0,4},{1,5},{2,6},{3,7},{4,0},{5,1},{6,2},{7,3},{8,12},{9,13},{10,... | collective-permute-start | bytes 3145736 | tf_op jit(solution)/shard_map/ppermute | solution.py:119
  394.5 74.9 %collective-permute-start.56 = (bf16[128,4096]{1,0:T(8,128)(2,1)}, bf16[128,4096]{1,0:T(8,128)(2,1)}, u32[]{:S(2)}, u32[]{:S(2)}) collective-permute-start(bf16[128,4096]{1,0:T(8,128)(2,1)} %get-tuple-element.74), channel_id=1, source_target_pairs={{0,4},{1,5},{2,6},{3,7},{4,0},{5,1},{6,2},{7,3},{8,12},{9,13},{10,... | collective-permute-start | bytes 3145736 | tf_op jit(solution)/shard_map/ppermute | solution.py:119
  404.4 24.3 %collective-permute-start.59 = (bf16[64,4096]{1,0:T(8,128)(2,1)}, bf16[64,4096]{1,0:T(8,128)(2,1)}, u32[]{:S(2)}, u32[]{:S(2)}) collective-permute-start(bf16[64,4096]{1,0:T(8,128)(2,1)} %get-tuple-element.85), channel_id=1, source_target_pairs={{0,16},{1,17},{2,18},{3,19},{4,20},{5,21},{6,22},{7,23},{8,24},{9,... | collective-permute-start | bytes 1572872 | tf_op jit(solution)/shard_map/ppermute | solution.py:119
  431.6 31.1 %collective-permute-start.74 = (bf16[512,1024]{1,0:T(8,128)(2,1)S(1)}, bf16[512,1024]{1,0:T(8,128)(2,1)S(1)}, u32[]{:S(2)}, u32[]{:S(2)}) collective-permute-start(bf16[512,1024]{1,0:T(8,128)(2,1)S(1)} %pad_maximum_fusion.18), channel_id=1, source_target_pairs={{0,16},{1,17},{2,18},{3,19},{4,20},{5,21},{6,22},{7,23},{8,24},{9,... | collective-permute-start | bytes 3145736 | tf_op jit(solution)/shard_map/ppermute | solution.py:119
  440.2 26.2 %collective-permute-start.71 = (bf16[512,1024]{1,0:T(8,128)(2,1)S(1)}, bf16[512,1024]{1,0:T(8,128)(2,1)}, u32[]{:S(2)}, u32[]{:S(2)}) collective-permute-start(bf16[512,1024]{1,0:T(8,128)(2,1)S(1)} %pad_maximum_fusion.17), channel_id=1, source_target_pairs={{0,8},{1,9},{2,10},{3,11},{4,12},{5,13},{6,14},{7,15},{8,0},{9,1},... | collective-permute-start | bytes 3145736 | tf_op jit(solution)/shard_map/ppermute | solution.py:119
  441.9 43.2 %collective-permute-start.63 = (bf16[128,4096]{1,0:T(8,128)(2,1)S(1)}, bf16[128,4096]{1,0:T(8,128)(2,1)S(1)}, u32[]{:S(2)}, u32[]{:S(2)}) collective-permute-start(bf16[128,4096]{1,0:T(8,128)(2,1)S(1)} %pad_maximum_fusion.16), channel_id=1, source_target_pairs={{0,16},{1,17},{2,18},{3,19},{4,20},{5,21},{6,22},{7,23},{8,24},{9,... | collective-permute-start | bytes 3145736 | tf_op jit(solution)/shard_map/ppermute | solution.py:119
  442.7 46.1 %collective-permute-start.60 = (bf16[128,4096]{1,0:T(8,128)(2,1)S(1)}, bf16[128,4096]{1,0:T(8,128)(2,1)S(1)}, u32[]{:S(2)}, u32[]{:S(2)}) collective-permute-start(bf16[128,4096]{1,0:T(8,128)(2,1)S(1)} %pad_maximum_fusion.15), channel_id=1, source_target_pairs={{0,8},{1,9},{2,10},{3,11},{4,12},{5,13},{6,14},{7,15},{8,0},{9,1},... | collective-permute-start | bytes 3145736 | tf_op jit(solution)/shard_map/ppermute | solution.py:119
  462.6 29.8 %collective-permute-start.45 = (bf16[128,4224]{1,0:T(8,128)(2,1)S(1)}, bf16[128,4224]{1,0:T(8,128)(2,1)S(1)}, u32[]{:S(2)}, u32[]{:S(2)}) collective-permute-start(bf16[128,4224]{1,0:T(8,128)(2,1)S(1)} %copy-done.21), channel_id=1, source_target_pairs={{0,4},{1,5},{2,6},{3,7},{4,0},{5,1},{6,2},{7,3},{8,12},{9,13},{10,... | collective-permute-start | bytes 3244040 | tf_op jit(solution)/shard_map/ppermute | solution.py:119
  466.4 41.3 %collective-permute-start.52 = (bf16[128,4224]{1,0:T(8,128)(2,1)S(1)}, bf16[128,4224]{1,0:T(8,128)(2,1)S(1)}, u32[]{:S(2)}, u32[]{:S(2)}) collective-permute-start(bf16[128,4224]{1,0:T(8,128)(2,1)S(1)} %pad_maximum_fusion.5), channel_id=1, source_target_pairs={{0,16},{1,17},{2,18},{3,19},{4,20},{5,21},{6,22},{7,23},{8,24},{9,... | collective-permute-start | bytes 3244040 | tf_op jit(solution)/shard_map/ppermute | solution.py:119
  469.4 40.6 %collective-permute-start.49 = (bf16[128,4224]{1,0:T(8,128)(2,1)S(1)}, bf16[128,4224]{1,0:T(8,128)(2,1)S(1)}, u32[]{:S(2)}, u32[]{:S(2)}) collective-permute-start(bf16[128,4224]{1,0:T(8,128)(2,1)S(1)} %pad_maximum_fusion.4), channel_id=1, source_target_pairs={{0,8},{1,9},{2,10},{3,11},{4,12},{5,13},{6,14},{7,15},{8,0},{9,1},... | collective-permute-start | bytes 3244040 | tf_op jit(solution)/shard_map/ppermute | solution.py:119
  485.1 27.2 %collective-permute-start.75 = (bf16[128,1024]{1,0:T(8,128)(2,1)S(1)}, bf16[128,1024]{1,0:T(8,128)(2,1)S(1)}, u32[]{:S(2)}, u32[]{:S(2)}) collective-permute-start(bf16[128,1024]{1,0:T(8,128)(2,1)S(1)} %dynamic-slice_convert_fusion.1), channel_id=1, source_target_pairs={{0,1},{1,3},{2,0},{3,2},{4,5},{5,7},{6,4},{7,6},{8,9},{9,11},{10,8... | collective-permute-start | bytes 786440 | tf_op jit(solution)/shard_map/ppermute | solution.py:125
  (123 other events, 1291.2 us)

commit v2 on v1

--- a/solution.py
+++ b/solution.py
@@ -16,6 +16,7 @@
 BF = jnp.bfloat16
 F32 = jnp.float32
 AXES = ("dp", "seq")
+MESH = pl.DeviceIdType.MESH
 RING = (0, 1, 3, 2)
 
 
@@ -128,26 +129,7 @@
         return jnp.array(RING, jnp.int32)[self.z]
 
     def gather(self, shard):
-        if not self.short:
-            whole = lax.all_gather(shard, AXES, axis=0, tiled=True)
-            return list(jnp.split(whole, self.n_dp, axis=0))
-        rows = shard.shape[0]
-        held = [shard]
-        for _ in range(3):
-            held.append(self.ring(held[-1]))
-        held = jnp.stack(held)
-        place = self.place()
-        own = jnp.concatenate(
-            [lax.dynamic_index_in_dim(held, (place - RING[k]) % 4, 0, False) for k in range(4)]
-        )
-        half = 2 * rows
-        from_x = self.cross(own, 2)
-        from_y = self.cross(own, 4)
-        far = jnp.concatenate([self.cross(from_x[:half], 4), self.cross(from_y[half:], 2)])
-        blocks = []
-        for b in (own, from_x, from_y, far):
-            blocks += [b, self.cross(b, 1)]
-        return blocks
+        return lax.all_gather(shard, AXES, axis=0, tiled=True)
 
     def reduce(self, blocks):
         if not self.short:
@@ -185,9 +167,6 @@
             lax.dynamic_slice_in_dim(x, (self.dp ^ m) * width, width, axis) for m in range(self.n_dp)
         ]
 
-    def ordered(self, x, axis):
-        return jnp.concatenate(self.blocks_of(x, axis), axis=axis)
-
 
     def lead(self, d, slots):
         return d % 2 if self.n_seq > slots else 0
@@ -215,7 +194,8 @@
             index = jnp.clip((self.z + s) % n - lead, 0, slots - 1)
             part = lax.dynamic_index_in_dim(x, index, 0, False)
             parts.append(part if s == 0 else lax.ppermute(part, AXES, self.shift_pairs(s, slots)))
-        return jnp.concatenate(parts)
+        host = (clip >= 0) & (clip < slots)
+        return jnp.where(host, jnp.concatenate(parts), jnp.zeros((), x.dtype))
 
     def hand_back(self, y, slots):
         n = self.n_seq
@@ -230,6 +210,180 @@
         return jnp.stack(
             [lax.dynamic_index_in_dim(back, (c + lead - self.z) % n, 0, False) for c in range(slots)]
         )
+
+
+def guarded(cond, f):
+    if cond is None: f()
+    else: pl.when(cond)(f)
+
+class Copies:
+    def __init__(self, send, recv):
+        self.send, self.recv, self.n, self.sent = send, recv, 0, []
+        self.dp, self.z = lax.axis_index("dp"), lax.axis_index("seq")
+    def slots(self, k):
+        self.n += k
+        return list(range(self.n - k, self.n))
+    def remote(self, slot, src, dst, dev):
+        return pltpu.make_async_remote_copy(src_ref=src, dst_ref=dst, send_sem=self.send.at[slot], recv_sem=self.recv.at[slot], device_id=dev, device_id_type=MESH)
+    def start(self, slot, src, dst, dev, cond=None):
+        guarded(cond, lambda: self.remote(slot, src(), dst(), dev).start())
+        self.sent.append((slot, src, dst, dev, cond))
+    def arrived(self, slot, dst, cond=None):
+        guarded(cond, lambda: self.remote(slot, dst(), dst(), (self.dp ^ 1, self.z)).wait_recv())
+    def finish(self):
+        for slot, src, dst, dev, cond in self.sent:
+            guarded(cond, lambda: self.remote(slot, src(), dst(), dev).wait_send())
+        self.sent = []
+
+class Gather:
+    def __init__(self, io, shard, out, fine, local):
+        self.io, self.shard, self.out, self.fine = io, shard, out, fine
+        self.r = shard.shape[0]
+        self.local = pltpu.make_async_copy(shard, self.at(0, 0), local)
+        self.keys = (0, -1, 1, -2, 2, -3, 3) if fine else (None,)
+        self.z_slot = {(e * s): io.slots(1)[0] for e in (1, 2, 3) for s in (-1, 1)}
+        self.slot = {k: dict(x=io.slots(1), y=io.slots(1), d=io.slots(2), own=io.slots(1), cx=io.slots(1), cy=io.slots(1), cd=io.slots(2)) for k in self.keys}
+    def at(self, m, k, part=None):
+        io, r = self.io, self.r
+        if k is None: base, n = (io.dp ^ m) * 4 * r, 4 * r
+        else: base, n = ((io.dp ^ m) * 4 + io.z + k) * r, r
+        if part is not None: n = n // 2; base = base + part * n
+        return self.out.at[pl.ds(pl.multiple_of(base, 16), n)]
+    def ok(self, k):
+        if not k: return None
+        return (self.io.z + k >= 0) & (self.io.z + k <= 3)
+    def move(self, name, i, m, k, bit, part=None, src=None):
+        ref = lambda: self.at(m, k, part)
+        io = self.io
+        io.start(self.slot[k][name][i], src or ref, ref, (io.dp ^ bit, io.z), self.ok(k))
+    def got(self, name, i, m, k, part=None):
+        self.io.arrived(self.slot[k][name][i], lambda: self.at(m, k, part), self.ok(k))
+    def start_z(self):
+        io = self.io
+        self.local.start()
+        mine = lambda: self.shard
+        to = lambda: self.at(0, 0)
+        io.start(self.z_slot[-1], mine, to, (io.dp, io.z + 1), io.z < 3)
+        io.start(self.z_slot[1], mine, to, (io.dp, io.z - 1), io.z > 0)
+    def pass_z(self, e):
+        io = self.io
+        for s in (-1, 1):
+            k = s * e
+            ref = lambda k=k: self.at(0, k)
+            io.arrived(self.z_slot[k], ref, self.ok(k))
+            if e < 3:
+                to = io.z - s
+                io.start(self.z_slot[s * (e + 1)], ref, ref, (io.dp, to), self.ok(k) & (to >= 0) & (to <= 3))
+    def spread(self, k):
+        src = (lambda: self.shard) if k == 0 else None
+        self.move("x", 0, 0, k, 2, src=src)
+        self.move("y", 0, 0, k, 4, src=src)
+        self.move("own", 0, 0, k, 1, src=src)
+    def pass_on(self, k):
+        self.got("x", 0, 2, k)
+        self.move("d", 0, 2, k, 4, 0)
+        self.got("y", 0, 4, k)
+        self.move("d", 1, 4, k, 2, 1)
+        self.move("cx", 0, 2, k, 1)
+        self.move("cy", 0, 4, k, 1)
+    def far(self, k):
+        for h in range(2):
+            self.got("d", h, 6, k, h)
+            self.move("cd", h, 6, k, 1, h)
+    def done(self, k):
+        self.got("own", 0, 1, k)
+        self.got("cx", 0, 3, k)
+        self.got("cy", 0, 5, k)
+        for h in range(2): self.got("cd", h, 7, k, h)
+
+class Collect:
+    def __init__(self, io, src, dst, local):
+        self.io, self.src, self.dst = io, src, dst
+        self.slots = io.slots(4)
+        self.local = local
+        self.rows = src.shape[1]
+        self.host = self.valid(io.z)
+    def part(self, s): return self.dst.at[pl.ds(s * self.rows, self.rows)]
+    def valid(self, z):
+        clip = z - self.io.dp % 2
+        return (clip >= 0) & (clip < 3)
+    def start(self):
+        io = self.io
+        for s in range(4):
+            to = (io.z + s) % 4
+            src = lambda to=to: self.src.at[jnp.clip(to - io.dp % 2, 0, 2)]
+            if s == 0:
+                guarded(self.host, lambda: pltpu.make_async_copy(src(), self.part(0), self.local).start())
+            else:
+                io.start(self.slots[s], src, lambda s=s: self.part(s), (io.dp, to), self.valid(to))
+    def wait(self):
+        guarded(self.host, lambda: pltpu.make_async_copy(self.part(0), self.part(0), self.local).wait())
+        for s in range(1, 4):
+            self.io.arrived(self.slots[s], lambda s=s: self.part(s), self.host)
+
+N_SLOTS = 140
+def gather_kernel(a, u, d, x, c, wa, wu, wd, xb, cb, zero, send, recv, local):
+    io = Copies(send, recv)
+    ga, gu, gd = Gather(io, a, wa, True, local.at[0]), Gather(io, u, wu, False, local.at[1]), Gather(io, d, wd, False, local.at[2])
+    cx, cc = Collect(io, x, xb, local.at[3]), Collect(io, c, cb, local.at[4])
+    assert io.n <= N_SLOTS, io.n
+    bar = pltpu.get_barrier_semaphore()
+    partners = [(io.dp, io.z ^ k) for k in (1, 2, 3)] + [(io.dp ^ b, io.z) for b in (1, 2, 4)]
+    for p in partners: pl.semaphore_signal(bar, inc=1, device_id=p, device_id_type=MESH)
+    zero[...] = jnp.zeros_like(zero)
+    pl.semaphore_wait(bar, len(partners))
+    ga.start_z(); ga.spread(0)
+    ga.local.wait()
+    ga.pass_z(1); ga.spread(-1); ga.spread(1)
+    ga.pass_on(0)
+    ga.pass_z(2); ga.spread(-2); ga.spread(2)
+    gu.start_z()
+    ga.far(0)
+    ga.pass_on(-1); ga.pass_on(1)
+    ga.pass_z(3); ga.spread(-3); ga.spread(3)
+    gu.pass_z(1)
+    ga.far(-1); ga.far(1)
+    gu.pass_z(2)
+    cx.start()
+    ga.pass_on(-2); ga.pass_on(2)
+    gu.pass_z(3)
+    gu.local.wait()
+    gu.spread(None)
+    ga.far(-2); ga.far(2)
+    gd.start_z()
+    ga.pass_on(-3); ga.pass_on(3)
+    ga.far(-3); ga.far(3)
+    for i in ga.keys: ga.done(i)
+    gd.pass_z(1)
+    cx.wait()
+    gd.pass_z(2)
+    gd.pass_z(3)
+    gd.local.wait()
+    gd.spread(None)
+    cc.start()
+    gu.pass_on(None)
+    gu.far(None)
+    gu.done(None)
+    cc.wait()
+    gd.pass_on(None)
+    gd.far(None)
+    gd.done(None)
+    for col in (cx, cc):
+        def fill():
+            cp = pltpu.make_async_copy(zero, col.dst, local.at[5])
+            cp.start(); cp.wait()
+        guarded(jnp.logical_not(col.host), fill)
+    io.finish()
+
+def gather_all(a, u, d, x, c):
+    t = x.shape[1]*4
+    any_ = pl.BlockSpec(memory_space=pl.ANY)
+    sh = lambda r, c_: jax.ShapeDtypeStruct((r, c_), BF)
+    return pl.pallas_call(gather_kernel,
+        out_shape=[sh(32*a.shape[0], a.shape[1]), sh(32*u.shape[0], u.shape[1]), sh(32*d.shape[0], d.shape[1]), sh(t,1024), sh(t,1024)],
+        in_specs=[any_]*5, out_specs=[any_]*5,
+        scratch_shapes=[pltpu.VMEM((t,1024),BF), pltpu.SemaphoreType.DMA((N_SLOTS,)), pltpu.SemaphoreType.DMA((N_SLOTS,)), pltpu.SemaphoreType.DMA((8,))],
+        compiler_params=pltpu.CompilerParams(collective_id=0, has_side_effects=True, vmem_limit_bytes=56*2**20))(a,u,d,x,c)
 
 
 def norm_parts(v):
@@ -298,19 +452,18 @@
     shard_u = up_weight.reshape(rows, FF).astype(BF)
     shard_d = down_weight.reshape(FF // n, D).astype(BF)
 
-    x = links.collect(clips.astype(BF)).astype(F32)
-    blocks_a = links.gather(shard_a)
-    blocks_u = links.gather(shard_u)
-    out_grad = links.collect(out_cotangent.astype(BF))
-    blocks_d = links.gather(shard_d)
-
-    clip = links.my_clip(slots)
-    alive = (clip >= 0) & (clip < slots) & (clip < counts[0])
-    out_grad = jnp.where(alive, out_grad, jnp.zeros_like(out_grad))
-
-    a_mat = jnp.concatenate(blocks_a)
+    living = (jnp.arange(slots) < counts[0]).astype(F32)[:, None, None]
+    living_cot = living * out_cotangent
+    tokens = (clips.astype(BF), living_cot.astype(BF))
+    if links.short:
+        a_mat, u_mat, d_mat, x, out_grad = gather_all(shard_a, shard_u, shard_d, *tokens)
+    else:
+        a_mat, u_mat, d_mat = (links.gather(shard) for shard in (shard_a, shard_u, shard_d))
+        x, out_grad = (links.collect(t) for t in tokens)
+    x = x.astype(F32)
+
     table = a_mat[:, 4 * D :].reshape(n_dp, n_seq, rows * LANES)
-    table = links.ordered(table, 0).reshape(n, rows * LANES).astype(F32)
+    table = table.reshape(n, rows * LANES).astype(F32)
     vectors, at = [], 0
     for size in SMALL:
         vectors.append(table[:, at : at + size // n].reshape(size))
@@ -319,41 +472,35 @@
 
     vhat1, r1 = norm_parts(x)
     normed1 = (vhat1 * gain1 + shift1).astype(BF)
-    normed1_b = links.ordered(normed1, 1)
     qkv_bias = jnp.concatenate([q_bias, jnp.zeros_like(q_bias), v_bias])
     qkv_mat, proj_mat = a_mat[:, : 3 * D], a_mat[:, 3 * D : 4 * D]
-    qkv = (dot(normed1_b, qkv_mat) + qkv_bias).astype(BF)
+    qkv = (dot(normed1, qkv_mat) + qkv_bias).astype(BF)
     attended = attend(qkv)
-    attended_b = links.ordered(attended, 1)
-    branch = dot(attended_b, proj_mat) + p_bias
+    branch = dot(attended, proj_mat) + p_bias
     middle = x + branch
     vhat2, r2 = norm_parts(middle)
-    normed2_b = links.ordered((vhat2 * gain2 + shift2).astype(BF), 1)
-    u_mat = jnp.concatenate(blocks_u)
-    hidden, slope = gelu_both(dot(normed2_b, u_mat) + u_bias)
-    hidden_b = links.ordered(hidden.astype(BF), 1)
+    normed2 = (vhat2 * gain2 + shift2).astype(BF)
+    hidden, slope = gelu_both(dot(normed2, u_mat) + u_bias)
+    hidden = hidden.astype(BF)
     slope = slope.astype(BF)
-    d_mat = jnp.concatenate(blocks_d)
-    out_part = branch + dot(hidden_b, d_mat) + d_bias
-    living = (jnp.arange(slots) < counts[0]).astype(F32)[:, None, None]
+    out_part = branch + dot(hidden, d_mat) + d_bias
     block_out = living * (clips + links.hand_back(out_part.astype(BF), slots).astype(F32))
 
-    d_down = dot_tn(hidden_b, out_grad).astype(BF)
-    down_grad = links.reduce(jnp.split(d_down, n_dp, axis=0))
-    hidden_grad = links.ordered(dot_nt(out_grad, d_mat), 1)
+    d_down = dot_tn(hidden, out_grad).astype(BF)
+    down_grad = links.reduce(links.blocks_of(d_down, 0))
+    hidden_grad = dot_nt(out_grad, d_mat)
     upper_grad = (hidden_grad * slope).astype(BF)
-    d_up = dot_tn(normed2_b, upper_grad).astype(BF)
-    up_grad = links.reduce(jnp.split(d_up, n_dp, axis=0))
-    normed_grad = links.ordered(dot_nt(upper_grad, u_mat), 1)
+    d_up = dot_tn(normed2, upper_grad).astype(BF)
+    up_grad = links.reduce(links.blocks_of(d_up, 0))
+    normed_grad = dot_nt(upper_grad, u_mat)
     part, gain2_grad, shift2_grad = norm_back(vhat2, r2, gain2, normed_grad)
     middle_part = out_grad.astype(F32) + part
     branch_grad = middle_part.astype(BF)
-    attended_grad = links.ordered(dot_nt(branch_grad, proj_mat).astype(BF), 1)
+    attended_grad = dot_nt(branch_grad, proj_mat).astype(BF)
     dq, dk, dv = attend_back(qkv, attended_grad)
     joined = jnp.concatenate([dq, dk, dv], axis=1)
-    first_grad = links.ordered(dot_nt(joined, qkv_mat), 1)
+    first_grad = dot_nt(joined, qkv_mat)
     first_part, gain1_grad, shift1_grad = norm_back(vhat1, r1, gain1, first_grad)
-    living_cot = living * out_cotangent
     input_grad = living_cot + links.hand_back((part + first_part).astype(BF), slots).astype(F32)
 
     total = lambda g: jnp.sum(g.astype(F32), axis=0)
@@ -371,16 +518,15 @@
     grad_table = jnp.concatenate([g.reshape(n, -1) for g in small_grads], axis=1)
     width = grad_table.shape[1]
     grad_table = jnp.pad(grad_table, ((0, 0), (0, rows * LANES - width)))
-    grad_table = links.ordered(grad_table.reshape(n_dp, n_seq, rows * LANES), 0)
     d_a = jnp.concatenate(
         [
-            dot_tn(normed1_b, joined).astype(BF),
-            dot_tn(attended_b, branch_grad).astype(BF),
+            dot_tn(normed1, joined).astype(BF),
+            dot_tn(attended, branch_grad).astype(BF),
             grad_table.reshape(n * rows, LANES).astype(BF),
         ],
         axis=1,
     )
-    a_grad = links.reduce(jnp.split(d_a, n_dp, axis=0))
+    a_grad = links.reduce(links.blocks_of(d_a, 0))
     small_out = a_grad[:, 4 * D :].reshape(-1)
     pieces, at = [], 0
     for size in SMALL:

time: 563 us -> 507 us (0.901)
  Pallas kernels: 33.2 us -> 171 us
  waiting for transfers between devices: 219 us -> 108 us
  starting transfers between devices: 90.5 us -> 50 us
  local copies, waits for them, and re-layouts: 72 us -> 33.9 us
  between operations: 16.3 us -> 10.5 us
    pallas_call x0 -> x1, Pallas kernels: none -> 138 us  [gather_all(): pl.pallas_call(gather_kernel, out_shape=[sh(32 * a.shape[0], a.shape[1]),...]
    ppermute x48 -> x24, waiting for transfers between devices: 161 us -> 77.2 us  [cross(): return lax.ppermute(x, AXES, pairs)]
    unnamed x265 -> x91, local copies, waits for them, and re-layouts: 38.9 us -> 9.44 us
    ppermute x18 -> x9, waiting for transfers between devices: 56.3 us -> 30.9 us  [ring(): return lax.ppermute(x, AXES, pairs)]
    ppermute x6 -> x0, starting transfers between devices: 14.9 us -> none  [collect(): lax.ppermute(part, AXES, self.shift_pairs(s, slots))]
    ppermute x48 -> x24, starting transfers between devices: 32.4 us -> 17.6 us  [cross(): return lax.ppermute(x, AXES, pairs)]
    ppermute x18 -> x9, starting transfers between devices: 26.3 us -> 13.2 us  [ring(): return lax.ppermute(x, AXES, pairs)]
    dynamic_slice x0 -> x3, local copies, waits for them, and re-layouts: none -> 10.8 us  [blocks_of(): lax.dynamic_slice_in_dim(x, (self.dp ^ m) * width, width, axis)]
  transfers between devices with their start and end apart: 78 -> 39, of which waited for: 34 -> 17; matrix products, arithmetic and copies ran while one was open for 18% -> 22% of each run, Pallas kernels for 0% -> 4%
where the time goes in v2:
time: 507 us; the launch traced here: 503 us
  Pallas kernels  171 us (34%)
  waiting for transfers between devices  108 us (21%)
  matrix products  82.2 us (16%)
  starting transfers between devices  50 us (10%)
  other arithmetic  46.8 us (9%)
  local copies, waits for them, and re-layouts  33.9 us (7%)
  between operations  10.5 us (2%)
    pallas_call x1, Pallas kernels, gather_all(): pl.pallas_call(gather_kernel, out_shape=[sh(32 * a.shape[0], a.shape[1]),...  138 us
    ppermute x24, waiting for transfers between devices, cross(): return lax.ppermute(x, AXES, pairs)  77.2 us
    ppermute x9, waiting for transfers between devices, ring(): return lax.ppermute(x, AXES, pairs)  30.9 us
    dot_general x4, matrix products, dot_nt(): lax.dot_general(a, b, (((1,), (1,)), ((), ())), preferred_element_type=F32)  29.3 us
    dot_general x4, matrix products, dot_tn(): lax.dot_general(a, b, (((0,), (0,)), ((), ())), preferred_element_type=F32)  27.2 us
    dot_general x4, matrix products, dot(): return jnp.dot(a, b, preferred_element_type=F32)  25.7 us
    pallas_call x1, Pallas kernels, attend_back(): pl.pallas_call(attend_back_kernel, grid=(n,), out_shape=[jax.ShapeDtypeSt...  20.7 us
    ppermute x6, starting transfers between devices, hand_back(): back.append(part if s == 0 else lax.ppermute(part, AXES, pairs))  19.2 us
  transfers between devices with their start and end apart: 39, of which 17 were waited for; matrix products, arithmetic and copies ran while one was open for 22% of the time, Pallas kernels for 4%

profile of v2, /device:TPU:0, one launch (start us, length us, event | category | flops | bytes accessed | tf_op | source)
XLA Modules:
  0.0 502.8 jit_solution(12716421010192943426)
XLA Ops:
  16.8 138.4 %shard_map.325 = (bf16[1024,4224]{1,0:T(8,128)(2,1)}, bf16[1024,4096]{1,0:T(8,128)(2,1)}, bf16[4096,1024]{1,0:T(8,128)(2,1)}, bf16[512,1024]{1,0:T(8,128)(2,1)}, bf16[512,1024]{1,0:T(8,128)(2,1)}) custom-call(bf16[32,4224]{1,0:T(8,128)(2,1)} %pad_maximum_fusion.9.a, bf16[32,4096]{1,0:T(8,128)(2,1)} %convert_element_type.287.u, ...), custom_call_target="tpu_custom_call" | custom-call | tf_op jit(solution)/shard_map/pallas_call | solution.py:382
  157.8 7.1 %add_convert_fusion.q_ref.k_ref.v_ref = bf16[512,3072]{1,0:T(8,128)(2,1)S(1)} fusion(bf16[1024,4224]{1,0:T(8,128)(2,1)} %get-tuple-element.24, f32[3072]{0:T(1024)S(1)} %pad_maximum_fusion.10, bf16[512,1024]{1,0:T(8,128)(2,1)S(1)} %copy-done.2, f32[1024]{0:T(1024)S(1)} %add.436, f32[1024]{0:T(1024)S(1)} %mul.277, f32[512]{0:T(512)S(1)} %add_rsqrt_fusion.1, ...), kind=kOutput, calls=%fused_computation.12 | convolution fusion | flops 3227516928 | bytes 10510336 | tf_op jit(solution)/shard_map/dot_general | solution.py:24
  165.0 12.3 %shard_map.326 = bf16[512,1024]{1,0:T(8,128)(2,1)S(1)} custom-call(bf16[512,3072]{1,0:T(8,128)(2,1)S(1)} %add_convert_fusion.q_ref.k_ref.v_ref, bf16[512,3072]{1,0:T(8,128)(2,1)S(1)} %add_convert_fusion.q_ref.k_ref.v_ref, bf16[512,3072]{1,0:T(8,128)(2,1)S(1)} %add_convert_fusion.q_ref.k_ref.v_ref), custom_call_target="tpu_custom_call" | custom-call | flops 1073741824 | bytes 4194304 | tf_op jit(solution)/shard_map/pallas_call | solution.py:59
  180.9 8.6 %multiply_convert_fusion.1 = (bf16[512,4096]{1,0:T(8,128)(2,1)}, f32[512,4096]{1,0:T(8,128)}) fusion(f32[4096]{0:T(1024)S(1)} %slice_bitcast_fusion.5, bf16[1024,4096]{1,0:T(8,128)(2,1)S(1)} %bitcast.71, f32[512,1024]{1,0:T(8,128)S(1)} %get-tuple-element.42, f32[1024]{0:T(1024)S(1)} %add.446, f32[1024]{0:T(1024)S(1)} %mul.283, f32[512]{0:T(512)S(1)} %add_rsqrt_fusion, ...), kind=kOutput, calls=%fused_computation.8 | convolution fusion | flops 4310171648 | bytes 23097344 | tf_op jit(solution)/shard_map/dot_general | solution.py:24
  189.5 6.8 %add_convert_fusion.5 = bf16[512,1024]{1,0:T(8,128)(2,1)S(1)} fusion(f32[512,1024]{1,0:T(8,128)S(1)} %get-tuple-element.111, bf16[512,4096]{1,0:T(8,128)(2,1)} %get-tuple-element.114, bf16[4096,1024]{1,0:T(8,128)(2,1)S(1)} %bitcast.73, f32[1024]{0:T(1024)S(1)} %add.455, f32[1024]{0:T(1024)S(1)} %add.441), kind=kOutput, calls=%fused_computation.52 | convolution fusion | flops 4297064448 | bytes 15736832 | tf_op jit(solution)/shard_map/dot_general | solution.py:24
  204.6 12.2 %fusion.52 = (bf16[4096]{0:T(1024)(128)(2,1)S(1)}, bf16[512,4096]{1,0:T(8,128)(2,1)}) fusion(f32[512,4096]{1,0:T(8,128)} %get-tuple-element.115, f32[4096]{0:T(1024)S(1)} %slice_bitcast_fusion.5, bf16[512,1024]{1,0:T(8,128)(2,1)S(1)} %copy-done.23, bf16[4096,1024]{1,0:T(8,128)(2,1)} %get-tuple-element.26), kind=kOutput, calls=%fused_computation.156 | convolution fusion | flops 4324323328 | bytes 22044672 | tf_op jit(solution)/shard_map/dot_general | solution.py:28
  216.9 7.0 %multiply_reduce_fusion = (bf16[1024]{0:T(1024)(128)(2,1)S(1)}, f32[512]{0:T(512)S(1)}, f32[512]{0:T(512)S(1)}, bf16[1024]{0:T(1024)(128)(2,1)S(1)}, f32[512,1024]{1,0:T(8,128)S(1)}) fusion(f32[512,1024]{1,0:T(8,128)S(1)} %get-tuple-element.42, f32[512]{0:T(512)S(1)} %add_rsqrt_fusion, f32[512]{0:T(512)S(1)} %broadcast_multiply_fusion.4, ...), kind=kOutput, calls=%fused_computation.48 | convolution fusion | flops 4299682816 | bytes 16793600 | tf_op jit(solution)/shard_map/dot_general | solution.py:28
  228.8 20.7 %shard_map.327 = (bf16[512,1024]{1,0:T(8,128)(2,1)S(1)}, bf16[512,1024]{1,0:T(8,128)(2,1)S(1)}, bf16[512,1024]{1,0:T(8,128)(2,1)S(1)}) custom-call(bf16[512,3072]{1,0:T(8,128)(2,1)} %copy-done, bf16[512,3072]{1,0:T(8,128)(2,1)} %copy-done, bf16[512,3072]{1,0:T(8,128)(2,1)} %copy-done, bf16[512,1024]{1,0:T(8,128)(2,1)S(1)} %fusion.30.do_ref), custom_call_target="tpu_custom_call" | custom-call | flops 2684354560 | bytes 7340032 | tf_op jit(solution)/shard_map/pallas_call | solution.py:97
  250.1 7.2 %fusion.24 = (bf16[1024]{0:T(1024)(128)(2,1)S(1)}, f32[512]{0:T(512)S(1)}, f32[512]{0:T(512)S(1)}, bf16[1024]{0:T(1024)(128)(2,1)S(1)}, f32[512,1024]{1,0:T(8,128)S(1)}) fusion(bf16[512,1024]{1,0:T(8,128)(2,1)S(1)} %copy-done.3, f32[512]{0:T(512)S(1)} %add_rsqrt_fusion.1, f32[512]{0:T(512)S(1)} %broadcast_multiply_fusion.5, f32[1024]{0:T(1024)S(1)} %mul.277, ...), kind=kOutput, calls=%fused_computation.38 | convolution fusion | flops 3226465280 | bytes 12599296 | tf_op jit(solution)/shard_map/dot_general | solution.py:28
  259.7 4.6 collective-permute-start.5
  264.3 10.3 %convolution_convert_fusion = bf16[4096,1024]{1,0:T(8,128)(2,1)} fusion(bf16[512,4096]{1,0:T(8,128)(2,1)} %get-tuple-element.114, bf16[512,1024]{1,0:T(8,128)(2,1)} %get-tuple-element.27), kind=kOutput, calls=%fused_computation.10 | convolution fusion | flops 4299161600 | bytes 13631488 | tf_op jit(solution)/shard_map/dot_general | solution.py:32
  274.6 4.3 constant_dynamic-slice_fusion
  278.9 4.0 convolution_convert_fusion.3
  282.9 7.2 %convolution_convert_fusion.1 = bf16[1024,4096]{1,0:T(8,128)(2,1)} fusion(bf16[512,4096]{1,0:T(8,128)(2,1)S(1)} %copy-done.30, f32[512,1024]{1,0:T(8,128)S(1)} %get-tuple-element.42, f32[1024]{0:T(1024)S(1)} %add.446, f32[1024]{0:T(1024)S(1)} %mul.283, f32[512]{0:T(512)S(1)} %add_rsqrt_fusion, f32[512]{0:T(512)S(1)} %broadcast_multiply_fusion.4), kind=kOutput, calls=%fused_computation.11 | convolution fusion | flops 4301783040 | bytes 14692352 | tf_op jit(solution)/shard_map/dot_general | solution.py:32
  290.1 5.7 %convolution_convert_fusion.2 = bf16[1024,3072]{1,0:T(8,128)(2,1)} fusion(bf16[512,3072]{1,0:T(8,128)(2,1)S(1)} %copy-done.28, bf16[512,1024]{1,0:T(8,128)(2,1)S(1)} %copy-done.4, f32[1024]{0:T(1024)S(1)} %add.436, f32[1024]{0:T(1024)S(1)} %mul.277, f32[512]{0:T(512)S(1)} %add_rsqrt_fusion.1, f32[512]{0:T(512)S(1)} %broadcast_multiply_fusion.5), kind=kOutput, calls=%fused_computation.13 | convolution fusion | flops 3227516928 | bytes 10498048 | tf_op jit(solution)/shard_map/dot_general | solution.py:32
  296.8 3.7 pad_maximum_fusion
  305.4 5.1 %collective-permute-start.4 = (bf16[128,1024]{1,0:T(8,128)(2,1)}, bf16[128,1024]{1,0:T(8,128)(2,1)}, u32[]{:S(2)}, u32[]{:S(2)}) collective-permute-start(bf16[128,1024]{1,0:T(8,128)(2,1)} %get-tuple-element.80), channel_id=1, source_target_pairs={{2,0},{0,2},{1,3},{6,4},{7,5},{5,7},{10,8},{8,10},{9,11},{14,12},{... | collective-permute-start | bytes 786440 | tf_op jit(solution)/shard_map/ppermute | solution.py:208
  313.3 4.4 constant_dynamic-slice_fusion.7
  335.4 3.8 convert_add_fusion.6
  340.8 4.7 convert_add_fusion.9
  355.0 9.4 %collective-permute-done.31 = bf16[256,1024]{1,0:T(8,128)(2,1)} collective-permute-done((bf16[256,1024]{1,0:T(8,128)(2,1)}, bf16[256,1024]{1,0:T(8,128)(2,1)}, u32[]{:S(2)}, u32[]{:S(2)}) %collective-permute-start.31) | collective-permute-done | bytes 524320 | tf_op jit(solution)/shard_map/ppermute | solution.py:120
  369.6 5.9 %collective-permute-done.20 = bf16[64,4096]{1,0:T(8,128)(2,1)} collective-permute-done((bf16[64,4096]{1,0:T(8,128)(2,1)}, bf16[64,4096]{1,0:T(8,128)(2,1)}, u32[]{:S(2)}, u32[]{:S(2)}) %collective-permute-start.20) | collective-permute-done | bytes 524320 | tf_op jit(solution)/shard_map/ppermute | solution.py:120
  380.1 6.9 %collective-permute-done.9 = bf16[64,4224]{1,0:T(8,128)(2,1)S(1)} collective-permute-done((bf16[64,4224]{1,0:T(8,128)(2,1)S(1)}, bf16[64,4224]{1,0:T(8,128)(2,1)S(1)}, u32[]{:S(2)}, u32[]{:S(2)}) %collective-permute-start.9) | collective-permute-done | bytes 540704 | tf_op jit(solution)/shard_map/ppermute | solution.py:120
  392.1 17.4 %collective-permute-done.35 = bf16[512,1024]{1,0:T(8,128)(2,1)S(1)} collective-permute-done((bf16[512,1024]{1,0:T(8,128)(2,1)S(1)}, bf16[512,1024]{1,0:T(8,128)(2,1)S(1)}, u32[]{:S(2)}, u32[]{:S(2)}) %collective-permute-start.35) | collective-permute-done | bytes 1048608 | tf_op jit(solution)/shard_map/ppermute | solution.py:120
  418.1 13.9 %collective-permute-done.24 = bf16[128,4096]{1,0:T(8,128)(2,1)S(1)} collective-permute-done((bf16[128,4096]{1,0:T(8,128)(2,1)S(1)}, bf16[128,4096]{1,0:T(8,128)(2,1)S(1)}, u32[]{:S(2)}, u32[]{:S(2)}) %collective-permute-start.24) | collective-permute-done | bytes 1048608 | tf_op jit(solution)/shard_map/ppermute | solution.py:120
  439.6 15.1 %collective-permute-done.13 = bf16[128,4224]{1,0:T(8,128)(2,1)S(1)} collective-permute-done((bf16[128,4224]{1,0:T(8,128)(2,1)S(1)}, bf16[128,4224]{1,0:T(8,128)(2,1)S(1)}, u32[]{:S(2)}, u32[]{:S(2)}) %collective-permute-start.13) | collective-permute-done | bytes 1081376 | tf_op jit(solution)/shard_map/ppermute | solution.py:120
  463.1 5.1 %collective-permute-done.14 = bf16[32,4224]{1,0:T(8,128)(2,1)S(1)} collective-permute-done((bf16[32,4224]{1,0:T(8,128)(2,1)S(1)}, bf16[32,4224]{1,0:T(8,128)(2,1)S(1)}, u32[]{:S(2)}, u32[]{:S(2)}) %collective-permute-start.14) | collective-permute-done | bytes 270368 | tf_op jit(solution)/shard_map/ppermute | solution.py:126
  469.2 4.6 collective-permute-done.37
  474.8 4.6 collective-permute-done.26
  480.4 4.8 collective-permute-done.15
  486.2 4.6 collective-permute-done.38
  491.8 4.7 collective-permute-done.27
  (274 shorter events, 117.2 us)
Async XLA Ops:
  197.2 108.2 %collective-permute-start.2 = (bf16[128,1024]{1,0:T(8,128)(2,1)}, bf16[128,1024]{1,0:T(8,128)(2,1)}, u32[]{:S(2)}, u32[]{:S(2)}) collective-permute-start(bf16[128,1024]{1,0:T(8,128)(2,1)} %get-tuple-element.86), channel_id=1, source_target_pairs={{0,1},{1,2},{2,3},{7,4},{5,6},{6,7},{8,9},{9,10},{10,11},{15,12},{... | collective-permute-start | bytes 786440 | tf_op jit(solution)/shard_map/ppermute | solution.py:208
  199.2 111.3 %collective-permute-start.1 = (bf16[128,1024]{1,0:T(8,128)(2,1)}, bf16[128,1024]{1,0:T(8,128)(2,1)}, u32[]{:S(2)}, u32[]{:S(2)}) collective-permute-start(bf16[128,1024]{1,0:T(8,128)(2,1)} %get-tuple-element.87), channel_id=1, source_target_pairs={{2,0},{0,2},{1,3},{6,4},{7,5},{5,7},{10,8},{8,10},{9,11},{14,12},{... | collective-permute-start | bytes 786440 | tf_op jit(solution)/shard_map/ppermute | solution.py:208
  202.7 110.0 %collective-permute-start = (bf16[128,1024]{1,0:T(8,128)(2,1)}, bf16[128,1024]{1,0:T(8,128)(2,1)}, u32[]{:S(2)}, u32[]{:S(2)}) collective-permute-start(bf16[128,1024]{1,0:T(8,128)(2,1)} %get-tuple-element.88), channel_id=1, source_target_pairs={{1,0},{2,1},{0,3},{5,4},{6,5},{7,6},{9,8},{10,9},{8,11},{13,12},{1... | collective-permute-start | bytes 786440 | tf_op jit(solution)/shard_map/ppermute | solution.py:208
  259.7 53.0 %collective-permute-start.5 = (bf16[128,1024]{1,0:T(8,128)(2,1)}, bf16[128,1024]{1,0:T(8,128)(2,1)}, u32[]{:S(2)}, u32[]{:S(2)}) collective-permute-start(bf16[128,1024]{1,0:T(8,128)(2,1)} %get-tuple-element.79), channel_id=1, source_target_pairs={{0,1},{1,2},{2,3},{7,4},{5,6},{6,7},{8,9},{9,10},{10,11},{15,12},{... | collective-permute-start | bytes 786440 | tf_op jit(solution)/shard_map/ppermute | solution.py:208
  278.9 51.3 %collective-permute-start.33 = (bf16[512,1024]{1,0:T(8,128)(2,1)}, bf16[512,1024]{1,0:T(8,128)(2,1)}, u32[]{:S(2)}, u32[]{:S(2)}) collective-permute-start(bf16[512,1024]{1,0:T(8,128)(2,1)} %get-tuple-element.51), channel_id=1, source_target_pairs={{0,4},{1,5},{2,6},{3,7},{4,0},{5,1},{6,2},{7,3},{8,12},{9,13},{10,... | collective-permute-start | bytes 3145736 | tf_op jit(solution)/shard_map/ppermute | solution.py:120
  305.4 22.8 %collective-permute-start.4 = (bf16[128,1024]{1,0:T(8,128)(2,1)}, bf16[128,1024]{1,0:T(8,128)(2,1)}, u32[]{:S(2)}, u32[]{:S(2)}) collective-permute-start(bf16[128,1024]{1,0:T(8,128)(2,1)} %get-tuple-element.80), channel_id=1, source_target_pairs={{2,0},{0,2},{1,3},{6,4},{7,5},{5,7},{10,8},{8,10},{9,11},{14,12},{... | collective-permute-start | bytes 786440 | tf_op jit(solution)/shard_map/ppermute | solution.py:208
  310.6 17.8 %collective-permute-start.3 = (bf16[128,1024]{1,0:T(8,128)(2,1)}, bf16[128,1024]{1,0:T(8,128)(2,1)}, u32[]{:S(2)}, u32[]{:S(2)}) collective-permute-start(bf16[128,1024]{1,0:T(8,128)(2,1)} %get-tuple-element.81), channel_id=1, source_target_pairs={{1,0},{2,1},{0,3},{5,4},{6,5},{7,6},{9,8},{10,9},{8,11},{13,12},{1... | collective-permute-start | bytes 786440 | tf_op jit(solution)/shard_map/ppermute | solution.py:208
  312.7 21.6 %collective-permute-start.30 = (bf16[512,1024]{1,0:T(8,128)(2,1)S(1)}, bf16[512,1024]{1,0:T(8,128)(2,1)S(1)}, u32[]{:S(2)}, u32[]{:S(2)}) collective-permute-start(bf16[512,1024]{1,0:T(8,128)(2,1)S(1)} %copy-done.22), channel_id=1, source_target_pairs={{0,4},{1,5},{2,6},{3,7},{4,0},{5,1},{6,2},{7,3},{8,12},{9,13},{10,... | collective-permute-start | bytes 3145736 | tf_op jit(solution)/shard_map/ppermute | solution.py:120
  312.8 21.6 %collective-permute-start.29 = (bf16[512,1024]{1,0:T(8,128)(2,1)S(1)}, bf16[512,1024]{1,0:T(8,128)(2,1)}, u32[]{:S(2)}, u32[]{:S(2)}) collective-permute-start(bf16[512,1024]{1,0:T(8,128)(2,1)S(1)} %copy-done.21), channel_id=1, source_target_pairs={{0,4},{1,5},{2,6},{3,7},{4,0},{5,1},{6,2},{7,3},{8,12},{9,13},{10,... | collective-permute-start | bytes 3145736 | tf_op jit(solution)/shard_map/ppermute | solution.py:120
  334.3 56.0 %collective-permute-start.28 = (bf16[512,1024]{1,0:T(8,128)(2,1)}, bf16[512,1024]{1,0:T(8,128)(2,1)}, u32[]{:S(2)}, u32[]{:S(2)}) collective-permute-start(bf16[512,1024]{1,0:T(8,128)(2,1)} %get-tuple-element.50), channel_id=1, source_target_pairs={{0,4},{1,5},{2,6},{3,7},{4,0},{5,1},{6,2},{7,3},{8,12},{9,13},{10,... | collective-permute-start | bytes 3145736 | tf_op jit(solution)/shard_map/ppermute | solution.py:120
  334.4 81.7 %collective-permute-start.17 = (bf16[128,4096]{1,0:T(8,128)(2,1)}, bf16[128,4096]{1,0:T(8,128)(2,1)}, u32[]{:S(2)}, u32[]{:S(2)}) collective-permute-start(bf16[128,4096]{1,0:T(8,128)(2,1)} %get-tuple-element.57), channel_id=1, source_target_pairs={{0,4},{1,5},{2,6},{3,7},{4,0},{5,1},{6,2},{7,3},{8,12},{9,13},{10,... | collective-permute-start | bytes 3145736 | tf_op jit(solution)/shard_map/ppermute | solution.py:120
  349.3 15.0 %collective-permute-start.31 = (bf16[256,1024]{1,0:T(8,128)(2,1)}, bf16[256,1024]{1,0:T(8,128)(2,1)}, u32[]{:S(2)}, u32[]{:S(2)}) collective-permute-start(bf16[256,1024]{1,0:T(8,128)(2,1)} %get-tuple-element.66), channel_id=1, source_target_pairs={{0,16},{1,17},{2,18},{3,19},{4,20},{5,21},{6,22},{7,23},{8,24},{9,... | collective-permute-start | bytes 1572872 | tf_op jit(solution)/shard_map/ppermute | solution.py:120
  349.3 17.1 %collective-permute-start.34 = (bf16[256,1024]{1,0:T(8,128)(2,1)}, bf16[256,1024]{1,0:T(8,128)(2,1)}, u32[]{:S(2)}, u32[]{:S(2)}) collective-permute-start(bf16[256,1024]{1,0:T(8,128)(2,1)} %get-tuple-element.67), channel_id=1, source_target_pairs={{0,8},{1,9},{2,10},{3,11},{4,12},{5,13},{6,14},{7,15},{8,0},{9,1},... | collective-permute-start | bytes 1572872 | tf_op jit(solution)/shard_map/ppermute | solution.py:120
  352.1 23.5 %collective-permute-start.20 = (bf16[64,4096]{1,0:T(8,128)(2,1)}, bf16[64,4096]{1,0:T(8,128)(2,1)}, u32[]{:S(2)}, u32[]{:S(2)}) collective-permute-start(bf16[64,4096]{1,0:T(8,128)(2,1)} %get-tuple-element.68), channel_id=1, source_target_pairs={{0,16},{1,17},{2,18},{3,19},{4,20},{5,21},{6,22},{7,23},{8,24},{9,... | collective-permute-start | bytes 1572872 | tf_op jit(solution)/shard_map/ppermute | solution.py:120
  364.3 13.4 %collective-permute-start.23 = (bf16[64,4096]{1,0:T(8,128)(2,1)S(1)}, bf16[64,4096]{1,0:T(8,128)(2,1)S(1)}, u32[]{:S(2)}, u32[]{:S(2)}) collective-permute-start(bf16[64,4096]{1,0:T(8,128)(2,1)S(1)} %copy-done.26), channel_id=1, source_target_pairs={{0,8},{1,9},{2,10},{3,11},{4,12},{5,13},{6,14},{7,15},{8,0},{9,1},... | collective-permute-start | bytes 1572872 | tf_op jit(solution)/shard_map/ppermute | solution.py:120
  366.4 20.6 %collective-permute-start.9 = (bf16[64,4224]{1,0:T(8,128)(2,1)S(1)}, bf16[64,4224]{1,0:T(8,128)(2,1)S(1)}, u32[]{:S(2)}, u32[]{:S(2)}) collective-permute-start(bf16[64,4224]{1,0:T(8,128)(2,1)S(1)} %get-tuple-element.64), channel_id=1, source_target_pairs={{0,16},{1,17},{2,18},{3,19},{4,20},{5,21},{6,22},{7,23},{8,24},{9,... | collective-permute-start | bytes 1622024 | tf_op jit(solution)/shard_map/ppermute | solution.py:120
  375.6 13.4 %collective-permute-start.12 = (bf16[64,4224]{1,0:T(8,128)(2,1)S(1)}, bf16[64,4224]{1,0:T(8,128)(2,1)S(1)}, u32[]{:S(2)}, u32[]{:S(2)}) collective-permute-start(bf16[64,4224]{1,0:T(8,128)(2,1)S(1)} %get-tuple-element.65), channel_id=1, source_target_pairs={{0,8},{1,9},{2,10},{3,11},{4,12},{5,13},{6,14},{7,15},{8,0},{9,1},... | collective-permute-start | bytes 1622024 | tf_op jit(solution)/shard_map/ppermute | solution.py:120
  377.8 31.7 %collective-permute-start.35 = (bf16[512,1024]{1,0:T(8,128)(2,1)S(1)}, bf16[512,1024]{1,0:T(8,128)(2,1)S(1)}, u32[]{:S(2)}, u32[]{:S(2)}) collective-permute-start(bf16[512,1024]{1,0:T(8,128)(2,1)S(1)} %pad_maximum_fusion.8), channel_id=1, source_target_pairs={{0,16},{1,17},{2,18},{3,19},{4,20},{5,21},{6,22},{7,23},{8,24},{9,... | collective-permute-start | bytes 3145736 | tf_op jit(solution)/shard_map/ppermute | solution.py:120
  387.1 26.1 %collective-permute-start.32 = (bf16[512,1024]{1,0:T(8,128)(2,1)S(1)}, bf16[512,1024]{1,0:T(8,128)(2,1)S(1)}, u32[]{:S(2)}, u32[]{:S(2)}) collective-permute-start(bf16[512,1024]{1,0:T(8,128)(2,1)S(1)} %pad_maximum_fusion.7), channel_id=1, source_target_pairs={{0,8},{1,9},{2,10},{3,11},{4,12},{5,13},{6,14},{7,15},{8,0},{9,1},... | collective-permute-start | bytes 3145736 | tf_op jit(solution)/shard_map/ppermute | solution.py:120
  389.0 43.0 %collective-permute-start.24 = (bf16[128,4096]{1,0:T(8,128)(2,1)S(1)}, bf16[128,4096]{1,0:T(8,128)(2,1)S(1)}, u32[]{:S(2)}, u32[]{:S(2)}) collective-permute-start(bf16[128,4096]{1,0:T(8,128)(2,1)S(1)} %pad_maximum_fusion.6), channel_id=1, source_target_pairs={{0,16},{1,17},{2,18},{3,19},{4,20},{5,21},{6,22},{7,23},{8,24},{9,... | collective-permute-start | bytes 3145736 | tf_op jit(solution)/shard_map/ppermute | solution.py:120
  390.2 45.4 %collective-permute-start.21 = (bf16[128,4096]{1,0:T(8,128)(2,1)S(1)}, bf16[128,4096]{1,0:T(8,128)(2,1)S(1)}, u32[]{:S(2)}, u32[]{:S(2)}) collective-permute-start(bf16[128,4096]{1,0:T(8,128)(2,1)S(1)} %pad_maximum_fusion.5), channel_id=1, source_target_pairs={{0,8},{1,9},{2,10},{3,11},{4,12},{5,13},{6,14},{7,15},{8,0},{9,1},... | collective-permute-start | bytes 3145736 | tf_op jit(solution)/shard_map/ppermute | solution.py:120
  409.5 30.1 %collective-permute-start.6 = (bf16[128,4224]{1,0:T(8,128)(2,1)S(1)}, bf16[128,4224]{1,0:T(8,128)(2,1)S(1)}, u32[]{:S(2)}, u32[]{:S(2)}) collective-permute-start(bf16[128,4224]{1,0:T(8,128)(2,1)S(1)} %copy-done.20), channel_id=1, source_target_pairs={{0,4},{1,5},{2,6},{3,7},{4,0},{5,1},{6,2},{7,3},{8,12},{9,13},{10,... | collective-permute-start | bytes 3244040 | tf_op jit(solution)/shard_map/ppermute | solution.py:120
  413.2 41.5 %collective-permute-start.13 = (bf16[128,4224]{1,0:T(8,128)(2,1)S(1)}, bf16[128,4224]{1,0:T(8,128)(2,1)S(1)}, u32[]{:S(2)}, u32[]{:S(2)}) collective-permute-start(bf16[128,4224]{1,0:T(8,128)(2,1)S(1)} %pad_maximum_fusion.2), channel_id=1, source_target_pairs={{0,16},{1,17},{2,18},{3,19},{4,20},{5,21},{6,22},{7,23},{8,24},{9,... | collective-permute-start | bytes 3244040 | tf_op jit(solution)/shard_map/ppermute | solution.py:120
  416.0 41.0 %collective-permute-start.10 = (bf16[128,4224]{1,0:T(8,128)(2,1)S(1)}, bf16[128,4224]{1,0:T(8,128)(2,1)S(1)}, u32[]{:S(2)}, u32[]{:S(2)}) collective-permute-start(bf16[128,4224]{1,0:T(8,128)(2,1)S(1)} %pad_maximum_fusion.1), channel_id=1, source_target_pairs={{0,8},{1,9},{2,10},{3,11},{4,12},{5,13},{6,14},{7,15},{8,0},{9,1},... | collective-permute-start | bytes 3244040 | tf_op jit(solution)/shard_map/ppermute | solution.py:120
  432.0 27.7 %collective-permute-start.36 = (bf16[128,1024]{1,0:T(8,128)(2,1)S(1)}, bf16[128,1024]{1,0:T(8,128)(2,1)S(1)}, u32[]{:S(2)}, u32[]{:S(2)}) collective-permute-start(bf16[128,1024]{1,0:T(8,128)(2,1)S(1)} %dynamic-slice_convert_fusion.1), channel_id=1, source_target_pairs={{0,1},{1,3},{2,0},{3,2},{4,5},{5,7},{6,4},{7,6},{8,9},{9,11},{10,8... | collective-permute-start | bytes 786440 | tf_op jit(solution)/shard_map/ppermute | solution.py:126
  437.5 23.1 %collective-permute-start.25 = (bf16[32,4096]{1,0:T(8,128)(2,1)S(1)}, bf16[32,4096]{1,0:T(8,128)(2,1)S(1)}, u32[]{:S(2)}, u32[]{:S(2)}) collective-permute-start(bf16[32,4096]{1,0:T(8,128)(2,1)S(1)} %dynamic-slice_convert_fusion.2), channel_id=1, source_target_pairs={{0,1},{1,3},{2,0},{3,2},{4,5},{5,7},{6,4},{7,6},{8,9},{9,11},{10,8... | collective-permute-start | bytes 786440 | tf_op jit(solution)/shard_map/ppermute | solution.py:126
  459.7 14.1 %collective-permute-start.37 = (bf16[128,1024]{1,0:T(8,128)(2,1)S(1)}, bf16[128,1024]{1,0:T(8,128)(2,1)S(1)}, u32[]{:S(2)}, u32[]{:S(2)}) collective-permute-start(bf16[128,1024]{1,0:T(8,128)(2,1)S(1)} %add_convert_fusion.10), channel_id=1, source_target_pairs={{0,1},{1,3},{2,0},{3,2},{4,5},{5,7},{6,4},{7,6},{8,9},{9,11},{10,8... | collective-permute-start | bytes 786440 | tf_op jit(solution)/shard_map/ppermute | solution.py:126
  460.7 18.8 %collective-permute-start.26 = (bf16[32,4096]{1,0:T(8,128)(2,1)S(1)}, bf16[32,4096]{1,0:T(8,128)(2,1)S(1)}, u32[]{:S(2)}, u32[]{:S(2)}) collective-permute-start(bf16[32,4096]{1,0:T(8,128)(2,1)S(1)} %add_convert_fusion.12), channel_id=1, source_target_pairs={{0,1},{1,3},{2,0},{3,2},{4,5},{5,7},{6,4},{7,6},{8,9},{9,11},{10,8... | collective-permute-start | bytes 786440 | tf_op jit(solution)/shard_map/ppermute | solution.py:126
  468.3 17.0 %collective-permute-start.15 = (bf16[32,4224]{1,0:T(8,128)(2,1)S(1)}, bf16[32,4224]{1,0:T(8,128)(2,1)S(1)}, u32[]{:S(2)}, u32[]{:S(2)}) collective-permute-start(bf16[32,4224]{1,0:T(8,128)(2,1)S(1)} %add_convert_fusion.8), channel_id=1, source_target_pairs={{0,1},{1,3},{2,0},{3,2},{4,5},{5,7},{6,4},{7,6},{8,9},{9,11},{10,8... | collective-permute-start | bytes 811016 | tf_op jit(solution)/shard_map/ppermute | solution.py:126
  473.9 17.0 %collective-permute-start.38 = (bf16[128,1024]{1,0:T(8,128)(2,1)S(1)}, bf16[128,1024]{1,0:T(8,128)(2,1)S(1)}, u32[]{:S(2)}, u32[]{:S(2)}) collective-permute-start(bf16[128,1024]{1,0:T(8,128)(2,1)S(1)} %add_convert_fusion.9), channel_id=1, source_target_pairs={{0,1},{1,3},{2,0},{3,2},{4,5},{5,7},{6,4},{7,6},{8,9},{9,11},{10,8... | collective-permute-start | bytes 786440 | tf_op jit(solution)/shard_map/ppermute | solution.py:126
  479.5 17.0 %collective-permute-start.27 = (bf16[32,4096]{1,0:T(8,128)(2,1)S(1)}, bf16[32,4096]{1,0:T(8,128)(2,1)S(1)}, u32[]{:S(2)}, u32[]{:S(2)}) collective-permute-start(bf16[32,4096]{1,0:T(8,128)(2,1)S(1)} %add_convert_fusion.11), channel_id=1, source_target_pairs={{0,1},{1,3},{2,0},{3,2},{4,5},{5,7},{6,4},{7,6},{8,9},{9,11},{10,8... | collective-permute-start | bytes 786440 | tf_op jit(solution)/shard_map/ppermute | solution.py:126
  485.3 14.6 %collective-permute-start.16 = (bf16[32,4224]{1,0:T(8,128)(2,1)S(1)}, bf16[32,4224]{1,0:T(8,128)(2,1)S(1)}, u32[]{:S(2)}, u32[]{:S(2)}) collective-permute-start(bf16[32,4224]{1,0:T(8,128)(2,1)S(1)} %add_convert_fusion.7), channel_id=1, source_target_pairs={{0,1},{1,3},{2,0},{3,2},{4,5},{5,7},{6,4},{7,6},{8,9},{9,11},{10,8... | collective-permute-start | bytes 811016 | tf_op jit(solution)/shard_map/ppermute | solution.py:126
  (49 other events, 377.3 us)

commit v3 on v2

--- a/solution.py
+++ b/solution.py
@@ -17,7 +17,6 @@
 F32 = jnp.float32
 AXES = ("dp", "seq")
 MESH = pl.DeviceIdType.MESH
-RING = (0, 1, 3, 2)
 
 
 def dot(a, b):
@@ -69,8 +68,7 @@
     )(qkv, qkv, qkv)
 
 
-def attend_back_kernel(q_ref, k_ref, v_ref, do_ref, dq_ref, dk_ref, dv_ref):
-    q2, k2, v2, do2 = q_ref[...], k_ref[...], v_ref[...], do_ref[...]
+def attend_back_pair(q2, k2, v2, do2):
     low = lax.broadcasted_iota(jnp.int32, k2.shape, 1) < HEAD_DIM
     k_t = k2.T
     zero = jnp.zeros_like(k2)
@@ -85,9 +83,16 @@
         dk.append(dot(ds, q2))
         dq.append(dot(k_t[h * HEAD_DIM : (h + 1) * HEAD_DIM], ds))
     scale = HEAD_DIM**-0.5
-    dq_ref[...] = (jnp.concatenate(dq, axis=0).T * scale).astype(BF)
-    dk_ref[...] = (jnp.where(low, dk[0], dk[1]) * scale).astype(BF)
-    dv_ref[...] = jnp.where(low, dv[0], dv[1]).astype(BF)
+    return (
+        (jnp.concatenate(dq, axis=0).T * scale).astype(BF),
+        (jnp.where(low, dk[0], dk[1]) * scale).astype(BF),
+        jnp.where(low, dv[0], dv[1]).astype(BF),
+    )
+
+
+def attend_back_kernel(q_ref, k_ref, v_ref, do_ref, dq_ref, dk_ref, dv_ref):
+    grads = attend_back_pair(q_ref[...], k_ref[...], v_ref[...], do_ref[...])
+    dq_ref[...], dk_ref[...], dv_ref[...] = grads
 
 
 def attend_back(qkv, do):
@@ -110,62 +115,15 @@
 class Links:
     def __init__(self, n_dp, n_seq):
         self.n_dp, self.n_seq = n_dp, n_seq
-        self.short = n_dp == 8 and n_seq == len(RING)
+        self.short = n_dp == 8 and n_seq == 4
         self.dp = lax.axis_index("dp")
         self.z = lax.axis_index("seq")
 
-    def cross(self, x, bit):
-        s = self.n_seq
-        pairs = [(d * s + z, (d ^ bit) * s + z) for d in range(self.n_dp) for z in range(s)]
-        return lax.ppermute(x, AXES, pairs)
-
-    def ring(self, x):
-        s = self.n_seq
-        step = {RING[i]: RING[(i + 1) % s] for i in range(s)}
-        pairs = [(d * s + z, d * s + step[z]) for d in range(self.n_dp) for z in range(s)]
-        return lax.ppermute(x, AXES, pairs)
-
-    def place(self):
-        return jnp.array(RING, jnp.int32)[self.z]
-
     def gather(self, shard):
         return lax.all_gather(shard, AXES, axis=0, tiled=True)
 
-    def reduce(self, blocks):
-        if not self.short:
-            whole = jnp.concatenate(blocks).astype(BF)
-            return lax.psum_scatter(whole, AXES, scatter_dimension=0, tiled=True).astype(F32)
-        sums = []
-        for j in (3, 1, 2, 0):
-            theirs = self.cross(blocks[2 * j + 1].astype(BF), 1)
-            sums.append(blocks[2 * j].astype(F32) + theirs.astype(F32))
-        far, to_x, to_y, own = sums
-        half = far.shape[0] // 2
-        far = far.astype(BF)
-        low = self.cross(far[:half], 2).astype(F32)
-        high = self.cross(far[half:], 4).astype(F32)
-        to_y = jnp.concatenate([to_y[:half] + low, to_y[half:]])
-        to_x = jnp.concatenate([to_x[:half], to_x[half:] + high])
-        own = own + self.cross(to_x.astype(BF), 2).astype(F32) + self.cross(to_y.astype(BF), 4).astype(F32)
-        rows = own.shape[0] // 4
-        place = self.place()
-        order = jnp.array(RING, jnp.int32)
-
-        def piece(back):
-            return lax.dynamic_slice_in_dim(own, order[(place - back) % 4] * rows, rows, 0)
-
-        moving = self.ring(piece(1).astype(BF))
-        for back in (2, 3):
-            moving = self.ring((piece(back) + moving.astype(F32)).astype(BF))
-        return piece(4) + moving.astype(F32)
-
-    def blocks_of(self, x, axis):
-        width = x.shape[axis] // self.n_dp
-        if not self.short:
-            return jnp.split(x, self.n_dp, axis=axis)
-        return [
-            lax.dynamic_slice_in_dim(x, (self.dp ^ m) * width, width, axis) for m in range(self.n_dp)
-        ]
+    def reduce(self, grad):
+        return lax.psum_scatter(grad.astype(BF), AXES, scatter_dimension=0, tiled=True).astype(F32)
 
 
     def lead(self, d, slots):
@@ -200,13 +158,16 @@
     def hand_back(self, y, slots):
         n = self.n_seq
         rows = y.shape[0] // n
-        lead = self.z - self.my_clip(slots)
         back = []
         for s in range(n):
             part = y[s * rows : (s + 1) * rows]
             pairs = [(b, a) for a, b in self.shift_pairs(s, slots)]
             back.append(part if s == 0 else lax.ppermute(part, AXES, pairs))
-        back = jnp.stack(back)
+        return self.by_clip(jnp.stack(back), slots)
+
+    def by_clip(self, back, slots):
+        n = self.n_seq
+        lead = self.z - self.my_clip(slots)
         return jnp.stack(
             [lax.dynamic_index_in_dim(back, (c + lead - self.z) % n, 0, False) for c in range(slots)]
         )
@@ -217,8 +178,9 @@
     else: pl.when(cond)(f)
 
 class Copies:
-    def __init__(self, send, recv):
+    def __init__(self, send, recv, local=None):
         self.send, self.recv, self.n, self.sent = send, recv, 0, []
+        self.local, self.n_local = local, 0
         self.dp, self.z = lax.axis_index("dp"), lax.axis_index("seq")
     def slots(self, k):
         self.n += k
@@ -230,10 +192,23 @@
         self.sent.append((slot, src, dst, dev, cond))
     def arrived(self, slot, dst, cond=None):
         guarded(cond, lambda: self.remote(slot, dst(), dst(), (self.dp ^ 1, self.z)).wait_recv())
+    def sent_wait(self, which=None):
+        rest = []
+        for slot, src, dst, dev, cond in self.sent:
+            if which is None or slot == which:
+                guarded(cond, lambda: self.remote(slot, src(), dst(), dev).wait_send())
+            else:
+                rest.append((slot, src, dst, dev, cond))
+        self.sent = rest
     def finish(self):
-        for slot, src, dst, dev, cond in self.sent:
-            guarded(cond, lambda: self.remote(slot, src(), dst(), dev).wait_send())
-        self.sent = []
+        self.sent_wait()
+    def locals(self, k):
+        self.n_local += k
+        return self.n_local - k
+    def load(self, src, dst):
+        copy = pltpu.make_async_copy(src, dst, self.local.at[self.locals(1)])
+        copy.start()
+        return copy
 
 class Gather:
     def __init__(self, io, shard, out, fine, local):
@@ -386,6 +361,485 @@
         compiler_params=pltpu.CompilerParams(collective_id=0, has_side_effects=True, vmem_limit_bytes=56*2**20))(a,u,d,x,c)
 
 
+class Reduce:
+    def __init__(self, io, r, s, land, pieces, stage, out):
+        self.io, self.r, self.s, self.land, self.pieces = io, r, s, land, pieces
+        self.stage, self.out = stage, out
+        self.slot = io.slots(6)
+        self.z_slot = io.slots(4)
+
+    def half(self, j, h):
+        return self.s(j).at[pl.ds(h * 2 * self.r, 2 * self.r)]
+
+    def send(self, i, j, h, bit):
+        io = self.io
+        io.start(self.slot[i], lambda: self.half(j, h), lambda: self.land.at[i], (io.dp ^ bit, io.z))
+
+    def start(self):
+        self.send(0, 3, 0, 2)
+        self.send(1, 3, 1, 4)
+        self.send(2, 1, 0, 2)
+        self.send(3, 2, 1, 4)
+
+    def load(self, i, at):
+        self.io.arrived(self.slot[i], lambda: self.land.at[i])
+        return self.io.load(self.land.at[i], self.stage.at[at])
+
+    def relay(self):
+        for i, j, h, bit in ((0, 2, 0, 4), (1, 1, 1, 2)):
+            self.load(i, i).wait()
+            ref = self.half(j, h)
+            ref[...] = (ref[...].astype(F32) + self.stage[i].astype(F32)).astype(ref.dtype)
+            self.send(5 - i, j, h, bit)
+
+    def fold(self):
+        io, r = self.io, self.r
+        for i in (0, 1):
+            io.sent_wait(self.slot[i])
+        for h, (a, b) in enumerate(((2, 5), (4, 3))):
+            one, two = self.load(a, 0), self.load(b, 1)
+            one.wait()
+            two.wait()
+            own = self.half(0, h)[...]
+            total = own.astype(F32) + self.stage[0].astype(F32) + self.stage[1].astype(F32)
+            self.half(3, h)[...] = total.astype(own.dtype)
+        for k in (1, 2, 3):
+            io.start(
+                self.z_slot[k],
+                lambda k=k: self.piece(io.z ^ k),
+                lambda k=k: self.pieces.at[k],
+                (io.dp, io.z ^ k),
+            )
+
+    def piece(self, z):
+        return self.s(3).at[pl.ds(pl.multiple_of(z * self.r, self.r), self.r)]
+
+    def finish(self):
+        io, r = self.io, self.r
+        spots = [self.stage.at[i, pl.ds(h * r, r)] for i, h in ((0, 0), (0, 1), (1, 0))]
+        loads = []
+        for k in (1, 2, 3):
+            io.arrived(self.z_slot[k], lambda k=k: self.pieces.at[k])
+            loads.append(io.load(self.pieces.at[k], spots[k - 1]))
+        total = self.piece(io.z)[...].astype(F32)
+        for copy, spot in zip(loads, spots):
+            copy.wait()
+            total = total + spot[...].astype(F32)
+        self.out[...] = total
+
+
+class HandBack:
+    def __init__(self, io, src, dst):
+        self.io, self.src, self.dst = io, src, dst
+        self.slots = io.slots(4)
+        self.rows = dst.shape[1]
+
+    def host(self, z):
+        clip = z - self.io.dp % 2
+        return (clip >= 0) & (clip < 3)
+
+    def part(self, s):
+        return self.src.at[pl.ds(s * self.rows, self.rows)]
+
+    def start(self):
+        io = self.io
+        for s in range(1, 4):
+            to = (io.z + 4 - s) % 4
+            io.start(
+                self.slots[s], lambda s=s: self.part(s), lambda s=s: self.dst.at[s], (io.dp, to), self.host(io.z)
+            )
+        copy = io.load(self.part(0), self.dst.at[0])
+        copy.wait()
+
+    def wait(self):
+        io = self.io
+        for s in range(1, 4):
+            io.arrived(self.slots[s], lambda s=s: self.dst.at[s], self.host((io.z + s) % 4))
+
+
+N_BACK = 120
+N_LOCAL = 112
+
+
+def norm_rows(v):
+    center = v - jnp.mean(v, axis=-1, keepdims=True)
+    r = lax.rsqrt(jnp.mean(center * center, axis=-1, keepdims=True) + EPSILON)
+    return center * r, r
+
+
+def backward_kernel(
+    wa, wu, wd, og, x, middle, normed1, normed2, qkv_in, attended, hidden, slope, gain1, gain2, d_bias,
+    a_out, u_out, d_out, s_out, ret_out, ret_in, a_land, u_land, d_land, s_land, a_pieces, u_pieces, d_pieces, s_pieces,
+    og2, ug2, bg2, hj2, np2, n1p2, atp2, flip, qkv, ag, xv, part, wdb, wb, tiles, acc, s_d, s_u, stage_d, stage_u,
+    table, table_sib, s_s, stage_s, vec, ub,
+    send, recv, local, ready,
+):
+    io = Copies(send, recv, local)
+    dp, z = io.dp, io.z
+    t = og.shape[0]
+    own, sib = pl.ds(0, t), pl.ds(t, t)
+    core = (dp ^ 1, z)
+
+    red_d = Reduce(io, d_out.shape[0], lambda j: s_d.at[j], d_land, d_pieces, stage_d, d_out)
+    red_u = Reduce(io, u_out.shape[0], lambda j: s_u.at[j], u_land, u_pieces, stage_u, u_out)
+    n_a = a_out.shape[0]
+    red_a = Reduce(io, n_a, lambda j: ug2.at[pl.ds(j * 4 * n_a, 4 * n_a)], a_land, a_pieces, stage_u, a_out)
+    red_s = Reduce(io, s_out.shape[0], lambda j: s_s.at[j], s_land, s_pieces, stage_s, s_out)
+    back_in = HandBack(io, qkv.at[:, pl.ds(D, D)], ret_in)
+    back_out = HandBack(io, qkv.at[:, pl.ds(0, D)], ret_out)
+
+    bar = pltpu.get_barrier_semaphore()
+    partners = [(dp, z ^ k) for k in (1, 2, 3)] + [(dp ^ b, z) for b in (1, 2, 4)]
+    for p in partners:
+        pl.semaphore_signal(bar, inc=1, device_id=p, device_id_type=MESH)
+
+    def planes(src, dst):
+        width = dst.shape[1] // 4
+        return [
+            io.load(
+                src.at[:, pl.ds(pl.multiple_of((dp ^ (2 * j)) * width, LANES), width)],
+                dst.at[own, pl.ds(j * width, width)],
+            )
+            for j in range(4)
+        ]
+
+    first = [io.load(og, og2.at[own])] + planes(hidden, hj2.at[:, pl.ds(0, FF // 2)])
+    pl.semaphore_wait(bar, len(partners))
+
+    def swap_planes(src, dst):
+        width = dst.shape[1] // 4
+        slots = io.slots(4)
+        for j in range(4):
+            io.start(
+                slots[j],
+                lambda j=j: src.at[:, pl.ds(pl.multiple_of((dp ^ (2 * j + 1)) * width, LANES), width)],
+                lambda j=j: dst.at[sib, pl.ds(j * width, width)],
+                core,
+            )
+        return [(slots[j], lambda j=j: dst.at[sib, pl.ds(j * width, width)]) for j in range(4)]
+
+    og_slot = io.slots(1)[0]
+    io.start(og_slot, lambda: og, lambda: og2.at[sib], core)
+    swapped_h = swap_planes(hidden, hj2.at[:, pl.ds(0, FF // 2)])
+    swapped_2 = swap_planes(normed2, np2)
+    swapped_1 = swap_planes(normed1, n1p2) + swap_planes(attended, atp2)
+    second = planes(normed2, np2)
+    second_half = t
+    d_rows = wdb.shape[1]
+    w_rows = wb.shape[1]
+
+    def stream(n, copies, body):
+        base = io.locals(2 * len(copies(0, 0)))
+
+        def make(i, slot):
+            pairs = copies(i, slot)
+            return [
+                pltpu.make_async_copy(a, b, io.local.at[base + 2 * c + slot]) for c, (a, b) in enumerate(pairs)
+            ]
+
+        for c in make(0, 0):
+            c.start()
+
+        def step(i, _):
+            slot = i % 2
+
+            @pl.when(i + 1 < n)
+            def _():
+                for c in make(i + 1, (i + 1) % 2):
+                    c.start()
+
+            for c in make(i, slot):
+                c.wait()
+            body(i, slot)
+            return 0
+
+        lax.fori_loop(0, n, step, 0)
+
+    def lanes(i, width):
+        return pl.ds(pl.multiple_of(i * width, LANES), width)
+
+    for c in first:
+        c.wait()
+    io.arrived(og_slot, lambda: og2.at[sib])
+    for slot, ref in swapped_h:
+        io.arrived(slot, ref)
+    third = planes(normed1, n1p2) + planes(attended, atp2)
+    third += [io.load(qkv_in, qkv), io.load(x, xv), io.load(middle, part)]
+    width = FF // 8
+    for j in (3, 1, 2, 0):
+        s_d[j] = dot_tn(hj2[:, j * width : (j + 1) * width], og2[...]).astype(BF)
+        if j == 3:
+            red_d.send(0, 3, 0, 2)
+            red_d.send(1, 3, 1, 4)
+        elif j == 1:
+            red_d.send(2, 1, 0, 2)
+        elif j == 2:
+            red_d.send(3, 2, 1, 4)
+    pl.semaphore_signal(ready, inc=1, device_id=core, device_id_type=MESH)
+    vec[7:8] = jnp.sum(og2[own].astype(F32), axis=0, keepdims=True)
+
+    ug_slots = io.slots(FF // d_rows)
+
+    def ug_copy(i):
+        return io.remote(ug_slots[0] + i, ug2.at[own, lanes(i, d_rows)], ug2.at[sib, lanes(i, d_rows)], core)
+
+    def hidden_step(i, slot):
+        grad = dot_nt(og2[own], wdb[slot]) * tiles[slot].astype(F32)
+        low = grad.astype(BF)
+        ug2[own, lanes(i, d_rows)] = low
+        ub[:, lanes(i, d_rows)] = jnp.sum(low.astype(F32), axis=0, keepdims=True)
+        ug_copy(i).start()
+
+    stream(
+        FF // d_rows,
+        lambda i, slot: [
+            (wd.at[pl.ds(pl.multiple_of(i * d_rows, d_rows), d_rows)], wdb.at[slot]),
+            (slope.at[:, lanes(i, d_rows)], tiles.at[slot]),
+        ],
+        hidden_step,
+    )
+
+    for c in second:
+        c.wait()
+    for slot, ref in swapped_2:
+        io.arrived(slot, ref)
+    flip[...] = np2[...].T
+    for i in range(FF // d_rows):
+        ug_copy(i).wait_recv()
+
+    def up_step(i, _):
+        block = dot(flip[...], ug2[:, lanes(i, 512)]).astype(BF)
+        for j in range(4):
+            s_u[j, :, lanes(i, 512)] = block[j * LANES : (j + 1) * LANES]
+        return 0
+
+    lax.fori_loop(0, FF // 512, up_step, 0)
+    red_u.start()
+    red_d.relay()
+
+    def up_back(i, slot):
+        acc[:, lanes(i, w_rows)] = dot_nt(ug2[own], wb[slot, :, 0:FF])
+
+    w_tile = lambda ref, lo, n: lambda i, slot: [
+        (ref.at[pl.ds(pl.multiple_of(i * w_rows, w_rows), w_rows), pl.ds(lo, n)], wb.at[slot, :, pl.ds(0, n)])
+    ]
+    stream(D // w_rows, w_tile(wu, 0, FF), up_back)
+    for c in third:
+        c.wait()
+    for i in (0, 1, 4, 5, 6):
+        vec[i : i + 1] = jnp.zeros((1, D), F32)
+    chunk = 128
+
+    def second_norm(i, _):
+        rows = pl.ds(pl.multiple_of(i * chunk, chunk), chunk)
+        e = acc[rows]
+        vhat, r = norm_rows(part[rows])
+        g = e * gain2[...]
+        grad = r * (
+            g - jnp.mean(g, axis=-1, keepdims=True) - vhat * jnp.mean(g * vhat, axis=-1, keepdims=True)
+        )
+        vec[5:6] += jnp.sum(e * vhat, axis=0, keepdims=True)
+        vec[6:7] += jnp.sum(e, axis=0, keepdims=True)
+        part[rows] = grad
+        low = (og2[rows].astype(F32) + grad).astype(BF)
+        bg2[rows] = low
+        vec[4:5] += jnp.sum(low.astype(F32), axis=0, keepdims=True)
+        return 0
+
+    lax.fori_loop(0, t // chunk, second_norm, 0)
+    bg_slot = io.slots(1)[0]
+    io.start(bg_slot, lambda: bg2.at[own], lambda: bg2.at[sib], core)
+
+    def proj_back(i, slot):
+        ag[:, lanes(i, w_rows)] = dot_nt(bg2[own], wb[slot, :, 0:D]).astype(BF)
+
+    stream(D // w_rows, w_tile(wa, 3 * D, D), proj_back)
+
+    def heads(i, _):
+        def at(k):
+            return lanes(k * (D // LANES) + i, LANES)
+
+        dq, dk, dv = attend_back_pair(qkv[:, at(0)], qkv[:, at(1)], qkv[:, at(2)], ag[:, at(0)])
+        for k, grad in enumerate((dq, dk, dv)):
+            hj2[own, at(k)] = grad
+        vec[2:3, at(0)] = jnp.sum(dq.astype(F32), axis=0, keepdims=True)
+        vec[3:4, at(0)] = jnp.sum(dv.astype(F32), axis=0, keepdims=True)
+        return 0
+
+    lax.fori_loop(0, D // LANES, heads, 0)
+    jn_slot = io.slots(1)[0]
+    pl.semaphore_wait(ready, 1)
+    io.start(jn_slot, lambda: hj2.at[own], lambda: hj2.at[sib], core)
+    red_u.relay()
+    red_d.fold()
+
+    def qkv_back(i, slot):
+        acc[:, lanes(i, w_rows)] = dot_nt(hj2[own], wb[slot, :, 0 : 3 * D])
+
+    stream(D // w_rows, w_tile(wa, 0, 3 * D), qkv_back)
+
+    def first_norm(i, _):
+        rows = pl.ds(pl.multiple_of(i * chunk, chunk), chunk)
+        e = acc[rows]
+        vhat, r = norm_rows(xv[rows].astype(F32))
+        g = e * gain1[...]
+        grad = r * (
+            g - jnp.mean(g, axis=-1, keepdims=True) - vhat * jnp.mean(g * vhat, axis=-1, keepdims=True)
+        )
+        vec[0:1] += jnp.sum(e * vhat, axis=0, keepdims=True)
+        vec[1:2] += jnp.sum(e, axis=0, keepdims=True)
+        qkv[rows, D : 2 * D] = (part[rows] + grad).astype(BF)
+        return 0
+
+    lax.fori_loop(0, t // chunk, first_norm, 0)
+    back_in.start()
+
+    spread_n = lax.broadcasted_iota(jnp.int32, (32, D), 0)
+    spread_c = lax.broadcasted_iota(jnp.int32, (32, D), 1)
+    mine = (spread_c // 32) == spread_n
+    pick_c = lax.broadcasted_iota(jnp.int32, (D, LANES), 0)
+    pick_l = lax.broadcasted_iota(jnp.int32, (D, LANES), 1)
+    table[...] = jnp.zeros_like(table)
+    for k in range(2):
+        rows = jnp.zeros((32, LANES), F32)
+        for q in range(4):
+            spread = jnp.where(mine, vec[4 * k + q : 4 * k + q + 1], 0.0)
+            pick = jnp.where(pick_l == 32 * q + pick_c % 32, 1.0, 0.0)
+            rows = rows + jnp.dot(spread, pick, preferred_element_type=F32, precision=lax.Precision.HIGHEST)
+        for n in range(32):
+            table[8 * n + k : 8 * n + k + 1] = rows[n : n + 1]
+    for n in range(32):
+        table[8 * n + 2 : 8 * n + 3] = ub[:, n * LANES : (n + 1) * LANES]
+    table_slot = io.slots(1)[0]
+    io.start(table_slot, lambda: table, lambda: table_sib, core)
+
+    for slot in range(FF // d_rows):
+        ug_copy(slot).wait_send()
+    for slot, ref in swapped_1:
+        io.arrived(slot, ref)
+    flip[...] = atp2[...].T
+    io.arrived(bg_slot, lambda: bg2.at[sib])
+
+    def proj_step(i, _):
+        block = dot(flip[...], bg2[:, lanes(i, 512)]).astype(BF)
+        ug2[own, lanes(6 + i, 512)] = block
+        return 0
+
+    lax.fori_loop(0, D // 512, proj_step, 0)
+    flip[...] = n1p2[...].T
+    io.arrived(jn_slot, lambda: hj2.at[sib])
+
+    def qkv_step(i, _):
+        block = dot(flip[...], hj2[:, lanes(i, 512)]).astype(BF)
+        ug2[own, lanes(i, 512)] = block
+        return 0
+
+    lax.fori_loop(0, 3 * D // 512, qkv_step, 0)
+    red_a.start()
+    io.arrived(table_slot, lambda: table_sib)
+    for j in range(4):
+        rows = pl.ds(pl.multiple_of((dp ^ (2 * j)) * 32, 32), 32)
+        s_s[j] = table[rows] + table_sib[rows]
+    red_s.start()
+    red_d.finish()
+
+    load_middle = io.load(middle, part)
+    acc[...] = jnp.zeros_like(acc)
+
+    def down_step(i, slot):
+        acc[...] += dot(tiles[slot], wdb[slot])
+
+    stream(
+        FF // d_rows,
+        lambda i, slot: [
+            (wd.at[pl.ds(pl.multiple_of(i * d_rows, d_rows), d_rows)], wdb.at[slot]),
+            (hidden.at[:, lanes(i, d_rows)], tiles.at[slot]),
+        ],
+        down_step,
+    )
+    load_middle.wait()
+    qkv[:, 0:D] = (acc[...] + (part[...] - xv[...].astype(F32)) + d_bias[...]).astype(BF)
+    back_out.start()
+
+    red_u.fold()
+    red_s.relay()
+    red_a.relay()
+    red_u.finish()
+    red_s.fold()
+    red_a.fold()
+    red_s.finish()
+    back_in.wait()
+    back_out.wait()
+    red_a.finish()
+    io.finish()
+
+
+def backward(wa, wu, wd, og, x, middle, normed1, normed2, qkv, attended, hidden, slope, gain1, gain2, d_bias):
+    t = og.shape[0]
+    any_ = pl.BlockSpec(memory_space=pl.ANY)
+    vmem = pl.BlockSpec(memory_space=pltpu.VMEM)
+    sh = jax.ShapeDtypeStruct
+    ra, rd, rs = D // 32, FF // 32, 8
+    outs = [
+        (sh((ra, FF), F32), vmem),
+        (sh((ra, FF), F32), vmem),
+        (sh((rd, D), F32), vmem),
+        (sh((rs, LANES), F32), vmem),
+        (sh((4, t // 4, D), BF), any_),
+        (sh((4, t // 4, D), BF), any_),
+    ]
+    for count, k in ((6, 2), (4, 1)):
+        outs += [
+            (sh((count, k * ra, FF), BF), any_),
+            (sh((count, k * ra, FF), BF), any_),
+            (sh((count, k * rd, D), BF), any_),
+            (sh((count, k * rs, LANES), F32), any_),
+        ]
+    v = pltpu.VMEM
+    results = pl.pallas_call(
+        backward_kernel,
+        out_shape=[o for o, _ in outs],
+        in_specs=[any_] * 12 + [vmem] * 3,
+        out_specs=[o for _, o in outs],
+        scratch_shapes=[
+            v((2 * t, D), BF),
+            v((2 * t, FF), BF),
+            v((2 * t, D), BF),
+            v((2 * t, 3 * D), BF),
+            v((2 * t, D // 2), BF),
+            v((2 * t, D // 2), BF),
+            v((2 * t, D // 2), BF),
+            v((D // 2, 2 * t), BF),
+            v((t, 3 * D), BF),
+            v((t, D), BF),
+            v((t, D), BF),
+            v((t, D), F32),
+            v((2, 512, D), BF),
+            v((2, 256, FF), BF),
+            v((2, t, 512), BF),
+            v((t, D), F32),
+            v((4, 4 * rd, D), BF),
+            v((4, 4 * ra, FF), BF),
+            v((2, 2 * rd, D), BF),
+            v((2, 2 * ra, FF), BF),
+            v((32 * rs, LANES), F32),
+            v((32 * rs, LANES), F32),
+            v((4, 4 * rs, LANES), F32),
+            v((2, 2 * rs, LANES), F32),
+            v((8, D), F32),
+            v((1, FF), F32),
+            pltpu.SemaphoreType.DMA((N_BACK,)),
+            pltpu.SemaphoreType.DMA((N_BACK,)),
+            pltpu.SemaphoreType.DMA((N_LOCAL,)),
+            pltpu.SemaphoreType.REGULAR,
+        ],
+        compiler_params=pltpu.CompilerParams(
+            collective_id=1, has_side_effects=True, vmem_limit_bytes=60 * 2**20
+        ),
+    )(wa, wu, wd, og, x, middle, normed1, normed2, qkv, attended, hidden, slope, gain1, gain2, d_bias)
+    return results[:6]
+
+
 def norm_parts(v):
     center = v - jnp.mean(v, axis=-1, keepdims=True)
     r = lax.rsqrt(jnp.mean(center * center, axis=-1, keepdims=True) + EPSILON)
@@ -406,7 +860,7 @@
     return u * cdf, cdf + u * pdf
 
 
-SMALL = (D, D, D, D, D, D, D, FF, D)
+SMALL = (D, D, D, D, D, D, D, D, FF)
 
 
 def per_device(
@@ -441,8 +895,8 @@
         proj_bias,
         norm2_gain,
         norm2_shift,
+        down_bias,
         up_bias,
-        down_bias,
     )
     packed = jnp.concatenate(small)
     packed = jnp.pad(packed, (0, rows * LANES - packed.shape[0])).reshape(rows, LANES)
@@ -468,7 +922,7 @@
     for size in SMALL:
         vectors.append(table[:, at : at + size // n].reshape(size))
         at += size // n
-    gain1, shift1, q_bias, v_bias, p_bias, gain2, shift2, u_bias, d_bias = vectors
+    gain1, shift1, q_bias, v_bias, p_bias, gain2, shift2, d_bias, u_bias = vectors
 
     vhat1, r1 = norm_parts(x)
     normed1 = (vhat1 * gain1 + shift1).astype(BF)
@@ -483,65 +937,73 @@
     hidden, slope = gelu_both(dot(normed2, u_mat) + u_bias)
     hidden = hidden.astype(BF)
     slope = slope.astype(BF)
-    out_part = branch + dot(hidden, d_mat) + d_bias
-    block_out = living * (clips + links.hand_back(out_part.astype(BF), slots).astype(F32))
-
-    d_down = dot_tn(hidden, out_grad).astype(BF)
-    down_grad = links.reduce(links.blocks_of(d_down, 0))
-    hidden_grad = dot_nt(out_grad, d_mat)
-    upper_grad = (hidden_grad * slope).astype(BF)
-    d_up = dot_tn(normed2, upper_grad).astype(BF)
-    up_grad = links.reduce(links.blocks_of(d_up, 0))
-    normed_grad = dot_nt(upper_grad, u_mat)
-    part, gain2_grad, shift2_grad = norm_back(vhat2, r2, gain2, normed_grad)
-    middle_part = out_grad.astype(F32) + part
-    branch_grad = middle_part.astype(BF)
-    attended_grad = dot_nt(branch_grad, proj_mat).astype(BF)
-    dq, dk, dv = attend_back(qkv, attended_grad)
-    joined = jnp.concatenate([dq, dk, dv], axis=1)
-    first_grad = dot_nt(joined, qkv_mat)
-    first_part, gain1_grad, shift1_grad = norm_back(vhat1, r1, gain1, first_grad)
-    input_grad = living_cot + links.hand_back((part + first_part).astype(BF), slots).astype(F32)
-
-    total = lambda g: jnp.sum(g.astype(F32), axis=0)
-    small_grads = (
-        gain1_grad,
-        shift1_grad,
-        total(dq),
-        total(dv),
-        total(branch_grad),
-        gain2_grad,
-        shift2_grad,
-        total(upper_grad),
-        total(out_grad),
-    )
-    grad_table = jnp.concatenate([g.reshape(n, -1) for g in small_grads], axis=1)
-    width = grad_table.shape[1]
-    grad_table = jnp.pad(grad_table, ((0, 0), (0, rows * LANES - width)))
-    d_a = jnp.concatenate(
-        [
-            dot_tn(normed1, joined).astype(BF),
-            dot_tn(attended, branch_grad).astype(BF),
-            grad_table.reshape(n * rows, LANES).astype(BF),
-        ],
-        axis=1,
-    )
-    a_grad = links.reduce(links.blocks_of(d_a, 0))
-    small_out = a_grad[:, 4 * D :].reshape(-1)
+    if links.short:
+        row = lambda v: v.reshape(1, -1)
+        qkv_proj_grad, up_grad, down_grad, small_grad, out_back, in_back = backward(
+            a_mat,
+            u_mat,
+            d_mat,
+            out_grad,
+            x.astype(BF),
+            middle,
+            normed1,
+            normed2,
+            qkv,
+            attended,
+            hidden,
+            slope,
+            row(gain1),
+            row(gain2),
+            row(d_bias),
+        )
+        out_home, in_home = links.by_clip(out_back, slots), links.by_clip(in_back, slots)
+        small_out = small_grad[:3].reshape(-1)
+    else:
+        out_part = branch + dot(hidden, d_mat) + d_bias
+        out_home = links.hand_back(out_part.astype(BF), slots)
+        down_grad = links.reduce(dot_tn(hidden, out_grad))
+        upper_grad = (dot_nt(out_grad, d_mat) * slope).astype(BF)
+        up_grad = links.reduce(dot_tn(normed2, upper_grad))
+        part, gain2_grad, shift2_grad = norm_back(vhat2, r2, gain2, dot_nt(upper_grad, u_mat))
+        branch_grad = (out_grad.astype(F32) + part).astype(BF)
+        dq, dk, dv = attend_back(qkv, dot_nt(branch_grad, proj_mat).astype(BF))
+        joined = jnp.concatenate([dq, dk, dv], axis=1)
+        first_part, gain1_grad, shift1_grad = norm_back(vhat1, r1, gain1, dot_nt(joined, qkv_mat))
+        in_home = links.hand_back((part + first_part).astype(BF), slots)
+        total = lambda g: jnp.sum(g.astype(F32), axis=0)
+        small_grads = (
+            gain1_grad,
+            shift1_grad,
+            total(dq),
+            total(dv),
+            total(branch_grad),
+            gain2_grad,
+            shift2_grad,
+            total(out_grad),
+            total(upper_grad),
+        )
+        grad_table = jnp.concatenate([g.reshape(n, -1) for g in small_grads], axis=1)
+        width = grad_table.shape[1]
+        grad_table = jnp.pad(grad_table, ((0, 0), (0, rows * LANES - width)))
+        d_a = [dot_tn(normed1, joined), dot_tn(attended, branch_grad), grad_table.reshape(n * rows, LANES)]
+        a_grad = links.reduce(jnp.concatenate(d_a, axis=1))
+        qkv_proj_grad, small_out = a_grad[:, : 4 * D], a_grad[:, 4 * D :].reshape(-1)
+    block_out = living * (clips + out_home.astype(F32))
+    input_grad = living_cot + in_home.astype(F32)
     pieces, at = [], 0
     for size in SMALL:
         pieces.append(small_out[at : at + size // n])
         at += size // n
-    g1, s1, qb, vb, pb, g2, s2, ub, db = pieces
+    g1, s1, qb, vb, pb, g2, s2, db, ub = pieces
     return (
         block_out,
         input_grad,
         g1,
         s1,
-        a_grad[:, : 3 * D].reshape(-1),
+        qkv_proj_grad[:, : 3 * D].reshape(-1),
         qb,
         vb,
-        a_grad[:, 3 * D : 4 * D].reshape(-1),
+        qkv_proj_grad[:, 3 * D :].reshape(-1),
         pb,
         g2,
         s2,

time: 507 us -> 386 us (0.76)
  Pallas kernels: 171 us -> 332 us
  waiting for transfers between devices: 108 us -> 0 us
  matrix products: 82.2 us -> 21.8 us
  starting transfers between devices: 50 us -> 0 us
  other arithmetic: 46.8 us -> 12.1 us
  local copies, waits for them, and re-layouts: 33.9 us -> 13.1 us
  between operations: 10.5 us -> 1.92 us
    pallas_call x1, Pallas kernels: 20.7 us -> 181 us  [backward(): pl.pallas_call(backward_kernel, out_shape=[o for o, _ in outs], in_specs=...]
    ppermute x39 -> x0, waiting for transfers between devices: 108 us -> none  [the longest x24 77.2 us: cross(): return lax.ppermute(x, AXES, pairs)]
    dot_general x8 -> x0, matrix products: 56.5 us -> none  [the longest x4 29.3 us: dot_nt(): lax.dot_general(a, b, (((1,), (1,)), ((), ())), preferred_element_type=F32)]
    ppermute x39 -> x0, starting transfers between devices: 50 us -> none  [the longest x6 19.2 us: hand_back(): back.append(part if s == 0 else lax.ppermute(part, AXES, pairs))]
    add x8 -> x1, other arithmetic: 17.7 us -> 2.26 us  [per_device(): input_grad = living_cot + in_home.astype(F32)]
    another operation x19 -> x11, other arithmetic: 14.5 us -> 0.06 us
    dynamic_slice x7 -> x1, local copies, waits for them, and re-layouts: 12.1 us -> 1.67 us  [by_clip(): lax.dynamic_index_in_dim(back, (c + lead - self.z) % n, 0, False)]
    dot_general x4 -> x3, matrix products: 25.7 us -> 21.8 us  [dot(): return jnp.dot(a, b, preferred_element_type=F32)]
  transfers between devices with their start and end apart: 39 -> 0, of which waited for: 17 -> 0; matrix products, arithmetic and copies ran while one was open for 22% -> 0% of each run, Pallas kernels for 4% -> 0%
where the time goes in v3:
time: 386 us; the launch traced here: 381 us
  Pallas kernels  332 us (86%)
  matrix products  21.8 us (6%)
  local copies, waits for them, and re-layouts  13.1 us (3%)
  other arithmetic  12.1 us (3%)
    pallas_call x1, Pallas kernels, backward(): pl.pallas_call(backward_kernel, out_shape=[o for o, _ in outs], in_specs=...  181 us
    pallas_call x1, Pallas kernels, gather_all(): pl.pallas_call(gather_kernel, out_shape=[sh(32 * a.shape[0], a.shape[1]),...  138 us
    dot_general x3, matrix products, dot(): return jnp.dot(a, b, preferred_element_type=F32)  21.8 us
    pallas_call x1, Pallas kernels, attend(): pl.pallas_call(attend_kernel, grid=(n,), out_shape=jax.ShapeDtypeStruct((...  12.3 us

profile of v3, /device:TPU:0, one launch (start us, length us, event | category | flops | bytes accessed | tf_op | source)
XLA Modules:
  0.0 380.9 jit_solution(2392786505527689315)
XLA Ops:
  1.5 2.6 multiply_convert_fusion.1.c
  4.6 0.7 pad_maximum_fusion.a
  5.3 1.0 convert_element_type.62.x
  6.4 0.8 convert_element_type.59.u
  7.2 0.8 convert_element_type.61.d
  8.0 138.4 %shard_map.271 = (bf16[1024,4224]{1,0:T(8,128)(2,1)}, bf16[1024,4096]{1,0:T(8,128)(2,1)}, bf16[4096,1024]{1,0:T(8,128)(2,1)}, bf16[512,1024]{1,0:T(8,128)(2,1)}, bf16[512,1024]{1,0:T(8,128)(2,1)}) custom-call(bf16[32,4224]{1,0:T(8,128)(2,1)} %pad_maximum_fusion.a, bf16[32,4096]{1,0:T(8,128)(2,1)} %convert_element_type.59.u, ...), custom_call_target="tpu_custom_call" | custom-call | tf_op jit(solution)/shard_map/pallas_call | solution.py:357
  146.4 1.5 convert_reduce_fusion
  148.0 1.6 fusion.11
  149.6 1.0 slice_convert_fusion
  150.9 0.6 copy-done.9
  151.6 0.4 fusion.14.normed1
  152.2 6.6 %add_convert_fusion.q_ref.k_ref.v_ref.qkv_in = bf16[512,3072]{1,0:T(8,128)(2,1)S(1)} fusion(bf16[512,1024]{1,0:T(8,128)(2,1)S(1)} %fusion.14.normed1, bf16[1024,4224]{1,0:T(8,128)(2,1)} %get-tuple-element.26.wa, f32[3072]{0:T(1024)S(1)} %pad_maximum_fusion.1), kind=kOutput, calls=%fused_computation.8 | convolution fusion | flops 3224371200 | bytes 10498048 | tf_op jit(solution)/shard_map/dot_general | solution.py:23
  158.9 12.3 %shard_map.272.attended = bf16[512,1024]{1,0:T(8,128)(2,1)S(1)} custom-call(bf16[512,3072]{1,0:T(8,128)(2,1)S(1)} %add_convert_fusion.q_ref.k_ref.v_ref.qkv_in, bf16[512,3072]{1,0:T(8,128)(2,1)S(1)} %add_convert_fusion.q_ref.k_ref.v_ref.qkv_in, bf16[512,3072]{1,0:T(8,128)(2,1)S(1)} %add_convert_fusion.q_ref.k_ref.v_ref.qkv_in), custom_call_target="tpu_custom_call" | custom-call | flops 1073741824 | bytes 4194304 | tf_op jit(solution)/shard_map/pallas_call | solution.py:58
  171.3 3.5 fusion.21
  174.8 0.3 multiply_reduce_fusion
  175.3 0.4 add_convert_fusion.1.normed2
  175.7 0.4 copy-done.2
  176.2 0.7 slice_bitcast_fusion.2
  176.9 11.7 %fusion.4 = (bf16[512,4096]{1,0:T(8,128)(2,1)}, bf16[512,4096]{1,0:T(8,128)(2,1)}) fusion(f32[4096]{0:T(1024)S(1)} %slice_bitcast_fusion.2, bf16[512,1024]{1,0:T(8,128)(2,1)S(1)} %add_convert_fusion.1.normed2, bf16[1024,4096]{1,0:T(8,128)(2,1)} %get-tuple-element.27.wu), kind=kOutput, calls=%fused_computation.5 | convolution fusion | flops 4320133120 | bytes 17842176 | tf_op jit(solution)/shard_map/dot_general | solution.py:23
  188.5 0.7 broadcast_in_dim_reshape.4.gain1
  189.2 0.7 broadcast_in_dim_reshape.5.gain2
  189.9 0.7 reshape_reshape.2.d_bias
  190.6 181.3 %shard_map.273 = (f32[32,4096]{1,0:T(8,128)}, f32[32,4096]{1,0:T(8,128)}, f32[128,1024]{1,0:T(8,128)}, f32[8,128]{1,0:T(8,128)}, bf16[4,128,1024]{2,1,0:T(8,128)...) custom-call(bf16[1024,4224]{1,0:T(8,128)(2,1)} %get-tuple-element.26, ...), custom_call_target="tpu_custom_call" | custom-call | tf_op jit(solution)/shard_map/pallas_call | solution.py:799
  372.0 1.7 constant_dynamic-slice_fusion.2
  373.7 0.5 copy-done.6
  374.2 2.3 convert_add_fusion.1
  376.5 0.8 copy.31
  377.3 0.9 copy.33
  378.2 0.9 copy.34
  379.1 0.7 copy.32
  379.8 0.6 fusion.20
  380.4 0.5 slice_bitcast_fusion.4
  (87 shorter events, 1.3 us)
Async XLA Ops:
  0.7 3.5 copy-start.15
  0.7 3.6 copy-start.16
  0.7 3.6 copy-start.18
  0.7 3.7 copy-start.19
  0.7 3.7 copy-start.20
  0.7 3.7 copy-start.21
  0.7 3.7 copy-start.22
  0.7 3.7 copy-start.23
  0.7 3.7 copy-start.24
  0.7 3.7 copy-start.25
  0.8 3.7 copy-start.26
  1.5 3.9 %copy-start.5 = (f32[3,128,1024]{2,1,0:T(8,128)S(1)}, f32[3,128,1024]{2,1,0:T(8,128)}, u32[]{:S(2)}) copy-start(f32[3,128,1024]{2,1,0:T(8,128)} %param.16) | copy-start | bytes 4718596
  4.1 2.2 copy-start.10
  4.6 2.6 copy-start.11
  146.4 5.2 %copy-start.3 = (bf16[512,1024]{1,0:T(8,128)(2,1)S(1)}, bf16[512,1024]{1,0:T(8,128)(2,1)}, u32[]{:S(2)}) copy-start(bf16[512,1024]{1,0:T(8,128)(2,1)} %get-tuple-element.30.x) | copy-start | bytes 3145732
  150.7 0.8 copy-start.9
  152.1 6.8 %copy-start.7 = (bf16[512,1024]{1,0:T(8,128)(2,1)}, bf16[512,1024]{1,0:T(8,128)(2,1)S(1)}, u32[]{:S(2)}) copy-start(bf16[512,1024]{1,0:T(8,128)(2,1)S(1)} %fusion.14.normed1) | copy-start | bytes 3145732
  158.8 12.3 %copy-start = (bf16[512,3072]{1,0:T(8,128)(2,1)}, bf16[512,3072]{1,0:T(8,128)(2,1)S(1)}, u32[]{:S(2)}) copy-start(bf16[512,3072]{1,0:T(8,128)(2,1)S(1)} %add_convert_fusion.q_ref.k_ref.v_ref.qkv_in) | copy-start | bytes 9437188
  171.2 3.6 copy-start.1
  174.8 1.4 copy-start.2
  176.2 12.4 %copy-start.8 = (bf16[512,1024]{1,0:T(8,128)(2,1)}, bf16[512,1024]{1,0:T(8,128)(2,1)S(1)}, u32[]{:S(2)}) copy-start(bf16[512,1024]{1,0:T(8,128)(2,1)S(1)} %add_convert_fusion.1.normed2) | copy-start | bytes 3145732
  371.9 1.9 copy-start.4
  371.9 2.3 copy-start.6
  374.2 2.3 copy-start.12
  374.2 3.1 copy-start.14
  376.5 1.7 copy-start.13
  376.5 3.3 copy-start.17

commit v4 on v3

--- a/solution.py
+++ b/solution.py
@@ -38,8 +38,7 @@
     return e * (1.0 / jnp.sum(e, axis=0, keepdims=True))
 
 
-def attend_kernel(q_ref, k_ref, v_ref, o_ref):
-    q2, k2, v2 = q_ref[...], k_ref[...], v_ref[...]
+def attend_pair(q2, k2, v2):
     low = lax.broadcasted_iota(jnp.int32, k2.shape, 1) < HEAD_DIM
     v_t = v2.T
     zero = jnp.zeros_like(k2)
@@ -48,7 +47,11 @@
         k_half = jnp.where(low == (h == 0), k2, zero)
         p_t = soft_t(q2, k_half).astype(BF)
         parts.append(dot(v_t[h * HEAD_DIM : (h + 1) * HEAD_DIM], p_t))
-    o_ref[...] = jnp.concatenate(parts, axis=0).T.astype(BF)
+    return jnp.concatenate(parts, axis=0).T.astype(BF)
+
+
+def attend_kernel(q_ref, k_ref, v_ref, o_ref):
+    o_ref[...] = attend_pair(q_ref[...], k_ref[...], v_ref[...])
 
 
 def attend(qkv):
@@ -171,6 +174,18 @@
         return jnp.stack(
             [lax.dynamic_index_in_dim(back, (c + lead - self.z) % n, 0, False) for c in range(slots)]
         )
+
+
+def norm_rows(v):
+    center = v - jnp.mean(v, axis=-1, keepdims=True)
+    r = lax.rsqrt(jnp.mean(center * center, axis=-1, keepdims=True) + EPSILON)
+    return center * r, r
+
+
+def gelu_both(u):
+    cdf = 0.5 * (1.0 + lax.erf(u * 0.7071067811865476))
+    pdf = 0.3989422804014327 * jnp.exp(-0.5 * u * u)
+    return u * cdf, cdf + u * pdf
 
 
 def guarded(cond, f):
@@ -210,50 +225,50 @@
         copy.start()
         return copy
 
+
 class Gather:
-    def __init__(self, io, shard, out, fine, local):
-        self.io, self.shard, self.out, self.fine = io, shard, out, fine
+    def __init__(self, io, shard, out):
+        self.io, self.shard, self.out = io, shard, out
         self.r = shard.shape[0]
-        self.local = pltpu.make_async_copy(shard, self.at(0, 0), local)
-        self.keys = (0, -1, 1, -2, 2, -3, 3) if fine else (None,)
-        self.z_slot = {(e * s): io.slots(1)[0] for e in (1, 2, 3) for s in (-1, 1)}
-        self.slot = {k: dict(x=io.slots(1), y=io.slots(1), d=io.slots(2), own=io.slots(1), cx=io.slots(1), cy=io.slots(1), cd=io.slots(2)) for k in self.keys}
+        self.local = io.load(shard, self.at(0, 0))
+        self.keys = (0, 1, 2, 3)
+        self.z_slot = io.slots(4)
+        self.slot = {k: {name: io.slots(2) for name in ("x", "y", "d", "own", "cx", "cy", "cd")} for k in self.keys}
+
     def at(self, m, k, part=None):
         io, r = self.io, self.r
-        if k is None: base, n = (io.dp ^ m) * 4 * r, 4 * r
-        else: base, n = ((io.dp ^ m) * 4 + io.z + k) * r, r
-        if part is not None: n = n // 2; base = base + part * n
+        base, n = ((io.dp ^ m) * 4 + (io.z ^ k)) * r, r
+        if part is not None:
+            n = n // 2
+            base = base + part * n
         return self.out.at[pl.ds(pl.multiple_of(base, 16), n)]
-    def ok(self, k):
-        if not k: return None
-        return (self.io.z + k >= 0) & (self.io.z + k <= 3)
+
     def move(self, name, i, m, k, bit, part=None, src=None):
+        io = self.io
         ref = lambda: self.at(m, k, part)
-        io = self.io
-        io.start(self.slot[k][name][i], src or ref, ref, (io.dp ^ bit, io.z), self.ok(k))
+        io.start(self.slot[k][name][i], src or ref, ref, (io.dp ^ bit, io.z))
+
     def got(self, name, i, m, k, part=None):
-        self.io.arrived(self.slot[k][name][i], lambda: self.at(m, k, part), self.ok(k))
+        self.io.arrived(self.slot[k][name][i], lambda: self.at(m, k, part))
+
     def start_z(self):
         io = self.io
-        self.local.start()
-        mine = lambda: self.shard
-        to = lambda: self.at(0, 0)
-        io.start(self.z_slot[-1], mine, to, (io.dp, io.z + 1), io.z < 3)
-        io.start(self.z_slot[1], mine, to, (io.dp, io.z - 1), io.z > 0)
-    def pass_z(self, e):
+        for k in (1, 2):
+            io.start(self.z_slot[k], lambda: self.shard, lambda: self.at(0, 0), (io.dp, io.z ^ k))
+
+    def arrive_z(self, k):
         io = self.io
-        for s in (-1, 1):
-            k = s * e
-            ref = lambda k=k: self.at(0, k)
-            io.arrived(self.z_slot[k], ref, self.ok(k))
-            if e < 3:
-                to = io.z - s
-                io.start(self.z_slot[s * (e + 1)], ref, ref, (io.dp, to), self.ok(k) & (to >= 0) & (to <= 3))
+        ref = lambda: self.at(0, k)
+        io.arrived(self.z_slot[k], ref)
+        if k == 2:
+            io.start(self.z_slot[3], ref, ref, (io.dp, io.z ^ 1))
+
     def spread(self, k):
         src = (lambda: self.shard) if k == 0 else None
         self.move("x", 0, 0, k, 2, src=src)
         self.move("y", 0, 0, k, 4, src=src)
         self.move("own", 0, 0, k, 1, src=src)
+
     def pass_on(self, k):
         self.got("x", 0, 2, k)
         self.move("d", 0, 2, k, 4, 0)
@@ -261,104 +276,314 @@
         self.move("d", 1, 4, k, 2, 1)
         self.move("cx", 0, 2, k, 1)
         self.move("cy", 0, 4, k, 1)
+
     def far(self, k):
         for h in range(2):
             self.got("d", h, 6, k, h)
             self.move("cd", h, 6, k, 1, h)
-    def done(self, k):
-        self.got("own", 0, 1, k)
-        self.got("cx", 0, 3, k)
-        self.got("cy", 0, 5, k)
-        for h in range(2): self.got("cd", h, 7, k, h)
+
+    def done(self):
+        for k in self.keys:
+            self.got("own", 0, 1, k)
+            self.got("cx", 0, 3, k)
+            self.got("cy", 0, 5, k)
+            for h in range(2):
+                self.got("cd", h, 7, k, h)
+
 
 class Collect:
-    def __init__(self, io, src, dst, local):
+    def __init__(self, io, src, dst):
         self.io, self.src, self.dst = io, src, dst
         self.slots = io.slots(4)
-        self.local = local
+        self.local = io.locals(1)
         self.rows = src.shape[1]
         self.host = self.valid(io.z)
-    def part(self, s): return self.dst.at[pl.ds(s * self.rows, self.rows)]
+
+    def part(self, s):
+        return self.dst.at[pl.ds(s * self.rows, self.rows)]
+
     def valid(self, z):
         clip = z - self.io.dp % 2
         return (clip >= 0) & (clip < 3)
+
     def start(self):
         io = self.io
         for s in range(4):
             to = (io.z + s) % 4
             src = lambda to=to: self.src.at[jnp.clip(to - io.dp % 2, 0, 2)]
             if s == 0:
-                guarded(self.host, lambda: pltpu.make_async_copy(src(), self.part(0), self.local).start())
+                copy = lambda: pltpu.make_async_copy(src(), self.part(0), io.local.at[self.local]).start()
+                guarded(self.host, copy)
             else:
                 io.start(self.slots[s], src, lambda s=s: self.part(s), (io.dp, to), self.valid(to))
+
     def wait(self):
-        guarded(self.host, lambda: pltpu.make_async_copy(self.part(0), self.part(0), self.local).wait())
+        io = self.io
+        copy = lambda: pltpu.make_async_copy(self.part(0), self.part(0), io.local.at[self.local]).wait()
+        guarded(self.host, copy)
         for s in range(1, 4):
-            self.io.arrived(self.slots[s], lambda s=s: self.part(s), self.host)
-
-N_SLOTS = 140
-def gather_kernel(a, u, d, x, c, wa, wu, wd, xb, cb, zero, send, recv, local):
-    io = Copies(send, recv)
-    ga, gu, gd = Gather(io, a, wa, True, local.at[0]), Gather(io, u, wu, False, local.at[1]), Gather(io, d, wd, False, local.at[2])
-    cx, cc = Collect(io, x, xb, local.at[3]), Collect(io, c, cb, local.at[4])
-    assert io.n <= N_SLOTS, io.n
+            io.arrived(self.slots[s], lambda s=s: self.part(s), self.host)
+
+        def clear():
+            self.dst[...] = jnp.zeros_like(self.dst)
+
+        guarded(jnp.logical_not(self.host), clear)
+
+
+N_FORE = 200
+CHUNK = 128
+COLS = 512
+
+
+def stream(io, n, copies, body):
+    base = io.locals(2 * len(copies(0, 0)))
+
+    def make(i, slot):
+        return [
+            pltpu.make_async_copy(a, b, io.local.at[base + 2 * c + slot])
+            for c, (a, b) in enumerate(copies(i, slot))
+        ]
+
+    for c in make(0, 0):
+        c.start()
+
+    def step(i, _):
+        slot = i % 2
+
+        @pl.when(i + 1 < n)
+        def _():
+            for c in make(i + 1, (i + 1) % 2):
+                c.start()
+
+        for c in make(i, slot):
+            c.wait()
+        body(i, slot)
+        return 0
+
+    lax.fori_loop(0, n, step, 0)
+
+
+def lanes(i, width):
+    return pl.ds(pl.multiple_of(i * width, LANES), width)
+
+
+def meet(io):
     bar = pltpu.get_barrier_semaphore()
     partners = [(io.dp, io.z ^ k) for k in (1, 2, 3)] + [(io.dp ^ b, io.z) for b in (1, 2, 4)]
-    for p in partners: pl.semaphore_signal(bar, inc=1, device_id=p, device_id_type=MESH)
-    zero[...] = jnp.zeros_like(zero)
+    for p in partners:
+        pl.semaphore_signal(bar, inc=1, device_id=p, device_id_type=MESH)
     pl.semaphore_wait(bar, len(partners))
-    ga.start_z(); ga.spread(0)
-    ga.local.wait()
-    ga.pass_z(1); ga.spread(-1); ga.spread(1)
-    ga.pass_on(0)
-    ga.pass_z(2); ga.spread(-2); ga.spread(2)
-    gu.start_z()
-    ga.far(0)
-    ga.pass_on(-1); ga.pass_on(1)
-    ga.pass_z(3); ga.spread(-3); ga.spread(3)
-    gu.pass_z(1)
-    ga.far(-1); ga.far(1)
-    gu.pass_z(2)
-    cx.start()
-    ga.pass_on(-2); ga.pass_on(2)
-    gu.pass_z(3)
-    gu.local.wait()
-    gu.spread(None)
-    ga.far(-2); ga.far(2)
-    gd.start_z()
-    ga.pass_on(-3); ga.pass_on(3)
-    ga.far(-3); ga.far(3)
-    for i in ga.keys: ga.done(i)
-    gd.pass_z(1)
+
+
+def spread_vectors(table, wide, vec, ub):
+    wide[...] = table[...].astype(F32)
+    spread_n = lax.broadcasted_iota(jnp.int32, (32, D), 0)
+    spread_c = lax.broadcasted_iota(jnp.int32, (32, D), 1)
+    mine = (spread_c // 32) == spread_n
+    pick_l = lax.broadcasted_iota(jnp.int32, (LANES, D), 0)
+    pick_c = lax.broadcasted_iota(jnp.int32, (LANES, D), 1)
+    for k in range(2):
+        rows = jnp.concatenate([wide[32 * n + k : 32 * n + k + 1] for n in range(32)], axis=0).astype(BF)
+        for q in range(4):
+            pick = jnp.where(pick_l == 32 * q + pick_c % 32, 1.0, 0.0).astype(BF)
+            spread = jnp.where(mine, dot(rows, pick), 0.0)
+            vec[4 * k + q : 4 * k + q + 1] = jnp.sum(spread, axis=0, keepdims=True)
+    for n in range(32):
+        ub[:, n * LANES : (n + 1) * LANES] = wide[32 * n + 2 : 32 * n + 3]
+
+
+def forward_kernel(
+    a, u, d, clips, cot,
+    wa, wu, wd, og, x_out, middle_out, n1_out, n2_out, qkv_out, att_out, hidden, slope, vec,
+    xv, ogv, n1, n2, qkv, att, middle, wb, hid, slo, table, wide, ub, bias,
+    send, recv, local,
+):
+    io = Copies(send, recv, local)
+    ga, gu, gd = Gather(io, a, wa), Gather(io, u, wu), Gather(io, d, wd)
+    cx, cc = Collect(io, clips, xv), Collect(io, cot, ogv)
+    t = xv.shape[0]
+    meet(io)
+
+    line = [(g, k) for g in (ga, gu, gd) for k in range(4)]
+    place = [0]
+
+    def advance(n=1):
+        for _ in range(n):
+            i = place[0]
+            place[0] += 1
+            if i < len(line):
+                g, k = line[i]
+                if k == 2 and g is not gd:
+                    g.arrive_z(2)
+                    (gu if g is ga else gd).start_z()
+                    if g is ga:
+                        cx.start()
+                    else:
+                        cc.start()
+                elif k:
+                    g.arrive_z(k)
+                g.spread(k)
+            if 1 <= i <= len(line):
+                g, k = line[i - 1]
+                g.pass_on(k)
+            if 3 <= i <= len(line) + 2:
+                g, k = line[i - 3]
+                g.far(k)
+
+    ga.start_z()
+    advance(3)
+    for g in (ga, gu, gd):
+        g.local.wait()
+    advance(4)
+    outs = []
+
+    ga.done()
+    io.load(wa.at[:, pl.ds(4 * D, LANES)], table).wait()
+    spread_vectors(table, wide, vec, ub)
+    bias[:, 0:D] = vec[2:3]
+    bias[:, D : 2 * D] = jnp.zeros((1, D), F32)
+    bias[:, 2 * D : 3 * D] = vec[3:4]
     cx.wait()
-    gd.pass_z(2)
-    gd.pass_z(3)
-    gd.local.wait()
-    gd.spread(None)
-    cc.start()
-    gu.pass_on(None)
-    gu.far(None)
-    gu.done(None)
+    outs.append(io.load(xv, x_out))
+
+    def first_norm(i, _):
+        rows = pl.ds(pl.multiple_of(i * CHUNK, CHUNK), CHUNK)
+        vhat, _r = norm_rows(xv[rows].astype(F32))
+        n1[rows] = (vhat * vec[0:1] + vec[1:2]).astype(BF)
+        return 0
+
+    lax.fori_loop(0, t // CHUNK, first_norm, 0)
+    outs.append(io.load(n1, n1_out))
+    advance()
+
+    def columns(ref, lo):
+        return lambda i, slot: [(ref.at[:, pl.ds(pl.multiple_of(lo + i * COLS, LANES), COLS)], wb.at[slot])]
+
+    def qkv_step(i, slot):
+        qkv[:, lanes(i, COLS)] = (dot(n1[...], wb[slot]) + bias[:, lanes(i, COLS)]).astype(BF)
+
+    stream(io, 3 * D // COLS, columns(wa, 0), qkv_step)
+    outs.append(io.load(qkv, qkv_out))
+    advance()
+
+    def heads(i, _):
+        def at(k):
+            return lanes(k * (D // LANES) + i, LANES)
+
+        att[:, at(0)] = attend_pair(qkv[:, at(0)], qkv[:, at(1)], qkv[:, at(2)])
+        return 0
+
+    n_pairs = D // LANES
+    lax.fori_loop(0, n_pairs // 2, heads, 0)
+    advance()
+    lax.fori_loop(n_pairs // 2, n_pairs, heads, 0)
+    outs.append(io.load(att, att_out))
+    advance()
+
+    def proj_step(i, slot):
+        cols = lanes(i, COLS)
+        middle[:, cols] = xv[:, cols].astype(F32) + (dot(att[...], wb[slot]) + vec[4:5, cols])
+
+    stream(io, D // COLS, columns(wa, 3 * D), proj_step)
+    outs.append(io.load(middle, middle_out))
+
+    def second_norm(i, _):
+        rows = pl.ds(pl.multiple_of(i * CHUNK, CHUNK), CHUNK)
+        vhat, _r = norm_rows(middle[rows])
+        n2[rows] = (vhat * vec[5:6] + vec[6:7]).astype(BF)
+        return 0
+
+    lax.fori_loop(0, t // CHUNK, second_norm, 0)
+    outs.append(io.load(n2, n2_out))
+    while place[0] < 7 + 4:
+        advance()
+    gu.done()
+
+    out_base = io.locals(4)
+
+    def hidden_out(i, slot):
+        return [
+            pltpu.make_async_copy(buf.at[slot], out.at[:, lanes(i, COLS)], io.local.at[out_base + 2 * c + slot])
+            for c, (buf, out) in enumerate(((hid, hidden), (slo, slope)))
+        ]
+
+    def up_step(i, slot):
+        @pl.when(i >= 2)
+        def _():
+            for c in hidden_out(i - 2, slot):
+                c.wait()
+
+        value, grad = gelu_both(dot(n2[...], wb[slot]) + ub[:, lanes(i, COLS)])
+        hid[slot] = value.astype(BF)
+        slo[slot] = grad.astype(BF)
+        for c in hidden_out(i, slot):
+            c.start()
+
+    n_up = FF // COLS
+    stream(io, n_up // 2, columns(wu, 0), up_step)
+    advance()
+    stream(io, n_up // 2, columns(wu, FF // 2), lambda i, slot: up_step(i + n_up // 2, slot))
+    for i in (n_up - 2, n_up - 1):
+        for c in hidden_out(i, i % 2):
+            c.wait()
     cc.wait()
-    gd.pass_on(None)
-    gd.far(None)
-    gd.done(None)
-    for col in (cx, cc):
-        def fill():
-            cp = pltpu.make_async_copy(zero, col.dst, local.at[5])
-            cp.start(); cp.wait()
-        guarded(jnp.logical_not(col.host), fill)
+    outs.append(io.load(ogv, og))
+    while place[0] < len(line) + 3:
+        advance()
+    gd.done()
+    for c in outs:
+        c.wait()
     io.finish()
 
-def gather_all(a, u, d, x, c):
-    t = x.shape[1]*4
+
+def forward(a, u, d, clips, cot):
+    t = clips.shape[1] * 4
     any_ = pl.BlockSpec(memory_space=pl.ANY)
-    sh = lambda r, c_: jax.ShapeDtypeStruct((r, c_), BF)
-    return pl.pallas_call(gather_kernel,
-        out_shape=[sh(32*a.shape[0], a.shape[1]), sh(32*u.shape[0], u.shape[1]), sh(32*d.shape[0], d.shape[1]), sh(t,1024), sh(t,1024)],
-        in_specs=[any_]*5, out_specs=[any_]*5,
-        scratch_shapes=[pltpu.VMEM((t,1024),BF), pltpu.SemaphoreType.DMA((N_SLOTS,)), pltpu.SemaphoreType.DMA((N_SLOTS,)), pltpu.SemaphoreType.DMA((8,))],
-        compiler_params=pltpu.CompilerParams(collective_id=0, has_side_effects=True, vmem_limit_bytes=56*2**20))(a,u,d,x,c)
+    vmem = pl.BlockSpec(memory_space=pltpu.VMEM)
+    sh = jax.ShapeDtypeStruct
+    v = pltpu.VMEM
+    return pl.pallas_call(
+        forward_kernel,
+        out_shape=[
+            sh((D, a.shape[1]), BF),
+            sh((D, FF), BF),
+            sh((FF, D), BF),
+            sh((t, D), BF),
+            sh((t, D), BF),
+            sh((t, D), F32),
+            sh((t, D), BF),
+            sh((t, D), BF),
+            sh((t, 3 * D), BF),
+            sh((t, D), BF),
+            sh((t, FF), BF),
+            sh((t, FF), BF),
+            sh((8, D), F32),
+        ],
+        in_specs=[any_] * 5,
+        out_specs=[any_] * 12 + [vmem],
+        scratch_shapes=[
+            v((t, D), BF),
+            v((t, D), BF),
+            v((t, D), BF),
+            v((t, D), BF),
+            v((t, 3 * D), BF),
+            v((t, D), BF),
+            v((t, D), F32),
+            v((2, D, COLS), BF),
+            v((2, t, COLS), BF),
+            v((2, t, COLS), BF),
+            v((D, LANES), BF),
+            v((D, LANES), F32),
+            v((1, FF), F32),
+            v((1, 3 * D), F32),
+            pltpu.SemaphoreType.DMA((N_FORE,)),
+            pltpu.SemaphoreType.DMA((N_FORE,)),
+            pltpu.SemaphoreType.DMA((48,)),
+        ],
+        compiler_params=pltpu.CompilerParams(
+            collective_id=0, has_side_effects=True, vmem_limit_bytes=56 * 2**20
+        ),
+    )(a, u, d, clips, cot)
 
 
 class Reduce:
@@ -403,26 +628,36 @@
             own = self.half(0, h)[...]
             total = own.astype(F32) + self.stage[0].astype(F32) + self.stage[1].astype(F32)
             self.half(3, h)[...] = total.astype(own.dtype)
-        for k in (1, 2, 3):
+        for i, k in ((0, 3), (1, 1)):
             io.start(
-                self.z_slot[k],
+                self.z_slot[i],
                 lambda k=k: self.piece(io.z ^ k),
-                lambda k=k: self.pieces.at[k],
-                (io.dp, io.z ^ k),
+                lambda i=i: self.pieces.at[i],
+                (io.dp, io.z ^ 1),
             )
 
     def piece(self, z):
         return self.s(3).at[pl.ds(pl.multiple_of(z * self.r, self.r), self.r)]
 
+    def take(self, i):
+        spot = self.stage.at[i // 2, pl.ds(i % 2 * self.r, self.r)]
+        self.io.arrived(self.z_slot[i], lambda: self.pieces.at[i])
+        return self.io.load(self.pieces.at[i], spot), spot
+
+    def cross(self):
+        io = self.io
+        copy, spot = self.take(0)
+        copy.wait()
+        ref = self.piece(io.z ^ 2)
+        ref[...] = (ref[...].astype(F32) + spot[...].astype(F32)).astype(ref.dtype)
+        io.start(
+            self.z_slot[2], lambda: self.piece(io.z ^ 2), lambda: self.pieces.at[2], (io.dp, io.z ^ 2)
+        )
+
     def finish(self):
-        io, r = self.io, self.r
-        spots = [self.stage.at[i, pl.ds(h * r, r)] for i, h in ((0, 0), (0, 1), (1, 0))]
-        loads = []
-        for k in (1, 2, 3):
-            io.arrived(self.z_slot[k], lambda k=k: self.pieces.at[k])
-            loads.append(io.load(self.pieces.at[k], spots[k - 1]))
-        total = self.piece(io.z)[...].astype(F32)
-        for copy, spot in zip(loads, spots):
+        one, two = self.take(1), self.take(2)
+        total = self.piece(self.io.z)[...].astype(F32)
+        for copy, spot in (one, two):
             copy.wait()
             total = total + spot[...].astype(F32)
         self.out[...] = total
@@ -461,14 +696,8 @@
 N_LOCAL = 112
 
 
-def norm_rows(v):
-    center = v - jnp.mean(v, axis=-1, keepdims=True)
-    r = lax.rsqrt(jnp.mean(center * center, axis=-1, keepdims=True) + EPSILON)
-    return center * r, r
-
-
 def backward_kernel(
-    wa, wu, wd, og, x, middle, normed1, normed2, qkv_in, attended, hidden, slope, gain1, gain2, d_bias,
+    wa, wu, wd, og, x, middle, normed1, normed2, qkv_in, attended, hidden, slope, params,
     a_out, u_out, d_out, s_out, ret_out, ret_in, a_land, u_land, d_land, s_land, a_pieces, u_pieces, d_pieces, s_pieces,
     og2, ug2, bg2, hj2, np2, n1p2, atp2, flip, qkv, ag, xv, part, wdb, wb, tiles, acc, s_d, s_u, stage_d, stage_u,
     table, table_sib, s_s, stage_s, vec, ub,
@@ -527,36 +756,6 @@
     second_half = t
     d_rows = wdb.shape[1]
     w_rows = wb.shape[1]
-
-    def stream(n, copies, body):
-        base = io.locals(2 * len(copies(0, 0)))
-
-        def make(i, slot):
-            pairs = copies(i, slot)
-            return [
-                pltpu.make_async_copy(a, b, io.local.at[base + 2 * c + slot]) for c, (a, b) in enumerate(pairs)
-            ]
-
-        for c in make(0, 0):
-            c.start()
-
-        def step(i, _):
-            slot = i % 2
-
-            @pl.when(i + 1 < n)
-            def _():
-                for c in make(i + 1, (i + 1) % 2):
-                    c.start()
-
-            for c in make(i, slot):
-                c.wait()
-            body(i, slot)
-            return 0
-
-        lax.fori_loop(0, n, step, 0)
-
-    def lanes(i, width):
-        return pl.ds(pl.multiple_of(i * width, LANES), width)
 
     for c in first:
         c.wait()
@@ -591,6 +790,7 @@
         ug_copy(i).start()
 
     stream(
+        io,
         FF // d_rows,
         lambda i, slot: [
             (wd.at[pl.ds(pl.multiple_of(i * d_rows, d_rows), d_rows)], wdb.at[slot]),
@@ -623,7 +823,7 @@
     w_tile = lambda ref, lo, n: lambda i, slot: [
         (ref.at[pl.ds(pl.multiple_of(i * w_rows, w_rows), w_rows), pl.ds(lo, n)], wb.at[slot, :, pl.ds(0, n)])
     ]
-    stream(D // w_rows, w_tile(wu, 0, FF), up_back)
+    stream(io, D // w_rows, w_tile(wu, 0, FF), up_back)
     for c in third:
         c.wait()
     for i in (0, 1, 4, 5, 6):
@@ -634,7 +834,7 @@
         rows = pl.ds(pl.multiple_of(i * chunk, chunk), chunk)
         e = acc[rows]
         vhat, r = norm_rows(part[rows])
-        g = e * gain2[...]
+        g = e * params[5:6]
         grad = r * (
             g - jnp.mean(g, axis=-1, keepdims=True) - vhat * jnp.mean(g * vhat, axis=-1, keepdims=True)
         )
@@ -653,7 +853,7 @@
     def proj_back(i, slot):
         ag[:, lanes(i, w_rows)] = dot_nt(bg2[own], wb[slot, :, 0:D]).astype(BF)
 
-    stream(D // w_rows, w_tile(wa, 3 * D, D), proj_back)
+    stream(io, D // w_rows, w_tile(wa, 3 * D, D), proj_back)
 
     def heads(i, _):
         def at(k):
@@ -666,23 +866,26 @@
         vec[3:4, at(0)] = jnp.sum(dv.astype(F32), axis=0, keepdims=True)
         return 0
 
-    lax.fori_loop(0, D // LANES, heads, 0)
+    n_pairs = D // LANES
+    lax.fori_loop(0, n_pairs // 2, heads, 0)
+    red_d.fold()
+    lax.fori_loop(n_pairs // 2, n_pairs, heads, 0)
     jn_slot = io.slots(1)[0]
     pl.semaphore_wait(ready, 1)
     io.start(jn_slot, lambda: hj2.at[own], lambda: hj2.at[sib], core)
     red_u.relay()
-    red_d.fold()
+    red_d.cross()
 
     def qkv_back(i, slot):
         acc[:, lanes(i, w_rows)] = dot_nt(hj2[own], wb[slot, :, 0 : 3 * D])
 
-    stream(D // w_rows, w_tile(wa, 0, 3 * D), qkv_back)
+    stream(io, D // w_rows, w_tile(wa, 0, 3 * D), qkv_back)
 
     def first_norm(i, _):
         rows = pl.ds(pl.multiple_of(i * chunk, chunk), chunk)
         e = acc[rows]
         vhat, r = norm_rows(xv[rows].astype(F32))
-        g = e * gain1[...]
+        g = e * params[0:1]
         grad = r * (
             g - jnp.mean(g, axis=-1, keepdims=True) - vhat * jnp.mean(g * vhat, axis=-1, keepdims=True)
         )
@@ -750,6 +953,7 @@
         acc[...] += dot(tiles[slot], wdb[slot])
 
     stream(
+        io,
         FF // d_rows,
         lambda i, slot: [
             (wd.at[pl.ds(pl.multiple_of(i * d_rows, d_rows), d_rows)], wdb.at[slot]),
@@ -758,15 +962,18 @@
         down_step,
     )
     load_middle.wait()
-    qkv[:, 0:D] = (acc[...] + (part[...] - xv[...].astype(F32)) + d_bias[...]).astype(BF)
+    qkv[:, 0:D] = (acc[...] + (part[...] - xv[...].astype(F32)) + params[7:8]).astype(BF)
     back_out.start()
 
     red_u.fold()
+    red_u.cross()
     red_s.relay()
     red_a.relay()
     red_u.finish()
     red_s.fold()
     red_a.fold()
+    red_s.cross()
+    red_a.cross()
     red_s.finish()
     back_in.wait()
     back_out.wait()
@@ -774,7 +981,7 @@
     io.finish()
 
 
-def backward(wa, wu, wd, og, x, middle, normed1, normed2, qkv, attended, hidden, slope, gain1, gain2, d_bias):
+def backward(wa, wu, wd, og, x, middle, normed1, normed2, qkv, attended, hidden, slope, params):
     t = og.shape[0]
     any_ = pl.BlockSpec(memory_space=pl.ANY)
     vmem = pl.BlockSpec(memory_space=pltpu.VMEM)
@@ -788,7 +995,7 @@
         (sh((4, t // 4, D), BF), any_),
         (sh((4, t // 4, D), BF), any_),
     ]
-    for count, k in ((6, 2), (4, 1)):
+    for count, k in ((6, 2), (3, 1)):
         outs += [
             (sh((count, k * ra, FF), BF), any_),
             (sh((count, k * ra, FF), BF), any_),
@@ -799,7 +1006,7 @@
     results = pl.pallas_call(
         backward_kernel,
         out_shape=[o for o, _ in outs],
-        in_specs=[any_] * 12 + [vmem] * 3,
+        in_specs=[any_] * 12 + [vmem],
         out_specs=[o for _, o in outs],
         scratch_shapes=[
             v((2 * t, D), BF),
@@ -836,7 +1043,7 @@
         compiler_params=pltpu.CompilerParams(
             collective_id=1, has_side_effects=True, vmem_limit_bytes=60 * 2**20
         ),
-    )(wa, wu, wd, og, x, middle, normed1, normed2, qkv, attended, hidden, slope, gain1, gain2, d_bias)
+    )(wa, wu, wd, og, x, middle, normed1, normed2, qkv, attended, hidden, slope, params)
     return results[:6]
 
 
@@ -852,12 +1059,6 @@
         t - jnp.mean(t, axis=-1, keepdims=True) - vhat * jnp.mean(t * vhat, axis=-1, keepdims=True)
     )
     return grad, jnp.sum(e * vhat, axis=0), jnp.sum(e, axis=0)
-
-
-def gelu_both(u):
-    cdf = 0.5 * (1.0 + lax.erf(u * 0.7071067811865476))
-    pdf = 0.3989422804014327 * jnp.exp(-0.5 * u * u)
-    return u * cdf, cdf + u * pdf
 
 
 SMALL = (D, D, D, D, D, D, D, D, FF)
@@ -910,55 +1111,36 @@
     living_cot = living * out_cotangent
     tokens = (clips.astype(BF), living_cot.astype(BF))
     if links.short:
-        a_mat, u_mat, d_mat, x, out_grad = gather_all(shard_a, shard_u, shard_d, *tokens)
+        saved = forward(shard_a, shard_u, shard_d, *tokens)
+        qkv_proj_grad, up_grad, down_grad, small_grad, out_back, in_back = backward(*saved)
+        out_home, in_home = links.by_clip(out_back, slots), links.by_clip(in_back, slots)
+        small_out = small_grad[:3].reshape(-1)
     else:
         a_mat, u_mat, d_mat = (links.gather(shard) for shard in (shard_a, shard_u, shard_d))
         x, out_grad = (links.collect(t) for t in tokens)
-    x = x.astype(F32)
-
-    table = a_mat[:, 4 * D :].reshape(n_dp, n_seq, rows * LANES)
-    table = table.reshape(n, rows * LANES).astype(F32)
-    vectors, at = [], 0
-    for size in SMALL:
-        vectors.append(table[:, at : at + size // n].reshape(size))
-        at += size // n
-    gain1, shift1, q_bias, v_bias, p_bias, gain2, shift2, d_bias, u_bias = vectors
-
-    vhat1, r1 = norm_parts(x)
-    normed1 = (vhat1 * gain1 + shift1).astype(BF)
-    qkv_bias = jnp.concatenate([q_bias, jnp.zeros_like(q_bias), v_bias])
-    qkv_mat, proj_mat = a_mat[:, : 3 * D], a_mat[:, 3 * D : 4 * D]
-    qkv = (dot(normed1, qkv_mat) + qkv_bias).astype(BF)
-    attended = attend(qkv)
-    branch = dot(attended, proj_mat) + p_bias
-    middle = x + branch
-    vhat2, r2 = norm_parts(middle)
-    normed2 = (vhat2 * gain2 + shift2).astype(BF)
-    hidden, slope = gelu_both(dot(normed2, u_mat) + u_bias)
-    hidden = hidden.astype(BF)
-    slope = slope.astype(BF)
-    if links.short:
-        row = lambda v: v.reshape(1, -1)
-        qkv_proj_grad, up_grad, down_grad, small_grad, out_back, in_back = backward(
-            a_mat,
-            u_mat,
-            d_mat,
-            out_grad,
-            x.astype(BF),
-            middle,
-            normed1,
-            normed2,
-            qkv,
-            attended,
-            hidden,
-            slope,
-            row(gain1),
-            row(gain2),
-            row(d_bias),
-        )
-        out_home, in_home = links.by_clip(out_back, slots), links.by_clip(in_back, slots)
-        small_out = small_grad[:3].reshape(-1)
-    else:
+        x = x.astype(F32)
+
+        table = a_mat[:, 4 * D :].reshape(n_dp, n_seq, rows * LANES)
+        table = table.reshape(n, rows * LANES).astype(F32)
+        vectors, at = [], 0
+        for size in SMALL:
+            vectors.append(table[:, at : at + size // n].reshape(size))
+            at += size // n
+        gain1, shift1, q_bias, v_bias, p_bias, gain2, shift2, d_bias, u_bias = vectors
+
+        vhat1, r1 = norm_parts(x)
+        normed1 = (vhat1 * gain1 + shift1).astype(BF)
+        qkv_bias = jnp.concatenate([q_bias, jnp.zeros_like(q_bias), v_bias])
+        qkv_mat, proj_mat = a_mat[:, : 3 * D], a_mat[:, 3 * D : 4 * D]
+        qkv = (dot(normed1, qkv_mat) + qkv_bias).astype(BF)
+        attended = attend(qkv)
+        branch = dot(attended, proj_mat) + p_bias
+        middle = x + branch
+        vhat2, r2 = norm_parts(middle)
+        normed2 = (vhat2 * gain2 + shift2).astype(BF)
+        hidden, slope = gelu_both(dot(normed2, u_mat) + u_bias)
+        hidden = hidden.astype(BF)
+        slope = slope.astype(BF)
         out_part = branch + dot(hidden, d_mat) + d_bias
         out_home = links.hand_back(out_part.astype(BF), slots)
         down_grad = links.reduce(dot_tn(hidden, out_grad))

time: 386 us -> 324 us (0.84)
  Pallas kernels: 332 us -> 306 us
  matrix products: 21.8 us -> 0 us
  other arithmetic: 12.1 us -> 6.71 us
  local copies, waits for them, and re-layouts: 13.1 us -> 8.48 us
    pallas_call x2 -> x1, Pallas kernels: 151 us -> 124 us  [forward(): pl.pallas_call(forward_kernel, out_shape=[sh((D, a.shape[1]), BF), sh((D,...]
    dot_general x3 -> x0, matrix products: 21.8 us -> none  [dot(): return jnp.dot(a, b, preferred_element_type=F32)]
where the time goes in v4:
time: 324 us; the launch traced here: 323 us
  Pallas kernels  306 us (94%)
  local copies, waits for them, and re-layouts  8.48 us (3%)
  other arithmetic  6.71 us (2%)
    pallas_call x1, Pallas kernels, backward(): pl.pallas_call(backward_kernel, out_shape=[o for o, _ in outs], in_specs=...  181 us
    pallas_call x1, Pallas kernels, forward(): pl.pallas_call(forward_kernel, out_shape=[sh((D, a.shape[1]), BF), sh((D,...  124 us

profile of v4, /device:TPU:0, one launch (start us, length us, event | category | flops | bytes accessed | tf_op | source)
XLA Modules:
  0.0 322.6 jit_solution(17398096219879437703)
XLA Ops:
  1.4 0.0 copy-start.8
  1.4 0.0 copy-start.10
  1.4 0.0 copy-start.11
  1.4 0.0 copy-start.12
  1.4 0.0 copy-start.13
  1.4 0.0 copy-start.14
  1.4 0.0 copy-start.15
  1.4 0.0 copy-start.16
  1.5 0.0 copy-start.17
  1.5 0.0 copy-start.18
  1.5 0.0 copy-start.1
  1.5 2.6 multiply_convert_fusion.cot
  4.2 0.1 reshape.67
  4.3 0.0 copy-start.2
  4.5 0.1 concatenate.8
  4.6 0.7 pad_maximum_fusion.a
  5.4 1.0 convert_element_type.37.clips
  6.4 0.8 convert_element_type.34.u
  7.2 0.8 convert_element_type.36.d
  8.1 124.1 %shard_map.271 = (bf16[1024,4224]{1,0:T(8,128)(2,1)}, bf16[1024,4096]{1,0:T(8,128)(2,1)}, bf16[4096,1024]{1,0:T(8,128)(2,1)}, bf16[512,1024]{1,0:T(8,128)(2,1)},...) custom-call(bf16[32,4224]{1,0:T(8,128)(2,1)} %pad_maximum_fusion.a, ...), custom_call_target="tpu_custom_call" | custom-call | tf_op jit(solution)/shard_map/pallas_call | solution.py:545
  132.2 181.5 %shard_map.272 = (f32[32,4096]{1,0:T(8,128)}, f32[32,4096]{1,0:T(8,128)}, f32[128,1024]{1,0:T(8,128)}, f32[8,128]{1,0:T(8,128)}, bf16[4,128,1024]{2,1,0:T(8,128)...) custom-call(bf16[1024,4224]{1,0:T(8,128)(2,1)} %get-tuple-element.34, ...), custom_call_target="tpu_custom_call" | custom-call | tf_op jit(solution)/shard_map/pallas_call | solution.py:1006
  313.7 0.0 copy-start
  313.8 1.6 constant_dynamic-slice_fusion.2
  315.4 0.2 copy-done
  315.6 2.2 convert_add_fusion
  317.9 0.8 copy.31
  318.7 0.2 copy-done.6
  319.0 0.9 copy.34
  319.8 0.9 copy.33
  320.7 0.7 copy.32
  321.4 0.6 fusion
  322.0 0.5 slice_bitcast_fusion.3
  (42 shorter events, 0.2 us)
Async XLA Ops:
  0.6 3.5 %copy-start.7 = (f32[98304]{0:T(1024)S(1)}, f32[98304]{0:T(1024)}, u32[]{:S(2)}) copy-start(f32[98304]{0:T(1024)} %param.21) | copy-start | bytes 1179652
  1.4 2.9 copy-start.8
  1.4 3.0 copy-start.10
  1.4 3.0 copy-start.11
  1.4 3.0 copy-start.12
  1.4 3.0 copy-start.13
  1.4 3.0 copy-start.14
  1.4 3.0 copy-start.15
  1.4 3.0 copy-start.16
  1.5 3.0 copy-start.17
  1.5 3.0 copy-start.18
  1.5 3.9 %copy-start.1 = (f32[3,128,1024]{2,1,0:T(8,128)S(1)}, f32[3,128,1024]{2,1,0:T(8,128)}, u32[]{:S(2)}) copy-start(f32[3,128,1024]{2,1,0:T(8,128)} %param.16) | copy-start | bytes 4718596
  4.3 2.1 copy-start.2
  5.4 1.9 copy-start.3
  313.7 1.9 copy-start
  315.6 2.2 copy-start.4
  317.9 1.1 copy-start.6
  317.9 2.0 copy-start.5
  317.9 3.5 %copy-start.9 = (f32[8,128]{1,0:T(8,128)S(1)}, f32[8,128]{1,0:T(8,128)}, u32[]{:S(2)}) copy-start(f32[8,128]{1,0:T(8,128)} %get-tuple-element.49) | copy-start | bytes 12292

commit v5 on v4

--- a/solution.py
+++ b/solution.py
@@ -394,14 +394,16 @@
 
 def forward_kernel(
     a, u, d, clips, cot,
-    wa, wu, wd, og, x_out, middle_out, n1_out, n2_out, qkv_out, att_out, hidden, slope, vec,
-    xv, ogv, n1, n2, qkv, att, middle, wb, hid, slo, table, wide, ub, bias,
+    wa, wu, wd, og, x_out, middle_out, n1_out, n2_out, qkv_out, att_out, hidden, slope, vec, d_terms,
+    xv, og2, n1, n2, qkv, att, middle, wb, hid, hid2, terms, slo, table, wide, ub, bias,
     send, recv, local,
 ):
     io = Copies(send, recv, local)
     ga, gu, gd = Gather(io, a, wa), Gather(io, u, wu), Gather(io, d, wd)
-    cx, cc = Collect(io, clips, xv), Collect(io, cot, ogv)
     t = xv.shape[0]
+    own, sib = pl.ds(0, t), pl.ds(t, t)
+    core = (io.dp ^ 1, io.z)
+    cx, cc = Collect(io, clips, xv), Collect(io, cot, og2.at[own])
     meet(io)
 
     line = [(g, k) for g in (ga, gu, gd) for k in range(4)]
@@ -499,35 +501,59 @@
         advance()
     gu.done()
 
-    out_base = io.locals(4)
-
-    def hidden_out(i, slot):
-        return [
-            pltpu.make_async_copy(buf.at[slot], out.at[:, lanes(i, COLS)], io.local.at[out_base + 2 * c + slot])
-            for c, (buf, out) in enumerate(((hid, hidden), (slo, slope)))
-        ]
+    out_base = io.locals(2)
+    hid_slots = io.slots(4)
+
+    def slope_out(i, slot):
+        return pltpu.make_async_copy(slo.at[slot], slope.at[:, lanes(i, COLS)], io.local.at[out_base + slot])
+
+    def hid_copy(i):
+        j = (io.dp ^ i) // 2
+        return io.remote(hid_slots[0] + j, hid.at[:, lanes(i, COLS)], hid2.at[sib, lanes(j, COLS)], core)
 
     def up_step(i, slot):
         @pl.when(i >= 2)
         def _():
-            for c in hidden_out(i - 2, slot):
-                c.wait()
+            slope_out(i - 2, slot).wait()
 
         value, grad = gelu_both(dot(n2[...], wb[slot]) + ub[:, lanes(i, COLS)])
-        hid[slot] = value.astype(BF)
+        hid[:, lanes(i, COLS)] = value.astype(BF)
         slo[slot] = grad.astype(BF)
-        for c in hidden_out(i, slot):
-            c.start()
+        slope_out(i, slot).start()
+
+        @pl.when((io.dp ^ i) % 2 == 1)
+        def _():
+            hid_copy(i).start()
+
+        @pl.when((io.dp ^ i) % 2 == 0)
+        def _():
+            hid2[own, lanes((io.dp ^ i) // 2, COLS)] = value.astype(BF)
 
     n_up = FF // COLS
     stream(io, n_up // 2, columns(wu, 0), up_step)
     advance()
     stream(io, n_up // 2, columns(wu, FF // 2), lambda i, slot: up_step(i + n_up // 2, slot))
+    outs.append(io.load(hid, hidden))
+    advance()
+    cc.wait()
+    outs.append(io.load(og2.at[own], og))
+    og_slot = io.slots(1)[0]
+    io.start(og_slot, lambda: og2.at[own], lambda: og2.at[sib], core)
     for i in (n_up - 2, n_up - 1):
-        for c in hidden_out(i, i % 2):
-            c.wait()
-    cc.wait()
-    outs.append(io.load(ogv, og))
+        slope_out(i, i % 2).wait()
+    advance()
+    io.arrived(og_slot, lambda: og2.at[sib])
+    for j in range(4):
+        hid_copy(io.dp ^ (2 * j + 1)).wait()
+
+    def down_terms(j, _):
+        terms[j] = dot_tn(hid2[:, lanes(j, COLS)], og2[...]).astype(BF)
+        return 0
+
+    lax.fori_loop(0, 2, down_terms, 0)
+    advance()
+    lax.fori_loop(2, 4, down_terms, 0)
+    outs.append(io.load(terms, d_terms))
     while place[0] < len(line) + 3:
         advance()
     gd.done()
@@ -558,19 +584,22 @@
             sh((t, FF), BF),
             sh((t, FF), BF),
             sh((8, D), F32),
+            sh((4, FF // 8, D), BF),
         ],
         in_specs=[any_] * 5,
-        out_specs=[any_] * 12 + [vmem],
+        out_specs=[any_] * 12 + [vmem, any_],
         scratch_shapes=[
             v((t, D), BF),
-            v((t, D), BF),
+            v((2 * t, D), BF),
             v((t, D), BF),
             v((t, D), BF),
             v((t, 3 * D), BF),
             v((t, D), BF),
             v((t, D), F32),
             v((2, D, COLS), BF),
-            v((2, t, COLS), BF),
+            v((t, FF), BF),
+            v((2 * t, FF // 2), BF),
+            v((4, FF // 8, D), BF),
             v((2, t, COLS), BF),
             v((D, LANES), BF),
             v((D, LANES), F32),
@@ -692,16 +721,17 @@
             io.arrived(self.slots[s], lambda s=s: self.dst.at[s], self.host((io.z + s) % 4))
 
 
-N_BACK = 120
-N_LOCAL = 112
+N_BACK = 140
+N_LOCAL = 150
 
 
 def backward_kernel(
-    wa, wu, wd, og, x, middle, normed1, normed2, qkv_in, attended, hidden, slope, params,
-    a_out, u_out, d_out, s_out, ret_out, ret_in, a_land, u_land, d_land, s_land, a_pieces, u_pieces, d_pieces, s_pieces,
-    og2, ug2, bg2, hj2, np2, n1p2, atp2, flip, qkv, ag, xv, part, wdb, wb, tiles, acc, s_d, s_u, stage_d, stage_u,
-    table, table_sib, s_s, stage_s, vec, ub,
-    send, recv, local, ready,
+    wa, wu, wd, og_in, x, middle, normed1, normed2, qkv_in, attended, hidden, slope, params, d_terms,
+    qkv_out, p_out, u_out, d_out, s_out, ret_out, ret_in,
+    a_land, u_land, d_land, s_land, a_pieces, u_pieces, d_pieces, s_pieces,
+    og, ug2, bg2, jn2, np2, n1p2, atp2, flip, qkv, ag, ob, xv, part, wdb, wb, tiles, hid, acc, s_d, s_u,
+    stage_d, stage_u, stage_a, table, table_sib, s_s, stage_s, vec, ub,
+    send, recv, local,
 ):
     io = Copies(send, recv, local)
     dp, z = io.dp, io.z
@@ -711,16 +741,17 @@
 
     red_d = Reduce(io, d_out.shape[0], lambda j: s_d.at[j], d_land, d_pieces, stage_d, d_out)
     red_u = Reduce(io, u_out.shape[0], lambda j: s_u.at[j], u_land, u_pieces, stage_u, u_out)
-    n_a = a_out.shape[0]
-    red_a = Reduce(io, n_a, lambda j: ug2.at[pl.ds(j * 4 * n_a, 4 * n_a)], a_land, a_pieces, stage_u, a_out)
+    n_a = p_out.shape[0]
+
+    def part_of_a(c):
+        blocks = lambda j: ug2.at[pl.ds(j * 4 * n_a, 4 * n_a), pl.ds(c * D, D)]
+        out = p_out if c == 3 else qkv_out.at[:, pl.ds(c * D, D)]
+        return Reduce(io, n_a, blocks, a_land.at[c], a_pieces.at[c], stage_a, out)
+
+    red_q, red_k, red_v, red_p = (part_of_a(c) for c in range(4))
     red_s = Reduce(io, s_out.shape[0], lambda j: s_s.at[j], s_land, s_pieces, stage_s, s_out)
     back_in = HandBack(io, qkv.at[:, pl.ds(D, D)], ret_in)
-    back_out = HandBack(io, qkv.at[:, pl.ds(0, D)], ret_out)
-
-    bar = pltpu.get_barrier_semaphore()
-    partners = [(dp, z ^ k) for k in (1, 2, 3)] + [(dp ^ b, z) for b in (1, 2, 4)]
-    for p in partners:
-        pl.semaphore_signal(bar, inc=1, device_id=p, device_id_type=MESH)
+    back_out = HandBack(io, ob, ret_out)
 
     def planes(src, dst):
         width = dst.shape[1] // 4
@@ -732,8 +763,12 @@
             for j in range(4)
         ]
 
-    first = [io.load(og, og2.at[own])] + planes(hidden, hj2.at[:, pl.ds(0, FF // 2)])
-    pl.semaphore_wait(bar, len(partners))
+    load_d = io.load(d_terms, s_d)
+    load_og = io.load(og_in, og)
+    load_x = [io.load(x, xv), io.load(middle, part)]
+    meet(io)
+    load_d.wait()
+    red_d.start()
 
     def swap_planes(src, dst):
         width = dst.shape[1] // 4
@@ -747,47 +782,24 @@
             )
         return [(slots[j], lambda j=j: dst.at[sib, pl.ds(j * width, width)]) for j in range(4)]
 
-    og_slot = io.slots(1)[0]
-    io.start(og_slot, lambda: og, lambda: og2.at[sib], core)
-    swapped_h = swap_planes(hidden, hj2.at[:, pl.ds(0, FF // 2)])
     swapped_2 = swap_planes(normed2, np2)
-    swapped_1 = swap_planes(normed1, n1p2) + swap_planes(attended, atp2)
-    second = planes(normed2, np2)
-    second_half = t
     d_rows = wdb.shape[1]
     w_rows = wb.shape[1]
-
-    for c in first:
-        c.wait()
-    io.arrived(og_slot, lambda: og2.at[sib])
-    for slot, ref in swapped_h:
-        io.arrived(slot, ref)
-    third = planes(normed1, n1p2) + planes(attended, atp2)
-    third += [io.load(qkv_in, qkv), io.load(x, xv), io.load(middle, part)]
-    width = FF // 8
-    for j in (3, 1, 2, 0):
-        s_d[j] = dot_tn(hj2[:, j * width : (j + 1) * width], og2[...]).astype(BF)
-        if j == 3:
-            red_d.send(0, 3, 0, 2)
-            red_d.send(1, 3, 1, 4)
-        elif j == 1:
-            red_d.send(2, 1, 0, 2)
-        elif j == 2:
-            red_d.send(3, 2, 1, 4)
-    pl.semaphore_signal(ready, inc=1, device_id=core, device_id_type=MESH)
-    vec[7:8] = jnp.sum(og2[own].astype(F32), axis=0, keepdims=True)
-
+    load_og.wait()
+
+    acc[...] = jnp.zeros_like(acc)
     ug_slots = io.slots(FF // d_rows)
 
     def ug_copy(i):
         return io.remote(ug_slots[0] + i, ug2.at[own, lanes(i, d_rows)], ug2.at[sib, lanes(i, d_rows)], core)
 
     def hidden_step(i, slot):
-        grad = dot_nt(og2[own], wdb[slot]) * tiles[slot].astype(F32)
+        grad = dot_nt(og[...], wdb[slot]) * tiles[slot].astype(F32)
         low = grad.astype(BF)
         ug2[own, lanes(i, d_rows)] = low
         ub[:, lanes(i, d_rows)] = jnp.sum(low.astype(F32), axis=0, keepdims=True)
         ug_copy(i).start()
+        acc[...] += dot(hid[slot], wdb[slot])
 
     stream(
         io,
@@ -795,9 +807,19 @@
         lambda i, slot: [
             (wd.at[pl.ds(pl.multiple_of(i * d_rows, d_rows), d_rows)], wdb.at[slot]),
             (slope.at[:, lanes(i, d_rows)], tiles.at[slot]),
+            (hidden.at[:, lanes(i, d_rows)], hid.at[slot]),
         ],
         hidden_step,
     )
+    for c in load_x:
+        c.wait()
+    ob[...] = (acc[...] + (part[...] - xv[...].astype(F32)) + params[7:8]).astype(BF)
+    back_out.start()
+    second = planes(normed2, np2)
+    third = planes(normed1, n1p2) + planes(attended, atp2)
+    third += [io.load(qkv_in, qkv)]
+    swapped_1 = swap_planes(normed1, n1p2)
+    swapped_3 = swap_planes(attended, atp2)
 
     for c in second:
         c.wait()
@@ -808,14 +830,14 @@
         ug_copy(i).wait_recv()
 
     def up_step(i, _):
-        block = dot(flip[...], ug2[:, lanes(i, 512)]).astype(BF)
+        block = dot(flip[...], ug2[:, lanes(i, COLS)]).astype(BF)
         for j in range(4):
-            s_u[j, :, lanes(i, 512)] = block[j * LANES : (j + 1) * LANES]
+            s_u[j, :, lanes(i, COLS)] = block[j * LANES : (j + 1) * LANES]
         return 0
 
-    lax.fori_loop(0, FF // 512, up_step, 0)
+    lax.fori_loop(0, FF // COLS, up_step, 0)
+    red_d.relay()
     red_u.start()
-    red_d.relay()
 
     def up_back(i, slot):
         acc[:, lanes(i, w_rows)] = dot_nt(ug2[own], wb[slot, :, 0:FF])
@@ -826,12 +848,10 @@
     stream(io, D // w_rows, w_tile(wu, 0, FF), up_back)
     for c in third:
         c.wait()
-    for i in (0, 1, 4, 5, 6):
-        vec[i : i + 1] = jnp.zeros((1, D), F32)
-    chunk = 128
+    vec[...] = jnp.zeros_like(vec)
 
     def second_norm(i, _):
-        rows = pl.ds(pl.multiple_of(i * chunk, chunk), chunk)
+        rows = pl.ds(pl.multiple_of(i * CHUNK, CHUNK), CHUNK)
         e = acc[rows]
         vhat, r = norm_rows(part[rows])
         g = e * params[5:6]
@@ -841,12 +861,14 @@
         vec[5:6] += jnp.sum(e * vhat, axis=0, keepdims=True)
         vec[6:7] += jnp.sum(e, axis=0, keepdims=True)
         part[rows] = grad
-        low = (og2[rows].astype(F32) + grad).astype(BF)
+        out_grad = og[rows].astype(F32)
+        low = (out_grad + grad).astype(BF)
         bg2[rows] = low
         vec[4:5] += jnp.sum(low.astype(F32), axis=0, keepdims=True)
+        vec[7:8] += jnp.sum(out_grad, axis=0, keepdims=True)
         return 0
 
-    lax.fori_loop(0, t // chunk, second_norm, 0)
+    lax.fori_loop(0, t // CHUNK, second_norm, 0)
     bg_slot = io.slots(1)[0]
     io.start(bg_slot, lambda: bg2.at[own], lambda: bg2.at[sib], core)
 
@@ -854,6 +876,19 @@
         ag[:, lanes(i, w_rows)] = dot_nt(bg2[own], wb[slot, :, 0:D]).astype(BF)
 
     stream(io, D // w_rows, w_tile(wa, 3 * D, D), proj_back)
+    for slot in range(FF // d_rows):
+        ug_copy(slot).wait_send()
+    for slot, ref in swapped_3:
+        io.arrived(slot, ref)
+    flip[...] = atp2[...].T
+    io.arrived(bg_slot, lambda: bg2.at[sib])
+
+    def proj_step(i, _):
+        ug2[own, lanes(6 + i, COLS)] = dot(flip[...], bg2[:, lanes(i, COLS)]).astype(BF)
+        return 0
+
+    lax.fori_loop(0, D // COLS, proj_step, 0)
+    red_p.start()
 
     def heads(i, _):
         def at(k):
@@ -861,7 +896,7 @@
 
         dq, dk, dv = attend_back_pair(qkv[:, at(0)], qkv[:, at(1)], qkv[:, at(2)], ag[:, at(0)])
         for k, grad in enumerate((dq, dk, dv)):
-            hj2[own, at(k)] = grad
+            jn2[own, at(k)] = grad
         vec[2:3, at(0)] = jnp.sum(dq.astype(F32), axis=0, keepdims=True)
         vec[3:4, at(0)] = jnp.sum(dv.astype(F32), axis=0, keepdims=True)
         return 0
@@ -871,18 +906,32 @@
     red_d.fold()
     lax.fori_loop(n_pairs // 2, n_pairs, heads, 0)
     jn_slot = io.slots(1)[0]
-    pl.semaphore_wait(ready, 1)
-    io.start(jn_slot, lambda: hj2.at[own], lambda: hj2.at[sib], core)
+    io.start(jn_slot, lambda: jn2.at[own], lambda: jn2.at[sib], core)
     red_u.relay()
     red_d.cross()
 
-    def qkv_back(i, slot):
-        acc[:, lanes(i, w_rows)] = dot_nt(hj2[own], wb[slot, :, 0 : 3 * D])
-
-    stream(io, D // w_rows, w_tile(wa, 0, 3 * D), qkv_back)
+    for slot, ref in swapped_1:
+        io.arrived(slot, ref)
+    flip[...] = n1p2[...].T
+
+    def first_back(i, slot):
+        acc[:, lanes(i, w_rows)] = dot_nt(jn2[own], wb[slot, :, 0 : 3 * D])
+
+    stream(io, D // w_rows, w_tile(wa, 0, 3 * D), first_back)
+    io.arrived(jn_slot, lambda: jn2.at[sib])
+
+    def qkv_step(i, _):
+        ug2[own, lanes(i, COLS)] = dot(flip[...], jn2[:, lanes(i, COLS)]).astype(BF)
+        return 0
+
+    for c, red in enumerate((red_q, red_k, red_v)):
+        lax.fori_loop(c * D // COLS, (c + 1) * D // COLS, qkv_step, 0)
+        red.start()
+    red_p.relay()
+    red_d.finish()
 
     def first_norm(i, _):
-        rows = pl.ds(pl.multiple_of(i * chunk, chunk), chunk)
+        rows = pl.ds(pl.multiple_of(i * CHUNK, CHUNK), CHUNK)
         e = acc[rows]
         vhat, r = norm_rows(xv[rows].astype(F32))
         g = e * params[0:1]
@@ -894,7 +943,7 @@
         qkv[rows, D : 2 * D] = (part[rows] + grad).astype(BF)
         return 0
 
-    lax.fori_loop(0, t // chunk, first_norm, 0)
+    lax.fori_loop(0, t // CHUNK, first_norm, 0)
     back_in.start()
 
     spread_n = lax.broadcasted_iota(jnp.int32, (32, D), 0)
@@ -916,79 +965,46 @@
     table_slot = io.slots(1)[0]
     io.start(table_slot, lambda: table, lambda: table_sib, core)
 
-    for slot in range(FF // d_rows):
-        ug_copy(slot).wait_send()
-    for slot, ref in swapped_1:
-        io.arrived(slot, ref)
-    flip[...] = atp2[...].T
-    io.arrived(bg_slot, lambda: bg2.at[sib])
-
-    def proj_step(i, _):
-        block = dot(flip[...], bg2[:, lanes(i, 512)]).astype(BF)
-        ug2[own, lanes(6 + i, 512)] = block
-        return 0
-
-    lax.fori_loop(0, D // 512, proj_step, 0)
-    flip[...] = n1p2[...].T
-    io.arrived(jn_slot, lambda: hj2.at[sib])
-
-    def qkv_step(i, _):
-        block = dot(flip[...], hj2[:, lanes(i, 512)]).astype(BF)
-        ug2[own, lanes(i, 512)] = block
-        return 0
-
-    lax.fori_loop(0, 3 * D // 512, qkv_step, 0)
-    red_a.start()
     io.arrived(table_slot, lambda: table_sib)
     for j in range(4):
         rows = pl.ds(pl.multiple_of((dp ^ (2 * j)) * 32, 32), 32)
         s_s[j] = table[rows] + table_sib[rows]
     red_s.start()
-    red_d.finish()
-
-    load_middle = io.load(middle, part)
-    acc[...] = jnp.zeros_like(acc)
-
-    def down_step(i, slot):
-        acc[...] += dot(tiles[slot], wdb[slot])
-
-    stream(
-        io,
-        FF // d_rows,
-        lambda i, slot: [
-            (wd.at[pl.ds(pl.multiple_of(i * d_rows, d_rows), d_rows)], wdb.at[slot]),
-            (hidden.at[:, lanes(i, d_rows)], tiles.at[slot]),
-        ],
-        down_step,
-    )
-    load_middle.wait()
-    qkv[:, 0:D] = (acc[...] + (part[...] - xv[...].astype(F32)) + params[7:8]).astype(BF)
-    back_out.start()
 
     red_u.fold()
+    red_q.relay()
+    red_k.relay()
+    red_v.relay()
+    red_s.relay()
     red_u.cross()
-    red_s.relay()
-    red_a.relay()
-    red_u.finish()
+    red_p.fold()
+    red_q.fold()
+    red_k.fold()
+    red_p.cross()
+    red_v.fold()
+    red_q.cross()
+    red_k.cross()
     red_s.fold()
-    red_a.fold()
+    red_v.cross()
     red_s.cross()
-    red_a.cross()
-    red_s.finish()
+    for red in (red_u, red_p, red_q, red_k):
+        red.finish()
     back_in.wait()
     back_out.wait()
-    red_a.finish()
+    red_v.finish()
+    red_s.finish()
     io.finish()
 
 
-def backward(wa, wu, wd, og, x, middle, normed1, normed2, qkv, attended, hidden, slope, params):
-    t = og.shape[0]
+def backward(*saved):
+    t = saved[3].shape[0]
     any_ = pl.BlockSpec(memory_space=pl.ANY)
     vmem = pl.BlockSpec(memory_space=pltpu.VMEM)
     sh = jax.ShapeDtypeStruct
     ra, rd, rs = D // 32, FF // 32, 8
     outs = [
-        (sh((ra, FF), F32), vmem),
+        (sh((ra, 3 * D), F32), vmem),
+        (sh((ra, D), F32), vmem),
         (sh((ra, FF), F32), vmem),
         (sh((rd, D), F32), vmem),
         (sh((rs, LANES), F32), vmem),
@@ -997,7 +1013,7 @@
     ]
     for count, k in ((6, 2), (3, 1)):
         outs += [
-            (sh((count, k * ra, FF), BF), any_),
+            (sh((4, count, k * ra, D), BF), any_),
             (sh((count, k * ra, FF), BF), any_),
             (sh((count, k * rd, D), BF), any_),
             (sh((count, k * rs, LANES), F32), any_),
@@ -1006,10 +1022,10 @@
     results = pl.pallas_call(
         backward_kernel,
         out_shape=[o for o, _ in outs],
-        in_specs=[any_] * 12 + [vmem],
+        in_specs=[any_] * 12 + [vmem, any_],
         out_specs=[o for _, o in outs],
         scratch_shapes=[
-            v((2 * t, D), BF),
+            v((t, D), BF),
             v((2 * t, FF), BF),
             v((2 * t, D), BF),
             v((2 * t, 3 * D), BF),
@@ -1020,15 +1036,18 @@
             v((t, 3 * D), BF),
             v((t, D), BF),
             v((t, D), BF),
+            v((t, D), BF),
             v((t, D), F32),
             v((2, 512, D), BF),
             v((2, 256, FF), BF),
+            v((2, t, 512), BF),
             v((2, t, 512), BF),
             v((t, D), F32),
             v((4, 4 * rd, D), BF),
             v((4, 4 * ra, FF), BF),
             v((2, 2 * rd, D), BF),
             v((2, 2 * ra, FF), BF),
+            v((2, 2 * ra, D), BF),
             v((32 * rs, LANES), F32),
             v((32 * rs, LANES), F32),
             v((4, 4 * rs, LANES), F32),
@@ -1038,13 +1057,12 @@
             pltpu.SemaphoreType.DMA((N_BACK,)),
             pltpu.SemaphoreType.DMA((N_BACK,)),
             pltpu.SemaphoreType.DMA((N_LOCAL,)),
-            pltpu.SemaphoreType.REGULAR,
         ],
         compiler_params=pltpu.CompilerParams(
             collective_id=1, has_side_effects=True, vmem_limit_bytes=60 * 2**20
         ),
-    )(wa, wu, wd, og, x, middle, normed1, normed2, qkv, attended, hidden, slope, params)
-    return results[:6]
+    )(*saved)
+    return results[:7]
 
 
 def norm_parts(v):
@@ -1112,7 +1130,7 @@
     tokens = (clips.astype(BF), living_cot.astype(BF))
     if links.short:
         saved = forward(shard_a, shard_u, shard_d, *tokens)
-        qkv_proj_grad, up_grad, down_grad, small_grad, out_back, in_back = backward(*saved)
+        qkv_grad, proj_grad, up_grad, down_grad, small_grad, out_back, in_back = backward(*saved)
         out_home, in_home = links.by_clip(out_back, slots), links.by_clip(in_back, slots)
         small_out = small_grad[:3].reshape(-1)
     else:
@@ -1169,7 +1187,8 @@
         grad_table = jnp.pad(grad_table, ((0, 0), (0, rows * LANES - width)))
         d_a = [dot_tn(normed1, joined), dot_tn(attended, branch_grad), grad_table.reshape(n * rows, LANES)]
         a_grad = links.reduce(jnp.concatenate(d_a, axis=1))
-        qkv_proj_grad, small_out = a_grad[:, : 4 * D], a_grad[:, 4 * D :].reshape(-1)
+        qkv_grad, proj_grad = a_grad[:, : 3 * D], a_grad[:, 3 * D : 4 * D]
+        small_out = a_grad[:, 4 * D :].reshape(-1)
     block_out = living * (clips + out_home.astype(F32))
     input_grad = living_cot + in_home.astype(F32)
     pieces, at = [], 0
@@ -1182,10 +1201,10 @@
         input_grad,
         g1,
         s1,
-        qkv_proj_grad[:, : 3 * D].reshape(-1),
+        qkv_grad.reshape(-1),
         qb,
         vb,
-        qkv_proj_grad[:, 3 * D :].reshape(-1),
+        proj_grad.reshape(-1),
         pb,
         g2,
         s2,

time: 324 us -> 291 us (0.90)
  Pallas kernels: 306 us -> 272 us
    pallas_call x1, Pallas kernels: 181 us -> 144 us  [backward(): pl.pallas_call(backward_kernel, out_shape=[o for o, _ in outs], in_specs=...]
    pallas_call x1, Pallas kernels: 124 us -> 129 us  [forward(): pl.pallas_call(forward_kernel, out_shape=[sh((D, a.shape[1]), BF), sh((D,...]
where the time goes in v5:
time: 291 us; the launch traced here: 289 us
  Pallas kernels  272 us (93%)
  local copies, waits for them, and re-layouts  8.23 us (3%)
  other arithmetic  6.71 us (2%)
    pallas_call x1, Pallas kernels, backward(): pl.pallas_call(backward_kernel, out_shape=[o for o, _ in outs], in_specs=...  144 us
    pallas_call x1, Pallas kernels, forward(): pl.pallas_call(forward_kernel, out_shape=[sh((D, a.shape[1]), BF), sh((D,...  129 us

profile of v5, /device:TPU:0, one launch (start us, length us, event | category | flops | bytes accessed | tf_op | source)
XLA Modules:
  0.0 288.8 jit_solution(13776563152564583908)
XLA Ops:
  1.4 0.0 copy-start.8
  1.4 0.0 copy-start.11
  1.4 0.0 copy-start.12
  1.4 0.0 copy-start.13
  1.4 0.0 copy-start.14
  1.4 0.0 copy-start.15
  1.4 0.0 copy-start.16
  1.4 0.0 copy-start.17
  1.5 0.0 copy-start.18
  1.5 0.0 copy-start.19
  1.5 0.0 copy-start.1
  1.5 2.6 multiply_convert_fusion.cot
  4.2 0.1 reshape.67
  4.3 0.0 copy-start.2
  4.3 0.0 copy-done.12
  4.5 0.1 concatenate.8
  4.6 0.7 pad_maximum_fusion.a
  5.4 1.0 convert_element_type.37.clips
  6.4 0.8 convert_element_type.34.u
  7.2 0.8 convert_element_type.36.d
  8.1 128.5 %shard_map.271 = (bf16[1024,4224]{1,0:T(8,128)(2,1)}, bf16[1024,4096]{1,0:T(8,128)(2,1)}, bf16[4096,1024]{1,0:T(8,128)(2,1)}, bf16[512,1024]{1,0:T(8,128)(2,1)},...) custom-call(bf16[32,4224]{1,0:T(8,128)(2,1)} %pad_maximum_fusion.a, ...), custom_call_target="tpu_custom_call" | custom-call | tf_op jit(solution)/shard_map/pallas_call | solution.py:571
  136.6 143.5 %shard_map.272 = (f32[32,3072]{1,0:T(8,128)}, f32[32,1024]{1,0:T(8,128)}, f32[32,4096]{1,0:T(8,128)}, f32[128,1024]{1,0:T(8,128)}, f32[8,128]{1,0:T(8,128)}, /*i...) custom-call(bf16[1024,4224]{1,0:T(8,128)(2,1)} %get-tuple-element.36, ...), custom_call_target="tpu_custom_call" | custom-call | tf_op jit(solution)/shard_map/pallas_call | solution.py:1022
  280.2 0.0 copy-start
  280.2 1.6 constant_dynamic-slice_fusion.2
  281.9 0.2 copy-done
  282.1 2.2 convert_add_fusion
  284.4 0.9 copy.34
  285.2 0.9 copy.33
  286.1 0.8 copy.31
  287.0 0.7 copy.32
  287.6 0.6 fusion
  288.2 0.5 slice_bitcast_fusion.1
  (42 shorter events, 0.2 us)
Async XLA Ops:
  0.6 3.5 %copy-start.6 = (f32[98304]{0:T(1024)S(1)}, f32[98304]{0:T(1024)}, u32[]{:S(2)}) copy-start(f32[98304]{0:T(1024)} %param.21) | copy-start | bytes 1179652
  1.4 2.9 copy-start.8
  1.4 3.0 %copy-start.11 = (f32[32]{0:T(128)S(1)}, f32[32]{0:T(128)}, u32[]{:S(2)}) copy-start(f32[32]{0:T(128)} %param.19) | copy-start | bytes 388
  1.4 3.0 %copy-start.12 = (f32[32]{0:T(128)S(1)}, f32[32]{0:T(128)}, u32[]{:S(2)}) copy-start(f32[32]{0:T(128)} %param.20) | copy-start | bytes 388
  1.4 3.0 %copy-start.13 = (f32[32]{0:T(128)S(1)}, f32[32]{0:T(128)}, u32[]{:S(2)}) copy-start(f32[32]{0:T(128)} %param.22) | copy-start | bytes 388
  1.4 3.0 %copy-start.14 = (f32[32]{0:T(128)S(1)}, f32[32]{0:T(128)}, u32[]{:S(2)}) copy-start(f32[32]{0:T(128)} %param.23) | copy-start | bytes 388
  1.4 3.0 %copy-start.15 = (f32[32]{0:T(128)S(1)}, f32[32]{0:T(128)}, u32[]{:S(2)}) copy-start(f32[32]{0:T(128)} %param.25) | copy-start | bytes 388
  1.4 3.0 %copy-start.16 = (f32[32]{0:T(128)S(1)}, f32[32]{0:T(128)}, u32[]{:S(2)}) copy-start(f32[32]{0:T(128)} %param.26) | copy-start | bytes 388
  1.4 3.0 %copy-start.17 = (f32[32]{0:T(128)S(1)}, f32[32]{0:T(128)}, u32[]{:S(2)}) copy-start(f32[32]{0:T(128)} %param.27) | copy-start | bytes 388
  1.5 3.0 %copy-start.18 = (f32[32]{0:T(128)S(1)}, f32[32]{0:T(128)}, u32[]{:S(2)}) copy-start(f32[32]{0:T(128)} %param.31) | copy-start | bytes 388
  1.5 3.0 %copy-start.19 = (f32[128]{0:T(128)S(1)}, f32[128]{0:T(128)}, u32[]{:S(2)}) copy-start(f32[128]{0:T(128)} %param.29) | copy-start | bytes 1540
  1.5 3.9 %copy-start.1 = (f32[3,128,1024]{2,1,0:T(8,128)S(1)}, f32[3,128,1024]{2,1,0:T(8,128)}, u32[]{:S(2)}) copy-start(f32[3,128,1024]{2,1,0:T(8,128)} %param.16) | copy-start | bytes 4718596
  4.3 2.1 copy-start.2
  5.4 1.9 copy-start.3
  280.2 1.9 copy-start
  282.1 2.3 copy-start.5
  282.1 3.1 %copy-start.4 = (f32[32,4096]{1,0:T(8,128)S(1)}, f32[32,4096]{1,0:T(8,128)}, u32[]{:S(2)}) copy-start(f32[32,4096]{1,0:T(8,128)} %get-tuple-element.55) | copy-start | bytes 1572868
  284.3 1.8 copy-start.7
  284.3 2.6 copy-start.9
  284.4 3.3 %copy-start.10 = (f32[8,128]{1,0:T(8,128)S(1)}, f32[8,128]{1,0:T(8,128)}, u32[]{:S(2)}) copy-start(f32[8,128]{1,0:T(8,128)} %get-tuple-element.52) | copy-start | bytes 12292

commit v6 on v5

--- a/solution.py
+++ b/solution.py
@@ -616,8 +616,9 @@
 
 
 class Reduce:
-    def __init__(self, io, r, s, land, pieces, stage, out):
+    def __init__(self, io, r, s, land, pieces, stage, out, direct=False):
         self.io, self.r, self.s, self.land, self.pieces = io, r, s, land, pieces
+        self.direct = direct
         self.stage, self.out = stage, out
         self.slot = io.slots(6)
         self.z_slot = io.slots(4)
@@ -657,12 +658,12 @@
             own = self.half(0, h)[...]
             total = own.astype(F32) + self.stage[0].astype(F32) + self.stage[1].astype(F32)
             self.half(3, h)[...] = total.astype(own.dtype)
-        for i, k in ((0, 3), (1, 1)):
+        for i, k, by in ((0, 3, 3 if self.direct else 1), (1, 1, 1), (2, 2, 2))[: 3 if self.direct else 2]:
             io.start(
                 self.z_slot[i],
                 lambda k=k: self.piece(io.z ^ k),
                 lambda i=i: self.pieces.at[i],
-                (io.dp, io.z ^ 1),
+                (io.dp, io.z ^ by),
             )
 
     def piece(self, z):
@@ -684,9 +685,9 @@
         )
 
     def finish(self):
-        one, two = self.take(1), self.take(2)
+        taken = [self.take(i) for i in ((1, 2, 0) if self.direct else (1, 2))]
         total = self.piece(self.io.z)[...].astype(F32)
-        for copy, spot in (one, two):
+        for copy, spot in taken:
             copy.wait()
             total = total + spot[...].astype(F32)
         self.out[...] = total
@@ -746,10 +747,10 @@
     def part_of_a(c):
         blocks = lambda j: ug2.at[pl.ds(j * 4 * n_a, 4 * n_a), pl.ds(c * D, D)]
         out = p_out if c == 3 else qkv_out.at[:, pl.ds(c * D, D)]
-        return Reduce(io, n_a, blocks, a_land.at[c], a_pieces.at[c], stage_a, out)
+        return Reduce(io, n_a, blocks, a_land.at[c], a_pieces.at[c], stage_a, out, direct=c == 2)
 
     red_q, red_k, red_v, red_p = (part_of_a(c) for c in range(4))
-    red_s = Reduce(io, s_out.shape[0], lambda j: s_s.at[j], s_land, s_pieces, stage_s, s_out)
+    red_s = Reduce(io, s_out.shape[0], lambda j: s_s.at[j], s_land, s_pieces, stage_s, s_out, direct=True)
     back_in = HandBack(io, qkv.at[:, pl.ds(D, D)], ret_in)
     back_out = HandBack(io, ob, ret_out)
 
@@ -918,18 +919,6 @@
         acc[:, lanes(i, w_rows)] = dot_nt(jn2[own], wb[slot, :, 0 : 3 * D])
 
     stream(io, D // w_rows, w_tile(wa, 0, 3 * D), first_back)
-    io.arrived(jn_slot, lambda: jn2.at[sib])
-
-    def qkv_step(i, _):
-        ug2[own, lanes(i, COLS)] = dot(flip[...], jn2[:, lanes(i, COLS)]).astype(BF)
-        return 0
-
-    for c, red in enumerate((red_q, red_k, red_v)):
-        lax.fori_loop(c * D // COLS, (c + 1) * D // COLS, qkv_step, 0)
-        red.start()
-    red_p.relay()
-    red_d.finish()
-
     def first_norm(i, _):
         rows = pl.ds(pl.multiple_of(i * CHUNK, CHUNK), CHUNK)
         e = acc[rows]
@@ -945,6 +934,18 @@
 
     lax.fori_loop(0, t // CHUNK, first_norm, 0)
     back_in.start()
+
+    io.arrived(jn_slot, lambda: jn2.at[sib])
+
+    def qkv_step(i, _):
+        ug2[own, lanes(i, COLS)] = dot(flip[...], jn2[:, lanes(i, COLS)]).astype(BF)
+        return 0
+
+    for c, red in enumerate((red_q, red_k, red_v)):
+        lax.fori_loop(c * D // COLS, (c + 1) * D // COLS, qkv_step, 0)
+        red.start()
+    red_p.relay()
+    red_d.finish()
 
     spread_n = lax.broadcasted_iota(jnp.int32, (32, D), 0)
     spread_c = lax.broadcasted_iota(jnp.int32, (32, D), 1)
@@ -982,11 +983,9 @@
     red_k.fold()
     red_p.cross()
     red_v.fold()
+    red_s.fold()
     red_q.cross()
     red_k.cross()
-    red_s.fold()
-    red_v.cross()
-    red_s.cross()
     for red in (red_u, red_p, red_q, red_k):
         red.finish()
     back_in.wait()

time: 291 us -> 286 us (0.983)
  Pallas kernels: 272 us -> 267 us
    pallas_call x1, Pallas kernels: 144 us -> 139 us  [backward(): pl.pallas_call(backward_kernel, out_shape=[o for o, _ in outs], in_specs=...]
where the time goes in v6:
time: 286 us; the launch traced here: 284 us
  Pallas kernels  267 us (93%)
  local copies, waits for them, and re-layouts  8.23 us (3%)
  other arithmetic  6.71 us (2%)
    pallas_call x1, Pallas kernels, backward(): pl.pallas_call(backward_kernel, out_shape=[o for o, _ in outs], in_specs=...  139 us
    pallas_call x1, Pallas kernels, forward(): pl.pallas_call(forward_kernel, out_shape=[sh((D, a.shape[1]), BF), sh((D,...  129 us

profile of v6, /device:TPU:0, one launch (start us, length us, event | category | flops | bytes accessed | tf_op | source)
XLA Modules:
  0.0 284.1 jit_solution(5002767214080028327)
XLA Ops:
  0.6 0.0 copy-start.6
  1.4 0.0 copy-start.8
  1.4 0.0 copy-start.11
  1.4 0.0 copy-start.12
  1.4 0.0 copy-start.13
  1.4 0.0 copy-start.14
  1.4 0.0 copy-start.15
  1.4 0.0 copy-start.16
  1.4 0.0 copy-start.17
  1.5 0.0 copy-start.18
  1.5 0.0 copy-start.19
  1.5 0.0 copy-start.1
  1.5 2.6 multiply_convert_fusion.cot
  4.2 0.1 reshape.67
  4.3 0.0 copy-start.2
  4.5 0.1 concatenate.8
  4.6 0.7 pad_maximum_fusion.a
  5.4 1.0 convert_element_type.37.clips
  6.4 0.8 convert_element_type.34.u
  7.2 0.8 convert_element_type.36.d
  8.1 128.5 %shard_map.271 = (bf16[1024,4224]{1,0:T(8,128)(2,1)}, bf16[1024,4096]{1,0:T(8,128)(2,1)}, bf16[4096,1024]{1,0:T(8,128)(2,1)}, bf16[512,1024]{1,0:T(8,128)(2,1)},...) custom-call(bf16[32,4224]{1,0:T(8,128)(2,1)} %pad_maximum_fusion.a, ...), custom_call_target="tpu_custom_call" | custom-call | tf_op jit(solution)/shard_map/pallas_call | solution.py:571
  136.6 138.9 %shard_map.272 = (f32[32,3072]{1,0:T(8,128)}, f32[32,1024]{1,0:T(8,128)}, f32[32,4096]{1,0:T(8,128)}, f32[128,1024]{1,0:T(8,128)}, f32[8,128]{1,0:T(8,128)}, /*i...) custom-call(bf16[1024,4224]{1,0:T(8,128)(2,1)} %get-tuple-element.36, ...), custom_call_target="tpu_custom_call" | custom-call | tf_op jit(solution)/shard_map/pallas_call | solution.py:1021
  275.5 0.0 copy-start
  275.6 1.6 constant_dynamic-slice_fusion.2
  277.2 0.2 copy-done
  277.4 2.2 convert_add_fusion
  279.7 0.9 copy.34
  280.6 0.9 copy.33
  281.5 0.8 copy.31
  282.3 0.7 copy.32
  283.0 0.6 fusion
  283.6 0.5 slice_bitcast_fusion.1
  (42 shorter events, 0.2 us)
Async XLA Ops:
  0.6 3.5 %copy-start.6 = (f32[98304]{0:T(1024)S(1)}, f32[98304]{0:T(1024)}, u32[]{:S(2)}) copy-start(f32[98304]{0:T(1024)} %param.21) | copy-start | bytes 1179652
  1.4 2.9 %copy-start.8 = (f32[32768]{0:T(1024)S(1)}, f32[32768]{0:T(1024)}, u32[]{:S(2)}) copy-start(f32[32768]{0:T(1024)} %param.24) | copy-start | bytes 393220
  1.4 3.0 %copy-start.11 = (f32[32]{0:T(128)S(1)}, f32[32]{0:T(128)}, u32[]{:S(2)}) copy-start(f32[32]{0:T(128)} %param.19) | copy-start | bytes 388
  1.4 3.0 %copy-start.12 = (f32[32]{0:T(128)S(1)}, f32[32]{0:T(128)}, u32[]{:S(2)}) copy-start(f32[32]{0:T(128)} %param.20) | copy-start | bytes 388
  1.4 3.0 %copy-start.13 = (f32[32]{0:T(128)S(1)}, f32[32]{0:T(128)}, u32[]{:S(2)}) copy-start(f32[32]{0:T(128)} %param.22) | copy-start | bytes 388
  1.4 3.0 %copy-start.14 = (f32[32]{0:T(128)S(1)}, f32[32]{0:T(128)}, u32[]{:S(2)}) copy-start(f32[32]{0:T(128)} %param.23) | copy-start | bytes 388
  1.4 3.0 %copy-start.15 = (f32[32]{0:T(128)S(1)}, f32[32]{0:T(128)}, u32[]{:S(2)}) copy-start(f32[32]{0:T(128)} %param.25) | copy-start | bytes 388
  1.4 3.0 %copy-start.16 = (f32[32]{0:T(128)S(1)}, f32[32]{0:T(128)}, u32[]{:S(2)}) copy-start(f32[32]{0:T(128)} %param.26) | copy-start | bytes 388
  1.4 3.0 %copy-start.17 = (f32[32]{0:T(128)S(1)}, f32[32]{0:T(128)}, u32[]{:S(2)}) copy-start(f32[32]{0:T(128)} %param.27) | copy-start | bytes 388
  1.5 3.0 %copy-start.18 = (f32[32]{0:T(128)S(1)}, f32[32]{0:T(128)}, u32[]{:S(2)}) copy-start(f32[32]{0:T(128)} %param.31) | copy-start | bytes 388
  1.5 3.0 %copy-start.19 = (f32[128]{0:T(128)S(1)}, f32[128]{0:T(128)}, u32[]{:S(2)}) copy-start(f32[128]{0:T(128)} %param.29) | copy-start | bytes 1540
  1.5 3.9 %copy-start.1 = (f32[3,128,1024]{2,1,0:T(8,128)S(1)}, f32[3,128,1024]{2,1,0:T(8,128)}, u32[]{:S(2)}) copy-start(f32[3,128,1024]{2,1,0:T(8,128)} %param.16) | copy-start | bytes 4718596
  4.3 2.1 copy-start.2
  5.4 1.9 copy-start.3
  275.5 1.9 copy-start
  277.4 2.3 copy-start.5
  277.4 3.1 %copy-start.4 = (f32[32,4096]{1,0:T(8,128)S(1)}, f32[32,4096]{1,0:T(8,128)}, u32[]{:S(2)}) copy-start(f32[32,4096]{1,0:T(8,128)} %get-tuple-element.55) | copy-start | bytes 1572868
  279.7 1.8 copy-start.7
  279.7 2.6 copy-start.9
  279.7 3.3 %copy-start.10 = (f32[8,128]{1,0:T(8,128)S(1)}, f32[8,128]{1,0:T(8,128)}, u32[]{:S(2)}) copy-start(f32[8,128]{1,0:T(8,128)} %get-tuple-element.52) | copy-start | bytes 12292

commit v7 on v6

--- a/solution.py
+++ b/solution.py
@@ -230,7 +230,6 @@
     def __init__(self, io, shard, out):
         self.io, self.shard, self.out = io, shard, out
         self.r = shard.shape[0]
-        self.local = io.load(shard, self.at(0, 0))
         self.keys = (0, 1, 2, 3)
         self.z_slot = io.slots(4)
         self.slot = {k: {name: io.slots(2) for name in ("x", "y", "d", "own", "cx", "cy", "cd")} for k in self.keys}
@@ -250,6 +249,9 @@
 
     def got(self, name, i, m, k, part=None):
         self.io.arrived(self.slot[k][name][i], lambda: self.at(m, k, part))
+
+    def begin(self):
+        self.local = self.io.load(self.shard, self.at(0, 0))
 
     def start_z(self):
         io = self.io
@@ -393,9 +395,9 @@
 
 
 def forward_kernel(
-    a, u, d, clips, cot,
+    qkv_flat, proj_flat, small, up_flat, down_flat, clips, cot, living,
     wa, wu, wd, og, x_out, middle_out, n1_out, n2_out, qkv_out, att_out, hidden, slope, vec, d_terms,
-    xv, og2, n1, n2, qkv, att, middle, wb, hid, hid2, terms, slo, table, wide, ub, bias,
+    wide_q, wide_p, wide_s, wide_u, wide_d, a, u, d, wide_x, wide_c, low_x, low_c, xv, og2, n1, n2, qkv, att, middle, wb, hid, hid2, terms, slo, table, wide, ub, bias,
     send, recv, local,
 ):
     io = Copies(send, recv, local)
@@ -403,7 +405,23 @@
     t = xv.shape[0]
     own, sib = pl.ds(0, t), pl.ds(t, t)
     core = (io.dp ^ 1, io.z)
-    cx, cc = Collect(io, clips, xv), Collect(io, cot, og2.at[own])
+    cx, cc = Collect(io, low_x, xv), Collect(io, low_c, og2.at[own])
+    load_a = [io.load(qkv_flat, wide_q), io.load(proj_flat, wide_p), io.load(small, wide_s)]
+    load_u, load_d = io.load(up_flat, wide_u), io.load(down_flat, wide_d)
+    load_x, load_c = io.load(clips, wide_x), io.load(cot, wide_c)
+
+    def fill(dst, at, flat):
+        n = dst.shape[0]
+        tiles = flat.shape[0] // n
+        for c in range(tiles):
+            dst[:, at + c * LANES : at + (c + 1) * LANES] = flat[pl.ds(c, n, stride=tiles), :].astype(BF)
+
+    for c in load_a:
+        c.wait()
+    fill(a, 0, wide_q)
+    fill(a, 3 * D, wide_p)
+    a[:, 4 * D : 4 * D + LANES] = wide_s[...].astype(BF)
+    ga.begin()
     meet(io)
 
     line = [(g, k) for g in (ga, gu, gd) for k in range(4)]
@@ -433,9 +451,21 @@
                 g.far(k)
 
     ga.start_z()
-    advance(3)
+    advance()
+    load_x.wait()
+    low_x[...] = wide_x[...].astype(BF)
+    load_u.wait()
+    fill(u, 0, wide_u)
+    gu.begin()
+    advance(2)
+    load_d.wait()
+    fill(d, 0, wide_d)
+    gd.begin()
     for g in (ga, gu, gd):
         g.local.wait()
+    load_c.wait()
+    for c in range(3):
+        low_c[c] = (wide_c[c] * living[c : c + 1, 0:1]).astype(BF)
     advance(4)
     outs = []
 
@@ -562,7 +592,9 @@
     io.finish()
 
 
-def forward(a, u, d, clips, cot):
+def forward(*args):
+    clips = args[5]
+    n = 32
     t = clips.shape[1] * 4
     any_ = pl.BlockSpec(memory_space=pl.ANY)
     vmem = pl.BlockSpec(memory_space=pltpu.VMEM)
@@ -571,7 +603,7 @@
     return pl.pallas_call(
         forward_kernel,
         out_shape=[
-            sh((D, a.shape[1]), BF),
+            sh((D, 4 * D + LANES), BF),
             sh((D, FF), BF),
             sh((FF, D), BF),
             sh((t, D), BF),
@@ -586,9 +618,17 @@
             sh((8, D), F32),
             sh((4, FF // 8, D), BF),
         ],
-        in_specs=[any_] * 5,
+        in_specs=[any_] * 7 + [vmem],
         out_specs=[any_] * 12 + [vmem, any_],
-        scratch_shapes=[
+        scratch_shapes=[v(w.shape, F32) for w in args[:5]]
+        + [
+            v((D // n, 4 * D + LANES), BF),
+            v((D // n, FF), BF),
+            v((FF // n, D), BF),
+            v(clips.shape, F32),
+            v(clips.shape, F32),
+            v(clips.shape, BF),
+            v(clips.shape, BF),
             v((t, D), BF),
             v((2 * t, D), BF),
             v((t, D), BF),
@@ -612,7 +652,7 @@
         compiler_params=pltpu.CompilerParams(
             collective_id=0, has_side_effects=True, vmem_limit_bytes=56 * 2**20
         ),
-    )(a, u, d, clips, cot)
+    )(*args)
 
 
 class Reduce:
@@ -697,6 +737,7 @@
     def __init__(self, io, src, dst):
         self.io, self.src, self.dst = io, src, dst
         self.slots = io.slots(4)
+        self.local = io.locals(1)
         self.rows = dst.shape[1]
 
     def host(self, z):
@@ -1118,23 +1159,33 @@
     )
     packed = jnp.concatenate(small)
     packed = jnp.pad(packed, (0, rows * LANES - packed.shape[0])).reshape(rows, LANES)
-    shard_a = jnp.concatenate(
-        [qkv_weight.reshape(rows, 3 * D), proj_weight.reshape(rows, D), packed], axis=1
-    ).astype(BF)
-    shard_u = up_weight.reshape(rows, FF).astype(BF)
-    shard_d = down_weight.reshape(FF // n, D).astype(BF)
 
     living = (jnp.arange(slots) < counts[0]).astype(F32)[:, None, None]
     living_cot = living * out_cotangent
-    tokens = (clips.astype(BF), living_cot.astype(BF))
     if links.short:
-        saved = forward(shard_a, shard_u, shard_d, *tokens)
+        living_rows = jnp.broadcast_to(living.reshape(slots, 1), (slots, LANES))
+        flat = lambda w: w.reshape(-1, LANES)
+        saved = forward(
+            flat(qkv_weight),
+            flat(proj_weight),
+            packed,
+            flat(up_weight),
+            flat(down_weight),
+            clips,
+            out_cotangent,
+            living_rows,
+        )
         qkv_grad, proj_grad, up_grad, down_grad, small_grad, out_back, in_back = backward(*saved)
         out_home, in_home = links.by_clip(out_back, slots), links.by_clip(in_back, slots)
         small_out = small_grad[:3].reshape(-1)
     else:
+        shard_a = jnp.concatenate(
+            [qkv_weight.reshape(rows, 3 * D), proj_weight.reshape(rows, D), packed], axis=1
+        ).astype(BF)
+        shard_u = up_weight.reshape(rows, FF).astype(BF)
+        shard_d = down_weight.reshape(FF // n, D).astype(BF)
         a_mat, u_mat, d_mat = (links.gather(shard) for shard in (shard_a, shard_u, shard_d))
-        x, out_grad = (links.collect(t) for t in tokens)
+        x, out_grad = (links.collect(t.astype(BF)) for t in (clips, living_cot))
         x = x.astype(F32)
 
         table = a_mat[:, 4 * D :].reshape(n_dp, n_seq, rows * LANES)

time: 286 us -> 284 us (level)
  other arithmetic: 6.71 us -> 2.23 us
    convert_element_type x4 -> x0, other arithmetic: 3.68 us -> none  [the longest x2 3.62 us: per_device(): tokens = (clips.astype(BF), living_cot.astype(BF))]
where the time goes in v7:
time: 284 us; the launch traced here: 282 us
  Pallas kernels  269 us (95%)
  local copies, waits for them, and re-layouts  8.86 us (3%)
    pallas_call x1, Pallas kernels, backward(): pl.pallas_call(backward_kernel, out_shape=[o for o, _ in outs], in_specs=...  139 us
    pallas_call x1, Pallas kernels, forward(): pl.pallas_call(forward_kernel, out_shape=[sh((D, 4 * D + LANES), BF), sh(...  130 us

profile of v7, /device:TPU:0, one launch (start us, length us, event | category | flops | bytes accessed | tf_op | source)
XLA Modules:
  0.0 281.9 jit_solution(5663728276694648355)
XLA Ops:
  1.3 0.6 broadcast_in_dim.2.living
  2.0 0.9 concatenate.3
  2.8 0.6 pad_bitcast_fusion.small
  3.4 130.3 %shard_map.271 = (bf16[1024,4224]{1,0:T(8,128)(2,1)}, bf16[1024,4096]{1,0:T(8,128)(2,1)}, bf16[4096,1024]{1,0:T(8,128)(2,1)}, bf16[512,1024]{1,0:T(8,128)(2,1)},...) custom-call(f32[768,128]{1,0:T(8,128)} %bitcast.26, ...), custom_call_target="tpu_custom_call" | custom-call | tf_op jit(solution)/shard_map/pallas_call | solution.py:603
  133.7 139.1 %shard_map.272 = (f32[32,3072]{1,0:T(8,128)}, f32[32,1024]{1,0:T(8,128)}, f32[32,4096]{1,0:T(8,128)}, f32[128,1024]{1,0:T(8,128)}, f32[8,128]{1,0:T(8,128)}, /*i...) custom-call(bf16[1024,4224]{1,0:T(8,128)(2,1)} %get-tuple-element.36, ...), custom_call_target="tpu_custom_call" | custom-call | tf_op jit(solution)/shard_map/pallas_call | solution.py:1062
  272.9 0.0 copy-start
  272.9 0.0 copy-start.1
  272.9 1.7 constant_dynamic-slice_fusion.2
  274.6 0.2 copy-done
  274.8 0.5 copy-done.1
  275.3 0.0 copy-start.3
  275.3 0.0 copy-start.2
  275.3 2.2 convert_add_fusion
  277.5 0.0 copy-start.4
  277.5 0.0 copy-start.5
  277.5 0.0 copy-done.3
  277.5 0.0 copy-start.6
  277.5 0.9 copy.33
  278.4 0.0 copy-done.2
  278.4 0.9 copy.34
  279.3 0.0 copy-done.4
  279.3 0.8 copy.31
  280.1 0.0 copy-done.5
  280.1 0.7 copy.32
  280.8 0.0 copy-done.6
  280.8 0.6 fusion
  281.4 0.5 slice_bitcast_fusion.1
  (2 shorter events, 0.0 us)
Async XLA Ops:
  272.9 1.9 copy-start
  272.9 2.3 copy-start.1
  275.3 2.2 copy-start.3
  275.3 3.1 %copy-start.2 = (f32[128,1024]{1,0:T(8,128)S(1)}, f32[128,1024]{1,0:T(8,128)}, u32[]{:S(2)}) copy-start(f32[128,1024]{1,0:T(8,128)} %get-tuple-element.56) | copy-start | bytes 1572868
  277.5 1.8 copy-start.4
  277.5 2.6 copy-start.5
  277.5 3.3 %copy-start.6 = (f32[8,128]{1,0:T(8,128)S(1)}, f32[8,128]{1,0:T(8,128)}, u32[]{:S(2)}) copy-start(f32[8,128]{1,0:T(8,128)} %get-tuple-element.52) | copy-start | bytes 12292
